TPU v7x, 32 devices: a whole 2x2x4 slice. The times are simulated.
32 devices in a mesh: dp: 8 (over z, y), vocab: 4 (over x, core).
Axes of the slice: x: 2, y: 2, z: 4, core: 2. Of those that a mesh axis runs over, the one named last changes fastest.
Arguments:
- enc_ids: int32 [8, 512], P('dp'), may hold values from 0 to 96102
- labels: int32 [8, 256], P('dp'), may hold values from 0 to 96102
- target_lengths: int32 [8], P('dp'), may hold values from 1 to 256, as said below
- loss_positions: int32 [8, 64], P('dp'), may hold values from 0 to 255, as said below
- embedding: float32 [96104, 768], P('vocab', 'dp'), as said below
- attn_in: float32 [3, 768, 2304], P(None, 'dp'), may hold values from -0.21875 to 0.21875
- attn_out: float32 [3, 768, 768], P(None, 'dp'), may hold values from -1.75 to 1.75
- ffn_up: float32 [2, 768, 3072], P(None, 'dp'), may hold values from -0.21875 to 0.21875
- ffn_down: float32 [2, 3072, 768], P(None, 'dp'), may hold values from -0.109375 to 0.109375
- norms: float32 [14, 768], P(None, 'dp'), as said below
- embedding_first: float32 [96104, 768], P('vocab', 'dp'), may hold values from -1.4305115e-06 to 1.4305115e-06
- attn_in_first: float32 [3, 768, 2304], P(None, 'dp'), may hold values from -1.4305115e-06 to 1.4305115e-06
- attn_out_first: float32 [3, 768, 768], P(None, 'dp'), may hold values from -1.4305115e-06 to 1.4305115e-06
- ffn_up_first: float32 [2, 768, 3072], P(None, 'dp'), may hold values from -1.4305115e-06 to 1.4305115e-06
- ffn_down_first: float32 [2, 3072, 768], P(None, 'dp'), may hold values from -1.4305115e-06 to 1.4305115e-06
- norms_first: float32 [14, 768], P(None, 'dp'), may hold values from -5.722046e-06 to 5.722046e-06
- embedding_second: float32 [96104, 768], P('vocab', 'dp'), may hold values from 2.2140133e-15 to 3.5424212e-14
- attn_in_second: float32 [3, 768, 2304], P(None, 'dp'), may hold values from 2.2140133e-15 to 3.5424212e-14
- attn_out_second: float32 [3, 768, 768], P(None, 'dp'), may hold values from 2.2140133e-15 to 3.5424212e-14
- ffn_up_second: float32 [2, 768, 3072], P(None, 'dp'), may hold values from 2.2140133e-15 to 3.5424212e-14
- ffn_down_second: float32 [2, 3072, 768], P(None, 'dp'), may hold values from 2.2140133e-15 to 3.5424212e-14
- norms_second: float32 [14, 768], P(None, 'dp'), may hold values from 3.5424212e-14 to 5.667874e-13
Outputs:
- loss_sum: float32 [], replicated
- token_count: float32 [], replicated
- grad_norm: float32 [], replicated
- new_embedding: float32 [96104, 768], P('vocab', 'dp')
- new_attn_in: float32 [3, 768, 2304], P(None, 'dp')
- new_attn_out: float32 [3, 768, 768], P(None, 'dp')
- new_ffn_up: float32 [2, 768, 3072], P(None, 'dp')
- new_ffn_down: float32 [2, 3072, 768], P(None, 'dp')
- new_norms: float32 [14, 768], P(None, 'dp')
- embedding_first_out: float32 [96104, 768], P('vocab', 'dp')
- attn_in_first_out: float32 [3, 768, 2304], P(None, 'dp')
- attn_out_first_out: float32 [3, 768, 768], P(None, 'dp')
- ffn_up_first_out: float32 [2, 768, 3072], P(None, 'dp')
- ffn_down_first_out: float32 [2, 3072, 768], P(None, 'dp')
- norms_first_out: float32 [14, 768], P(None, 'dp')
- embedding_second_out: float32 [96104, 768], P('vocab', 'dp')
- attn_in_second_out: float32 [3, 768, 2304], P(None, 'dp')
- attn_out_second_out: float32 [3, 768, 768], P(None, 'dp')
- ffn_up_second_out: float32 [2, 768, 3072], P(None, 'dp')
- ffn_down_second_out: float32 [2, 3072, 768], P(None, 'dp')
- norms_second_out: float32 [14, 768], P(None, 'dp')
Inputs may be any that keep to these rules, and one draw needn't show every extreme that they name: `target_lengths`: the last example's length is 256. `loss_positions`: each row holds 64 different positions. `embedding`: entries are of order 768^(-1/2) up to a factor of a few. `norms`: gains are positive and of order one; biases are of order a few tenths.
All inputs are finite; a program needn't handle non-finite values.
Results may differ from a plain program's by a relative error of at most 0.02.
Values may be sent and summed in bfloat16 or wider, within the bound.
A program may use at most 576 MiB of HBM per device.

v0:
```python
from functools import partial
import math

import jax
import jax.numpy as jnp
from jax import lax
from jax.sharding import PartitionSpec as P

HEADS = 12
HEAD_DIM = 64
STEP = 10


EPS_NORM = 1e-05
SMOOTH = 0.1
CLIP = 0.02
RATES = (0.05, 0.05, 0.4, 0.05, 0.05, 0.8)
BETA_ONE = 0.9
BETA_TWO = 0.999
ADAM_EPS = 1e-08
DECAY = 0.01


def lowered(tensor):
    return tensor.astype(jnp.bfloat16)


def matmul(left_side, right_side):
    return jnp.dot(left_side, right_side, preferred_element_type=jnp.float32)


def times_transposed(left_side, right_side):
    return lax.dot_general(
        left_side, right_side, (((1,), (1,)), ((), ())), preferred_element_type=jnp.float32
    )


def contract_rows(left_side, right_side):
    return lax.dot_general(
        left_side, right_side, (((0,), (0,)), ((), ())), preferred_element_type=jnp.float32
    )


def positions_table(length, model_width):
    position_col = jnp.arange(length, dtype=jnp.float32)[:, None]
    freq_index = jnp.arange(model_width // 2, dtype=jnp.float32)[None, :]
    angles = position_col * jnp.exp(freq_index * (-2.0 * math.log(10000.0) / model_width))
    return jnp.concatenate([jnp.sin(angles), jnp.cos(angles)], axis=1)


def norm_forward(tensor, gain_row, shift_row):
    center = tensor - jnp.mean(tensor, axis=-1, keepdims=True)
    scale_inv = lax.rsqrt(jnp.mean(center * center, axis=-1, keepdims=True) + EPS_NORM)
    normed = center * scale_inv
    return (normed * gain_row + shift_row, (normed, scale_inv))


def norm_backward(grad_out, saved_parts, gain_row):
    normed, scale_inv = saved_parts
    grad_normed = grad_out * gain_row
    grad_in = scale_inv * (
        grad_normed
        - jnp.mean(grad_normed, axis=-1, keepdims=True)
        - normed * jnp.mean(grad_normed * normed, axis=-1, keepdims=True)
    )
    return (grad_in, jnp.sum(grad_out * normed, axis=0), jnp.sum(grad_out, axis=0))


def split_heads(rows, batch_size):
    return rows.reshape(batch_size, -1, HEADS, rows.shape[1] // HEADS)


def score_block(queries, key_rows, causal):
    scores = jnp.einsum(
        "qhe,khe->hqk", queries, key_rows, preferred_element_type=jnp.float32
    ) * HEAD_DIM ** (-0.5)
    if causal:
        allowed = jnp.arange(queries.shape[0])[:, None] >= jnp.arange(key_rows.shape[0])[None, :]
        scores = jnp.where(allowed[None], scores, -1e30)
    return scores


def attend_one(block_args, causal):
    queries, key_rows, value_rows = block_args
    scores = score_block(queries, key_rows, causal)
    row_top = jnp.max(scores, axis=-1, keepdims=True)
    exponent = jnp.exp(scores - row_top)
    row_total = jnp.sum(exponent, axis=-1, keepdims=True)
    softmax_out = lowered(exponent / row_total)
    context = jnp.einsum(
        "hqk,khe->qhe", softmax_out, value_rows, preferred_element_type=jnp.float32
    )
    return (lowered(context), (row_top + jnp.log(row_total))[..., 0])


def attend_back(block_args, causal):
    queries, key_rows, value_rows, log_total, grad_context = block_args
    scores = score_block(queries, key_rows, causal)
    softmax_out = jnp.exp(scores - log_total[..., None])
    grad_values = jnp.einsum(
        "hqk,qhe->khe", lowered(softmax_out), grad_context, preferred_element_type=jnp.float32
    )
    grad_softmax = jnp.einsum(
        "qhe,khe->hqk", grad_context, value_rows, preferred_element_type=jnp.float32
    )
    grad_scores = lowered(
        softmax_out * (grad_softmax - jnp.sum(grad_softmax * softmax_out, axis=-1, keepdims=True))
    )
    grad_queries = jnp.einsum(
        "hqk,khe->qhe", grad_scores, key_rows, preferred_element_type=jnp.float32
    ) * HEAD_DIM ** (-0.5)
    grad_keys = jnp.einsum(
        "hqk,qhe->khe", grad_scores, queries, preferred_element_type=jnp.float32
    ) * HEAD_DIM ** (-0.5)
    return (lowered(grad_queries), lowered(grad_keys), lowered(grad_values))


def layer_forward(stream, memory, blocks, feed_parts, gain_rows, shifts, batch_size):
    kept_values = []
    for block_order, (w_in, w_out, norm_row) in enumerate(blocks):
        normed, norm_kept = norm_forward(stream, gain_rows[norm_row], shifts[norm_row])
        query_in = lowered(normed)
        model_width = w_out.shape[0]
        if block_order == 0:
            projected = lowered(matmul(query_in, w_in))
            queries = projected[:, :model_width]
            key_rows = projected[:, model_width : 2 * model_width]
            value_rows = projected[:, 2 * model_width :]
            memory_in = query_in
        else:
            memory_in = memory
            queries = lowered(matmul(query_in, w_in[:, :model_width]))
            paired = lowered(matmul(memory, w_in[:, model_width:]))
            key_rows, value_rows = (paired[:, :model_width], paired[:, model_width:])
        causal = memory is not None and block_order == 0
        heads = (
            split_heads(queries, batch_size),
            split_heads(key_rows, batch_size),
            split_heads(value_rows, batch_size),
        )
        context, log_total = lax.map(partial(attend_one, causal=causal), heads)
        context = context.reshape(-1, model_width)
        stream = stream + matmul(context, w_out)
        kept_values.append((norm_kept, query_in, memory_in, heads, context, log_total))
    w_up, w_down, norm_row = feed_parts
    normed, norm_kept = norm_forward(stream, gain_rows[norm_row], shifts[norm_row])
    hidden_in = lowered(normed)
    hidden_pre = matmul(hidden_in, w_up)
    activated = lowered(jax.nn.silu(hidden_pre))
    stream = stream + matmul(activated, w_down)
    kept_values.append((norm_kept, hidden_in, hidden_pre, activated))
    return (stream, kept_values)


def layer_backward(grad_stream, memory, blocks, feed_parts, gain_rows, kept_values, batch_size):
    w_up, w_down, norm_row = feed_parts
    norm_kept, hidden_in, hidden_pre, activated = kept_values[-1]
    grad_low = lowered(grad_stream)
    grad_down = contract_rows(activated, grad_low)
    sigmoid_pre = jax.nn.sigmoid(hidden_pre)
    grad_pre = lowered(
        times_transposed(grad_low, w_down) * sigmoid_pre * (1.0 + hidden_pre * (1.0 - sigmoid_pre))
    )
    grad_up = contract_rows(hidden_in, grad_pre)
    grad_in, grad_gain, grad_shift = norm_backward(
        times_transposed(grad_pre, w_up), norm_kept, gain_rows[norm_row]
    )
    grad_stream = grad_stream + grad_in
    norm_grads = [(norm_row, grad_gain, grad_shift)]
    block_grads = [None] * len(blocks)
    grad_memory = None
    for block_order in reversed(range(len(blocks))):
        w_in, w_out, norm_row = blocks[block_order]
        norm_kept, query_in, memory_in, heads, context, log_total = kept_values[block_order]
        model_width = w_out.shape[0]
        grad_low = lowered(grad_stream)
        grad_w_out = contract_rows(context, grad_low)
        grad_context = split_heads(lowered(times_transposed(grad_low, w_out)), batch_size)
        causal = memory is not None and block_order == 0
        grad_heads = lax.map(partial(attend_back, causal=causal), heads + (log_total, grad_context))
        grad_queries, grad_keys, grad_values = [
            member.reshape(-1, model_width) for member in grad_heads
        ]
        if block_order == 0:
            grad_proj = jnp.concatenate([grad_queries, grad_keys, grad_values], axis=1)
            grad_w_in = contract_rows(query_in, grad_proj)
            grad_normed = times_transposed(grad_proj, w_in)
        else:
            grad_pair = jnp.concatenate([grad_keys, grad_values], axis=1)
            grad_w_in = jnp.concatenate(
                [contract_rows(query_in, grad_queries), contract_rows(memory_in, grad_pair)], axis=1
            )
            grad_normed = times_transposed(grad_queries, w_in[:, :model_width])
            grad_memory = times_transposed(grad_pair, w_in[:, model_width:])
        grad_in, grad_gain, grad_shift = norm_backward(grad_normed, norm_kept, gain_rows[norm_row])
        grad_stream = grad_stream + grad_in
        norm_grads.append((norm_row, grad_gain, grad_shift))
        block_grads[block_order] = (grad_w_in, grad_w_out)
    return (grad_stream, grad_memory, block_grads, (grad_up, grad_down), norm_grads)


def adam_update(weight, first_moment, second_moment, gradient, factor, rate):
    clipped = gradient * factor
    new_first = BETA_ONE * first_moment + (1.0 - BETA_ONE) * clipped
    new_second = BETA_TWO * second_moment + (1.0 - BETA_TWO) * clipped * clipped
    corrected = (
        new_first
        / (1.0 - BETA_ONE**STEP)
        / (jnp.sqrt(new_second / (1.0 - BETA_TWO**STEP)) + ADAM_EPS)
    )
    return (weight - rate * (corrected + DECAY * weight), new_first, new_second)


def local(
    enc_ids,
    labels,
    target_lengths,
    loss_positions,
    embedding,
    attn_in,
    attn_out,
    ffn_up,
    ffn_down,
    norms,
    embedding_first,
    attn_in_first,
    attn_out_first,
    ffn_up_first,
    ffn_down_first,
    norms_first,
    embedding_second,
    attn_in_second,
    attn_out_second,
    ffn_up_second,
    ffn_down_second,
    norms_second,
):
    batch_size, enc_len = enc_ids.shape
    dec_len = labels.shape[1]
    emb_table, w_in_all, w_out_all, w_up_all, w_down_all, norm_table = (
        lax.all_gather(lowered(embedding), "dp", axis=1, tiled=True),
        lax.all_gather(lowered(attn_in), "dp", axis=1, tiled=True),
        lax.all_gather(lowered(attn_out), "dp", axis=1, tiled=True),
        lax.all_gather(lowered(ffn_up), "dp", axis=1, tiled=True),
        lax.all_gather(lowered(ffn_down), "dp", axis=1, tiled=True),
        lax.all_gather(lowered(norms), "dp", axis=1, tiled=True),
    )
    model_width = emb_table.shape[1]
    shard_rows = emb_table.shape[0]
    vocab_total = shard_rows * lax.axis_size("vocab")
    row_start = lax.axis_index("vocab") * shard_rows
    norm_values = norm_table.astype(jnp.float32)
    gain_rows, shifts = (norm_values[:7], norm_values[7:])
    dec_ids = jnp.concatenate([jnp.zeros((batch_size, 1), jnp.int32), labels[:, :-1]], axis=1)
    token_list = jnp.concatenate([enc_ids.reshape(-1), dec_ids.reshape(-1)])
    local_rows = token_list - row_start
    inside = (local_rows >= 0) & (local_rows < shard_rows)
    safe_rows = jnp.clip(local_rows, 0, shard_rows - 1)
    picked = jnp.where(
        inside[:, None], jnp.take(emb_table, safe_rows, axis=0).astype(jnp.float32), 0.0
    )
    looked = lax.psum(picked.astype(jnp.bfloat16), "vocab").astype(jnp.float32)
    root_width = math.sqrt(model_width)
    enc_tokens = batch_size * enc_len
    enc_stream = (
        looked[:enc_tokens].reshape(batch_size, enc_len, model_width) * root_width
        + positions_table(enc_len, model_width)
    ).reshape(enc_tokens, model_width)
    dec_stream = (
        looked[enc_tokens:].reshape(batch_size, dec_len, model_width) * root_width
        + positions_table(dec_len, model_width)
    ).reshape(batch_size * dec_len, model_width)
    enc_blocks = [(w_in_all[0], w_out_all[0], 0)]
    dec_blocks = [(w_in_all[1], w_out_all[1], 3), (w_in_all[2], w_out_all[2], 4)]
    enc_feed = (w_up_all[0], w_down_all[0], 1)
    dec_feed = (w_up_all[1], w_down_all[1], 5)
    enc_out, enc_kept = layer_forward(
        enc_stream, None, enc_blocks, enc_feed, gain_rows, shifts, batch_size
    )
    memory, memory_kept = norm_forward(enc_out, gain_rows[2], shifts[2])
    memory_low = lowered(memory)
    dec_out, dec_kept = layer_forward(
        dec_stream, memory_low, dec_blocks, dec_feed, gain_rows, shifts, batch_size
    )
    final, final_kept = norm_forward(dec_out, gain_rows[6], shifts[6])
    chosen = (jnp.arange(batch_size)[:, None] * dec_len + loss_positions).reshape(-1)
    selected = lowered(jnp.take(final, chosen, axis=0))
    logits = times_transposed(selected, emb_table)
    columns = row_start + jnp.arange(shard_rows)
    padding = columns == vocab_total - 1
    masked = jnp.where(padding[None, :], -1e30, logits)
    target_local = jnp.take_along_axis(labels, loss_positions, axis=1).reshape(-1) - row_start
    target_hit = (jnp.arange(shard_rows)[None, :] == target_local[:, None]).astype(jnp.float32)
    target_term = jnp.sum(target_hit * logits, axis=1)
    smooth_term = jnp.sum(jnp.where(padding[None, :], 0.0, logits), axis=1)
    local_max = jnp.max(masked, axis=1)
    row_max = lax.pmax(local_max, "vocab")
    exp_local = jnp.sum(jnp.exp(masked - row_max[:, None]), axis=1)
    exp_total, smooth_total, target_total = lax.psum((exp_local, smooth_term, target_term), "vocab")
    log_total = row_max + jnp.log(exp_total)
    per_row = log_total - (1.0 - SMOOTH) * target_total - SMOOTH * smooth_total / (vocab_total - 1)
    counted = (loss_positions < target_lengths[:, None]).reshape(-1).astype(jnp.float32)
    loss_sum, token_count = lax.psum((jnp.sum(counted * per_row), jnp.sum(counted)), "dp")
    softmax_rows = jnp.exp(masked - log_total[:, None])
    grad_logits = (counted / token_count)[:, None] * (
        softmax_rows - (1.0 - SMOOTH) * target_hit - SMOOTH / (vocab_total - 1)
    )
    grad_logits = lowered(jnp.where(padding[None, :], 0.0, grad_logits))
    grad_selected = lax.psum(matmul(grad_logits, emb_table).astype(jnp.bfloat16), "vocab").astype(
        jnp.float32
    )
    grad_final = jnp.zeros_like(final).at[chosen].add(grad_selected)
    grad_dec_out, gain_six, shift_six = norm_backward(grad_final, final_kept, gain_rows[6])
    grad_dec_stream, grad_memory, dec_block_grads, dec_feed_grads, dec_norm_grads = layer_backward(
        grad_dec_out, memory_low, dec_blocks, dec_feed, gain_rows, dec_kept, batch_size
    )
    grad_enc_out, gain_two, shift_two = norm_backward(grad_memory, memory_kept, gain_rows[2])
    grad_enc_stream, _, enc_block_grads, enc_feed_grads, enc_norm_grads = layer_backward(
        grad_enc_out, None, enc_blocks, enc_feed, gain_rows, enc_kept, batch_size
    )
    grad_attn_in = jnp.stack([enc_block_grads[0][0], dec_block_grads[0][0], dec_block_grads[1][0]])
    grad_attn_out = jnp.stack([enc_block_grads[0][1], dec_block_grads[0][1], dec_block_grads[1][1]])
    grad_up_all = jnp.stack([enc_feed_grads[0], dec_feed_grads[0]])
    grad_down_all = jnp.stack([enc_feed_grads[1], dec_feed_grads[1]])
    grad_norms = jnp.zeros((14, model_width), jnp.float32)
    for norm_row, grad_gain, grad_shift in (
        enc_norm_grads + dec_norm_grads + [(2, gain_two, shift_two), (6, gain_six, shift_six)]
    ):
        grad_norms = grad_norms.at[norm_row].set(grad_gain).at[norm_row + 7].set(grad_shift)
    grad_tokens = jnp.concatenate([grad_enc_stream, grad_dec_stream], axis=0) * root_width
    head_term = contract_rows(grad_logits, selected)
    lookup_term = (
        jnp.zeros((shard_rows, model_width), jnp.float32)
        .at[safe_rows]
        .add(jnp.where(inside[:, None], grad_tokens, 0.0))
    )
    g_attn_in, g_attn_out, g_up, g_down, g_norms, g_embedding = (
        lax.psum_scatter(
            grad_attn_in.astype(jnp.bfloat16), "dp", scatter_dimension=1, tiled=True
        ).astype(jnp.float32),
        lax.psum_scatter(
            grad_attn_out.astype(jnp.bfloat16), "dp", scatter_dimension=1, tiled=True
        ).astype(jnp.float32),
        lax.psum_scatter(
            grad_up_all.astype(jnp.bfloat16), "dp", scatter_dimension=1, tiled=True
        ).astype(jnp.float32),
        lax.psum_scatter(
            grad_down_all.astype(jnp.bfloat16), "dp", scatter_dimension=1, tiled=True
        ).astype(jnp.float32),
        lax.psum_scatter(
            grad_norms.astype(jnp.bfloat16), "dp", scatter_dimension=1, tiled=True
        ).astype(jnp.float32),
        lax.psum_scatter(
            (head_term + lookup_term).astype(jnp.bfloat16), "dp", scatter_dimension=1, tiled=True
        ).astype(jnp.float32),
    )
    gradients = (g_embedding, g_attn_in, g_attn_out, g_up, g_down, g_norms)
    dense_squares = sum((jnp.sum(member * member) for member in gradients[1:]))
    squares = lax.psum(
        dense_squares / lax.axis_size("vocab") + jnp.sum(g_embedding * g_embedding), ("dp", "vocab")
    )
    grad_norm = jnp.sqrt(squares)
    factor = jnp.minimum(1.0, CLIP / (grad_norm + 1e-06))
    params = (embedding, attn_in, attn_out, ffn_up, ffn_down, norms)
    firsts = (
        embedding_first,
        attn_in_first,
        attn_out_first,
        ffn_up_first,
        ffn_down_first,
        norms_first,
    )
    seconds = (
        embedding_second,
        attn_in_second,
        attn_out_second,
        ffn_up_second,
        ffn_down_second,
        norms_second,
    )
    updated = [
        adam_update(params[slot], firsts[slot], seconds[slot], gradients[slot], factor, RATES[slot])
        for slot in range(6)
    ]
    return (
        loss_sum,
        token_count,
        grad_norm,
        updated[0][0],
        updated[1][0],
        updated[2][0],
        updated[3][0],
        updated[4][0],
        updated[5][0],
        updated[0][1],
        updated[1][1],
        updated[2][1],
        updated[3][1],
        updated[4][1],
        updated[5][1],
        updated[0][2],
        updated[1][2],
        updated[2][2],
        updated[3][2],
        updated[4][2],
        updated[5][2],
    )


def solution(mesh):
    placed = (
        P("dp", None),
        P("dp", None),
        P("dp"),
        P("dp", None),
        P("vocab", "dp"),
        P(None, "dp", None),
        P(None, "dp", None),
        P(None, "dp", None),
        P(None, "dp", None),
        P(None, "dp"),
        P("vocab", "dp"),
        P(None, "dp", None),
        P(None, "dp", None),
        P(None, "dp", None),
        P(None, "dp", None),
        P(None, "dp"),
        P("vocab", "dp"),
        P(None, "dp", None),
        P(None, "dp", None),
        P(None, "dp", None),
        P(None, "dp", None),
        P(None, "dp"),
    )
    return jax.shard_map(
        local,
        mesh=mesh,
        in_specs=placed,
        out_specs=(
            P(),
            P(),
            P(),
            P("vocab", "dp"),
            P(None, "dp", None),
            P(None, "dp", None),
            P(None, "dp", None),
            P(None, "dp", None),
            P(None, "dp"),
            P("vocab", "dp"),
            P(None, "dp", None),
            P(None, "dp", None),
            P(None, "dp", None),
            P(None, "dp", None),
            P(None, "dp"),
            P("vocab", "dp"),
            P(None, "dp", None),
            P(None, "dp", None),
            P(None, "dp", None),
            P(None, "dp", None),
            P(None, "dp"),
        ),
        check_vma=False,
    )
```

profile of v0, /device:TPU:0, one launch (start us, length us, event | category | flops | bytes accessed | tf_op | source)
XLA Modules:
  0.0 2935.2 jit_solution(7523547431637875519)
XLA Ops:
  7.2 6.2 convert_element_type.265
  17.2 700.8 %all-gather.7.cloned.1.call-done = bf16[24026,768]{0,1:T(8,128)(2,1)} async-done(((bf16[24026,96]{0,1:T(8,128)(2,1)}), bf16[24026,768]{0,1:T(8,128)(2,1)}) %all-gather.7.cloned.1.call-update) | async-done | bytes 36903952 | tf_op jit(solution)/shard_map/all_gather | solution.py:241
  718.0 48.4 %copy.144 = bf16[24026,768]{1,0:T(8,128)(2,1)} copy(bf16[24026,768]{0,1:T(8,128)(2,1)} %all-gather.7.cloned.1.call-done) | data formatting | bytes 73807872 | tf_op jit(solution)/shard_map/all_gather | solution.py:241
  766.4 24.0 gather_fusion
  795.2 2.8 convert_element_type.286
  798.8 31.2 %all-gather = bf16[8,96,14]{1,2,0:T(8,128)(2,1)S(1)} all-gather(bf16[1,96,14]{1,2,0:T(8,128)(2,1)S(1)} %convert_bitcast_fusion), channel_id=1, replica_groups=mesh['dp'=8,'vocab'=4] {'dp'}, dimensions={0}, use_global_device_ids=true | all-gather | bytes 24192 | tf_op jit(solution)/shard_map/all_gather | solution.py:246
  835.5 2.8 fusion.88
  838.9 34.9 %all-gather.9.cloned.1.call-done = bf16[3,768,2304]{2,1,0:T(8,128)(2,1)} async-done(((bf16[3,96,2304]{2,1,0:T(8,128)(2,1)}), bf16[3,768,2304]{2,1,0:T(8,128)(2,1)}) %all-gather.9.cloned.1.call-update) | async-done | bytes 10616848 | tf_op jit(solution)/shard_map/all_gather | solution.py:242
  873.8 4.0 slice_bitcast_fusion.18
  877.8 34.4 %all-reduce.6.cloned.1.call-done = bf16[768,768]{1,0:T(8,128)(2,1)} async-done(((bf16[768,768]{1,0:T(8,128)(2,1)}), bf16[768,768]{1,0:T(8,128)(2,1)}) %all-reduce.6.cloned.1.call-update) | async-done | bytes 1179664 | tf_op jit(solution)/shard_map/psum | solution.py:262
  915.6 3.2 convolution_convert_fusion.7
  923.8 4.1 convolution_convert_fusion.6
  939.2 3.6 fusion.69
  942.8 37.5 %all-gather.11.cloned.1.call-done = bf16[3,768,768]{2,1,0:T(8,128)(2,1)} async-done(((bf16[3,96,768]{2,1,0:T(8,128)(2,1)}), bf16[3,768,768]{2,1,0:T(8,128)(2,1)}) %all-gather.11.cloned.1.call-update) | async-done | bytes 3538960 | tf_op jit(solution)/shard_map/all_gather | solution.py:243
  983.8 135.6 %all-gather.13.cloned.1.call-done = bf16[2,768,3072]{2,1,0:T(8,128)(2,1)} async-done(((bf16[2,96,3072]{2,1,0:T(8,128)(2,1)}), bf16[2,768,3072]{2,1,0:T(8,128)(2,1)}) %all-gather.13.cloned.1.call-update) | async-done | bytes 9437200 | tf_op jit(solution)/shard_map/all_gather | solution.py:244
  1119.5 7.0 fusion.19
  1126.5 131.9 %all-gather.15.cloned.1.call-done = bf16[2,3072,768]{2,1,0:T(8,128)(2,1)} async-done(((bf16[2,384,768]{2,1,0:T(8,128)(2,1)}), bf16[2,3072,768]{2,1,0:T(8,128)(2,1)}) %all-gather.15.cloned.1.call-update) | async-done | bytes 9437200 | tf_op jit(solution)/shard_map/all_gather | solution.py:245
  1258.4 7.8 fusion.147
  1291.1 2.8 fusion.149
  1302.7 21.4 select_reduce_fusion.2
  1324.1 6.3 pmax.7
  1330.4 4.8 exponential_reduce_fusion
  1335.2 6.7 all-reduce.2
  1343.2 19.8 all-reduce.1
  1363.7 18.3 convolution_convert_fusion.18
  1382.8 26.8 all-reduce.8.cloned.1.call-done
  1416.1 5.2 fusion.28
  1429.3 5.2 fusion.63
  1434.5 4.3 multiply_reduce_fusion.2
  1443.6 2.7 multiply_reduce_fusion.20
  1460.0 6.8 multiply_convert_fusion.1
  1466.8 3.2 multiply_reduce_fusion.8
  1473.7 7.9 fusion.66
  1481.6 9.1 multiply_reduce_fusion
  1490.8 7.2 multiply_convert_fusion
  1507.1 4.1 multiply_reduce_fusion.5
  1515.9 3.4 pad_maximum_fusion.3
  1520.5 5.3 fusion.16
  1525.9 5.2 fusion.13
  1531.1 8.3 pad_maximum_fusion.1
  1540.5 6.3 fusion.17
  1546.8 7.8 fusion.14
  1554.6 8.2 pad_maximum_fusion.2
  1572.6 4.9 pad_maximum_fusion
  1578.4 31.0 %fusion.124 = f32[24026,768]{1,0:T(8,128)} fusion(bf16[64,768]{1,0:T(8,128)(2,1)S(1)} %copy-done.76, pred[64]{0:T(512)(128)(4,1)S(1)} %copy-done.157, f32[64,24026]{1,0:T(8,128)} %get-tuple-element.514, f32[64]{0:T(128)S(1)} %copy-done.145, f32[64]{0:T(128)S(1)} %copy-done.147, s32[64]{0:T(128)S(1)} %copy-done.117, pred[24026]{0:T(1024)(128)(4,1)S(1)} %copy-done.88), kind=kOutput, calls=%fused_computation.346 | convolution fusion | flops 2375739904 | bytes 80081688 | tf_op jit(solution)/shard_map/dot_general | solution.py:39
  1612.8 123.1 %scatter_fusion = f32[24026,768]{1,0:T(8,128)} fusion(f32[24026,768]{1,0:T(8,128)} %fusion.124, s32[768]{0:T(1024)S(1)} %copy-done.109, f32[768,768]{1,0:T(8,128)S(1)} %fusion.50), kind=kCustom, calls=%fused_computation.4 | custom fusion | flops 589824 | bytes 7080960 | tf_op jit(solution)/shard_map/scatter-add | solution.py:335
  1736.0 36.3 %convert_element_type.341 = bf16[24026,768]{1,0:T(8,128)(2,1)} convert(f32[24026,768]{1,0:T(8,128)} %scatter_fusion) | non-fusion elementwise | flops 18451968 | bytes 110711808 | tf_op jit(solution)/shard_map/convert_element_type | solution.py:354
  1772.3 43.2 %copy.185 = bf16[24026,768]{0,1:T(8,128)(2,1)} copy(bf16[24026,768]{1,0:T(8,128)(2,1)} %convert_element_type.341) | data formatting | bytes 73807872
  1815.5 11.6 copy.170
  1827.1 11.6 copy.167
  1844.6 148.3 %reduce-scatter.17.cloned.1.call-done = bf16[2,384,768]{2,1,0:T(8,128)(2,1)} async-done(((bf16[2,3072,768]{2,1,0:T(8,128)(2,1)}), bf16[2,384,768]{2,1,0:T(8,128)(2,1)}) %reduce-scatter.17.cloned.1.call-update) | async-done | bytes 1179664 | tf_op jit(solution)/shard_map/reduce_scatter | solution.py:347
  1995.3 180.3 %reduce-scatter.11.cloned.1.call-done = bf16[3,96,2304]{2,1,0:T(8,128)(2,1)} async-done(((bf16[3,768,2304]{2,1,0:T(8,128)(2,1)}), bf16[3,96,2304]{2,1,0:T(8,128)(2,1)}) %reduce-scatter.11.cloned.1.call-update) | async-done | bytes 1327120 | tf_op jit(solution)/shard_map/reduce_scatter | solution.py:338
  2181.5 592.2 %reduce-scatter.21.cloned.1.call-done = bf16[96,24026]{1,0:T(8,128)(2,1)} async-done(((bf16[768,24026]{1,0:T(8,128)(2,1)}), bf16[96,24026]{1,0:T(8,128)(2,1)}) %reduce-scatter.21.cloned.1.call-update) | async-done | bytes 4613008
  2773.6 7.8 copy.186
  2781.5 5.9 fusion.2
  2788.0 11.6 copy.168
  2799.6 39.5 %psum.63 = f32[]{:T(128)} all-reduce(f32[]{:T(128)S(6)} %add.523), channel_id=1, replica_groups=mesh['dp'=8,'vocab'=4] {'dp','vocab'}, use_global_device_ids=true, to_apply=%region_79.80 | all-reduce | flops 1 | bytes 8 | tf_op jit(solution)/shard_map/psum | solution.py:359
  2839.9 29.9 %multiply_subtract_fusion = (f32[24026,96]{1,0:T(8,128)}, f32[24026,96]{1,0:T(8,128)}, f32[24026,96]{1,0:T(8,128)}) fusion(f32[24026,96]{1,0:T(8,128)} %copy.170, f32[]{:T(128)S(6)} %min.19, bf16[24026,96]{1,0:T(8,128)(2,1)} %copy.186, f32[24026,96]{1,0:T(8,128)} %copy.167, f32[24026,96]{1,0:T(8,128)} %copy.168), kind=kLoop, calls=%fused_computation.17 | loop fusion | flops 39210432 | bytes 59968900 | tf_op jit(solution)/shard_map/sub | solution.py:211
  2869.8 11.9 copy.171
  2881.8 11.9 copy.172
  2893.7 12.1 copy.173
  2906.5 7.7 multiply_subtract_fusion.1
  2917.2 4.4 multiply_subtract_fusion.3
  2923.1 4.1 multiply_subtract_fusion.2
  (637 shorter events, 154.0 us)
Async XLA Ops:
  7.2 710.8 %all-gather.7.cloned.1.call-start = ((), (), s32[]{:S(2)}) async-start(), calls=%async_computation.6 | async-start | bytes 41582592 | tf_op jit(solution)/shard_map/all_gather | solution.py:241
  13.5 860.3 %all-gather.9.cloned.1.call-start = ((), (), s32[]{:S(2)}) async-start(), calls=%async_computation.8 | async-start | bytes 11943936 | tf_op jit(solution)/shard_map/all_gather | solution.py:242
  16.4 895.8 %all-reduce.6.cloned.1.call-start = ((), (), s32[]{:S(2)}) async-start(), calls=%async_computation.7 | async-start | bytes 2359296 | tf_op jit(solution)/shard_map/psum | solution.py:262
  17.2 773.3 %copy-start.154 = (pred[768]{0:T(1024)(128)(4,1)}, pred[768]{0:T(1024)(128)(4,1)S(1)}, u32[]{:S(2)}) copy-start(pred[768]{0:T(1024)(128)(4,1)S(1)} %get-tuple-element.491) | copy-start | bytes 2308
  791.9 188.4 %all-gather.11.cloned.1.call-start = ((), (), s32[]{:S(2)}) async-start(), calls=%async_computation.9 | async-start | bytes 3981312 | tf_op jit(solution)/shard_map/all_gather | solution.py:243
  793.9 325.6 %all-gather.13.cloned.1.call-start = ((), (), s32[]{:S(2)}) async-start(), calls=%async_computation.10 | async-start | bytes 10616832 | tf_op jit(solution)/shard_map/all_gather | solution.py:244
  795.1 35.0 %copy-start.171 = (s32[1,64]{1,0:T(1,128)S(1)}, s32[1,64]{1,0:T(1,128)}, u32[]{:S(2)}) copy-start(s32[1,64]{1,0:T(1,128)} %param.53) | copy-start | bytes 772
  795.2 463.2 %all-gather.15.cloned.1.call-start = ((), (), s32[]{:S(2)}) async-start(), calls=%async_computation.11 | async-start | bytes 10616832 | tf_op jit(solution)/shard_map/all_gather | solution.py:245
  798.0 611.6 %all-reduce.8.cloned.1.call-start = ((), (), s32[]{:S(2)}) async-start(), calls=%async_computation.12 | async-start | bytes 196608 | tf_op jit(solution)/shard_map/psum | solution.py:309
  832.9 82.7 %copy-start.131 = (f32[768]{0:T(1024)}, f32[768]{0:T(1024)S(1)}, u32[]{:S(2)}) copy-start(f32[768]{0:T(1024)S(1)} %get-tuple-element.452) | copy-start | bytes 9220
  832.9 82.7 %copy-start.180 = (f32[768]{0:T(1024)}, f32[768]{0:T(1024)S(1)}, u32[]{:S(2)}) copy-start(f32[768]{0:T(1024)S(1)} %get-tuple-element.451) | copy-start | bytes 9220
  832.9 443.6 %copy-start.105 = (f32[768]{0:T(1024)}, f32[768]{0:T(1024)S(1)}, u32[]{:S(2)}) copy-start(f32[768]{0:T(1024)S(1)} %get-tuple-element.444) | copy-start | bytes 9220
  832.9 461.3 %copy-start.95 = (f32[768]{0:T(1024)}, f32[768]{0:T(1024)S(1)}, u32[]{:S(2)}) copy-start(f32[768]{0:T(1024)S(1)} %get-tuple-element.442) | copy-start | bytes 9220
  832.9 461.3 %copy-start.101 = (f32[768]{0:T(1024)}, f32[768]{0:T(1024)S(1)}, u32[]{:S(2)}) copy-start(f32[768]{0:T(1024)S(1)} %get-tuple-element.441) | copy-start | bytes 9220
  832.9 465.7 %copy-start.103 = (f32[768]{0:T(1024)}, f32[768]{0:T(1024)S(1)}, u32[]{:S(2)}) copy-start(f32[768]{0:T(1024)S(1)} %get-tuple-element.439) | copy-start | bytes 9220
  920.0 351.0 %copy-start.49 = (bf16[256,768]{0,1:T(8,128)(2,1)}, bf16[256,768]{0,1:T(8,128)(2,1)S(1)}, u32[]{:S(2)}) copy-start(bf16[256,768]{0,1:T(8,128)(2,1)S(1)} %copy.147) | copy-start | bytes 1179652
  922.7 57.6 %copy-start.3 = (f32[512,768]{1,0:T(8,128)}, f32[512,768]{1,0:T(8,128)S(1)}, u32[]{:S(2)}) copy-start(f32[512,768]{1,0:T(8,128)S(1)} %get-tuple-element.480) | copy-start | bytes 4718596
  982.7 275.7 %copy-start.14 = (f32[512,768]{1,0:T(8,128)}, f32[512,768]{1,0:T(8,128)S(1)}, u32[]{:S(2)}) copy-start(f32[512,768]{1,0:T(8,128)S(1)} %get-tuple-element.502) | copy-start | bytes 4718596
  982.7 143.8 %copy-start.122 = (f32[512]{0:T(512)}, f32[512]{0:T(512)S(1)}, u32[]{:S(2)}) copy-start(f32[512]{0:T(512)S(1)} %broadcast_multiply_fusion.7) | copy-start | bytes 6148
  983.1 136.4 %copy-start.164 = (f32[512]{0:T(512)}, f32[512]{0:T(512)S(1)}, u32[]{:S(2)}) copy-start(f32[512]{0:T(512)S(1)} %add_rsqrt_fusion.1) | copy-start | bytes 6148
  1126.5 140.8 %copy-start.140 = (f32[768]{0:T(1024)S(1)}, f32[768]{0:T(1024)}, u32[]{:S(2)}) copy-start(f32[768]{0:T(1024)} %get-tuple-element.446) | copy-start | bytes 9220
  1126.5 140.8 %copy-start.178 = (f32[768]{0:T(1024)S(1)}, f32[768]{0:T(1024)}, u32[]{:S(2)}) copy-start(f32[768]{0:T(1024)} %get-tuple-element.445) | copy-start | bytes 9220
  1258.4 8.9 copy-start.46
  1285.4 9.4 slice-start.8
  1285.4 10.9 slice-start.17
  1288.6 7.7 slice-start.18
  1288.6 7.7 slice-start.19
  1298.3 25.8 copy-start.115
  1302.7 27.7 copy-start.116
  1324.1 17.8 copy-start.172
  1343.2 38.8 %copy-start.144 = (f32[64]{0:T(128)}, f32[64]{0:T(128)S(1)}, u32[]{:S(2)}) copy-start(f32[64]{0:T(128)S(1)} %get-tuple-element.478) | copy-start | bytes 772
  1363.7 18.3 copy-start.146
  1382.0 456.8 %reduce-scatter.19.cloned.1.call-start = ((), (), s32[]{:S(2)}) async-start(), calls=%async_computation.17 | async-start | bytes 221184
  1411.9 9.4 slice-start.11
  1429.3 9.5 slice-start.3
  1457.1 9.7 slice-start.14
  1459.9 10.2 copy-start.41
  1470.7 33.9 %copy-start.12 = (f32[512,768]{1,0:T(8,128)}, f32[512,768]{1,0:T(8,128)S(1)}, u32[]{:S(2)}) copy-start(f32[512,768]{1,0:T(8,128)S(1)} %multiply_add_fusion.1) | copy-start | bytes 4718596
  1473.7 8.0 copy-start.53
  1473.7 17.1 slice-start
  1473.7 17.1 slice-start.1
  1481.6 9.1 slice-start.2
  1497.9 8.4 slice-start.5
  1515.9 324.3 %reduce-scatter.13.cloned.1.call-start = ((), (), s32[]{:S(2)}) async-start(), calls=%async_computation.14 | async-start | bytes 3981312 | tf_op jit(solution)/shard_map/reduce_scatter | solution.py:341
  1519.4 322.6 %reduce-scatter.15.cloned.1.call-start = ((), (), s32[]{:S(2)}) async-start(), calls=%async_computation.15 | async-start | bytes 10616832 | tf_op jit(solution)/shard_map/reduce_scatter | solution.py:344
  1539.3 453.5 %reduce-scatter.17.cloned.1.call-start = ((), (), s32[]{:S(2)}) async-start(), calls=%async_computation.16 | async-start | bytes 10616832 | tf_op jit(solution)/shard_map/reduce_scatter | solution.py:347
  1562.9 612.8 %reduce-scatter.11.cloned.1.call-start = ((), (), s32[]{:S(2)}) async-start(), calls=%async_computation.13 | async-start | bytes 11943936 | tf_op jit(solution)/shard_map/reduce_scatter | solution.py:338
  1577.5 31.9 %copy-start.189 = (f32[256]{0:T(256)S(1)}, f32[256]{0:T(256)}, u32[]{:S(2)}) copy-start(f32[256]{0:T(256)} %get-tuple-element.420) | copy-start | bytes 3076
  1577.5 31.9 %copy-start.188 = (f32[256]{0:T(256)S(1)}, f32[256]{0:T(256)}, u32[]{:S(2)}) copy-start(f32[256]{0:T(256)} %get-tuple-element.434) | copy-start | bytes 3076
  1577.5 31.9 %copy-start.183 = (f32[512]{0:T(512)S(1)}, f32[512]{0:T(512)}, u32[]{:S(2)}) copy-start(f32[512]{0:T(512)} %get-tuple-element.411) | copy-start | bytes 6148
  1577.5 31.9 %copy-start.182 = (f32[512]{0:T(512)S(1)}, f32[512]{0:T(512)}, u32[]{:S(2)}) copy-start(f32[512]{0:T(512)} %get-tuple-element.419) | copy-start | bytes 6148
  1577.5 31.9 %copy-start.23 = (f32[256,768]{1,0:T(8,128)S(1)}, f32[256,768]{1,0:T(8,128)}, u32[]{:S(2)}) copy-start(f32[256,768]{1,0:T(8,128)} %copy-done.21) | copy-start | bytes 2359300
  1577.6 31.9 %copy-start.133 = (f32[768]{0:T(1024)S(1)}, f32[768]{0:T(1024)}, u32[]{:S(2)}) copy-start(f32[768]{0:T(1024)} %copy-done.131) | copy-start | bytes 9220
  1577.6 31.9 %copy-start.150 = (f32[256]{0:T(256)S(1)}, f32[256]{0:T(256)}, u32[]{:S(2)}) copy-start(f32[256]{0:T(256)} %copy-done.148) | copy-start | bytes 3076
  1577.6 31.9 %copy-start.175 = (f32[256]{0:T(256)S(1)}, f32[256]{0:T(256)}, u32[]{:S(2)}) copy-start(f32[256]{0:T(256)} %copy-done.173) | copy-start | bytes 3076
  1577.6 1196.0 %reduce-scatter.21.cloned.1.call-start = ((), (), s32[]{:S(2)}) async-start(), calls=%async_computation.18 | async-start | bytes 41582592
  2893.7 12.1 copy-start.111
  2893.7 12.1 copy-start.168
  2893.7 12.1 copy-start.169
  2893.7 12.7 copy-start.30
  2906.5 7.7 copy-start.65
  2906.5 7.7 copy-start.77
  2906.5 9.7 copy-start.61
  2906.5 9.7 copy-start.62
  (165 other events, 531.2 us)
Sparse Core Ops, SparseCore 0:
  13.6 704.3 all-gather.6
  720.7 153.0 all-gather.8
  876.8 35.4 all-reduce.5
  914.9 65.3 all-gather.10
  982.9 136.5 all-gather.12
  1122.1 136.2 all-gather.14
  1382.1 27.4 all-reduce.7
  1516.0 61.1 reduce-scatter.18
  1581.3 78.1 reduce-scatter.12
  1663.3 162.9 reduce-scatter.14
  1830.4 162.4 reduce-scatter.16
  1996.7 178.8 reduce-scatter.10
  2179.6 593.9 reduce-scatter.20
where the time goes:
time: 2950 us; the launch traced here: 2940 us
  waiting for transfers between devices  2020 us (68%)
  other arithmetic  310 us (11%)
  local copies, waits for them, and re-layouts  242 us (8%)
  matrix products  231 us (8%)
  blocking collectives  103 us (3%)
    all_gather x1, waiting for transfers between devices, local(): lax.all_gather(lowered(embedding), 'dp', axis=1, tiled=True)  701 us
    unnamed x15, waiting for transfers between devices  592 us
    reduce_scatter x1, waiting for transfers between devices, local(): lax.psum_scatter(grad_attn_in.astype(jnp.bfloat16), 'dp', scatter_dimensi...  180 us
    reduce_scatter x1, waiting for transfers between devices, local(): lax.psum_scatter(grad_down_all.astype(jnp.bfloat16), 'dp', scatter_dimens...  148 us
    unnamed x442, local copies, waits for them, and re-layouts  146 us
    all_gather x1, waiting for transfers between devices, local(): lax.all_gather(lowered(ffn_up), 'dp', axis=1, tiled=True)  136 us
    all_gather x1, waiting for transfers between devices, local(): lax.all_gather(lowered(ffn_down), 'dp', axis=1, tiled=True)  132 us
    scatter-add x1, other arithmetic, local(): lookup_term = jnp.zeros((shard_rows, model_width), jnp.float32).at[safe_r...  123 us
  transfers between devices with their start and end apart: 13, of which 10 were waited for; matrix products, arithmetic and copies ran while one was open for 16% of the time, Pallas kernels for 0%

commit v1 on v0

--- a/solution.py
+++ b/solution.py
@@ -3,7 +3,10 @@
 
 import jax
 import jax.numpy as jnp
+import numpy as np
 from jax import lax
+from jax.experimental import pallas as pl
+from jax.experimental.pallas import tpu as pltpu
 from jax.sharding import PartitionSpec as P
 
 HEADS = 12
@@ -55,7 +58,7 @@
     return (normed * gain_row + shift_row, (normed, scale_inv))
 
 
-def norm_backward(grad_out, saved_parts, gain_row):
+def norm_backward_rows(grad_out, saved_parts, gain_row):
     normed, scale_inv = saved_parts
     grad_normed = grad_out * gain_row
     grad_in = scale_inv * (
@@ -162,7 +165,7 @@
         times_transposed(grad_low, w_down) * sigmoid_pre * (1.0 + hidden_pre * (1.0 - sigmoid_pre))
     )
     grad_up = contract_rows(hidden_in, grad_pre)
-    grad_in, grad_gain, grad_shift = norm_backward(
+    grad_in, grad_gain, grad_shift = norm_backward_rows(
         times_transposed(grad_pre, w_up), norm_kept, gain_rows[norm_row]
     )
     grad_stream = grad_stream + grad_in
@@ -192,7 +195,7 @@
             )
             grad_normed = times_transposed(grad_queries, w_in[:, :model_width])
             grad_memory = times_transposed(grad_pair, w_in[:, model_width:])
-        grad_in, grad_gain, grad_shift = norm_backward(grad_normed, norm_kept, gain_rows[norm_row])
+        grad_in, grad_gain, grad_shift = norm_backward_rows(grad_normed, norm_kept, gain_rows[norm_row])
         grad_stream = grad_stream + grad_in
         norm_grads.append((norm_row, grad_gain, grad_shift))
         block_grads[block_order] = (grad_w_in, grad_w_out)
@@ -211,7 +214,7 @@
     return (weight - rate * (corrected + DECAY * weight), new_first, new_second)
 
 
-def local(
+def local_copied(
     enc_ids,
     labels,
     target_lengths,
@@ -310,11 +313,11 @@
         jnp.float32
     )
     grad_final = jnp.zeros_like(final).at[chosen].add(grad_selected)
-    grad_dec_out, gain_six, shift_six = norm_backward(grad_final, final_kept, gain_rows[6])
+    grad_dec_out, gain_six, shift_six = norm_backward_rows(grad_final, final_kept, gain_rows[6])
     grad_dec_stream, grad_memory, dec_block_grads, dec_feed_grads, dec_norm_grads = layer_backward(
         grad_dec_out, memory_low, dec_blocks, dec_feed, gain_rows, dec_kept, batch_size
     )
-    grad_enc_out, gain_two, shift_two = norm_backward(grad_memory, memory_kept, gain_rows[2])
+    grad_enc_out, gain_two, shift_two = norm_backward_rows(grad_memory, memory_kept, gain_rows[2])
     grad_enc_stream, _, enc_block_grads, enc_feed_grads, enc_norm_grads = layer_backward(
         grad_enc_out, None, enc_blocks, enc_feed, gain_rows, enc_kept, batch_size
     )
@@ -407,6 +410,1289 @@
     )
 
 
+VMEM_BYTES = 60 * 1024 * 1024
+
+
+def positions_numpy(length, model_width):
+    place = np.arange(length, dtype=np.float32)[:, None]
+    index = np.arange(model_width // 2, dtype=np.float32)[None, :]
+    angles = place * np.exp(index * np.float32(-2.0 * math.log(10000.0) / model_width))
+    return np.concatenate([np.sin(angles), np.cos(angles)], axis=1).astype(np.float32)
+
+
+def pick_kernel(ids_ref, table_ref, out_ref, list_ref, count_ref, wide_ref):
+    count, rows = wide_ref.shape[0], table_ref.shape[0]
+
+    def one(step, found):
+        for inner in range(8):
+            slot = step * 8 + inner
+            row = ids_ref[slot]
+            hit = (row >= 0) & (row < rows)
+            safe = jnp.where(hit, row, 0)
+            wide_ref[pl.ds(slot, 1), :] = table_ref[pl.ds(safe, 1), :] * jnp.where(hit, 1.0, 0.0)
+            list_ref[found] = slot
+            found = found + jnp.where(hit, 1, 0)
+        return found
+
+    count_ref[0] = lax.fori_loop(0, count // 8, one, 0)
+    out_ref[...] = wide_ref[...].astype(jnp.bfloat16)
+
+
+def pick_rows(local_ids, table):
+    count, width = local_ids.shape[0], table.shape[1]
+    return pl.pallas_call(
+        pick_kernel,
+        out_shape=(
+            jax.ShapeDtypeStruct((count, width), jnp.bfloat16),
+            jax.ShapeDtypeStruct((count + 8,), jnp.int32),
+            jax.ShapeDtypeStruct((1,), jnp.int32),
+        ),
+        in_specs=[
+            pl.BlockSpec(memory_space=pltpu.SMEM),
+            pl.BlockSpec(memory_space=pltpu.VMEM),
+        ],
+        out_specs=(
+            pl.BlockSpec(memory_space=pltpu.VMEM),
+            pl.BlockSpec(memory_space=pltpu.SMEM),
+            pl.BlockSpec(memory_space=pltpu.SMEM),
+        ),
+        scratch_shapes=[pltpu.VMEM((count, width), jnp.float32)],
+        compiler_params=pltpu.CompilerParams(vmem_limit_bytes=VMEM_BYTES),
+        name="pick_rows",
+    )(local_ids, table)
+
+
+def spread_kernel(ids_ref, list_ref, count_ref, grads_ref, zero_ref, one_ref, two_ref, out_ref, squares_ref, wide_ref, rows_ref):
+    width = grads_ref.shape[1]
+    chunks, _, piece_columns = zero_ref.shape
+    chunk = 3 * piece_columns
+    rows_ref[...] = grads_ref[...].astype(jnp.float32)
+    wide_ref[...] = jnp.zeros_like(wide_ref)
+
+    def one(step, carry):
+        slot = list_ref[step]
+        row = ids_ref[slot]
+        wide_ref[pl.ds(row, 1), 0:width] += rows_ref[pl.ds(slot, 1), :]
+        return carry
+
+    lax.fori_loop(0, count_ref[0], one, 0)
+
+    def turn(piece, total):
+        for part in range(chunk // 128):
+            start = pl.multiple_of(piece * chunk + part * 128, 128)
+            head_ref = (zero_ref, one_ref, two_ref)[part * 128 // piece_columns]
+            column = part * 128 % piece_columns
+            block = jnp.transpose(wide_ref[pl.ds(start, 128), :])[:width]
+            block = block + head_ref[piece, :, column : column + 128].astype(jnp.float32)
+            out_ref[:, pl.ds(start, 128)] = block
+            total = total + block * block
+        return total
+
+    total = lax.fori_loop(0, chunks, turn, jnp.zeros((width, 128), jnp.float32))
+    squares_ref[...] = jnp.sum(total, axis=0, keepdims=True)
+
+
+def spread_rows(local_ids, hit_list, hit_count, grads, head):
+    chunks, width, piece_columns = head[0].shape
+    chunk = 3 * piece_columns
+    return pl.pallas_call(
+        spread_kernel,
+        out_shape=(
+            jax.ShapeDtypeStruct((width, chunks * chunk), jnp.float32),
+            jax.ShapeDtypeStruct((1, 128), jnp.float32),
+        ),
+        in_specs=[pl.BlockSpec(memory_space=pltpu.SMEM)] * 3
+        + [pl.BlockSpec(memory_space=pltpu.VMEM)] * 4,
+        out_specs=(
+            pl.BlockSpec(memory_space=pltpu.VMEM),
+            pl.BlockSpec(memory_space=pltpu.VMEM),
+        ),
+        scratch_shapes=[
+            pltpu.VMEM((chunks * chunk, 128), jnp.float32),
+            pltpu.VMEM(grads.shape, jnp.float32),
+        ],
+        compiler_params=pltpu.CompilerParams(vmem_limit_bytes=VMEM_BYTES),
+        name="spread_rows",
+    )(local_ids, hit_list, hit_count, grads, *head)
+
+
+MESH = pl.DeviceIdType.MESH
+
+
+def meet(devices):
+    barrier = pltpu.get_barrier_semaphore()
+    for device in devices:
+        pl.semaphore_signal(barrier, inc=1, device_id=device, device_id_type=MESH)
+    pl.semaphore_wait(barrier, len(devices))
+
+
+def send(source, target, send_sem, recv_sem, device):
+    copy = pltpu.make_async_remote_copy(
+        src_ref=source,
+        dst_ref=target,
+        send_sem=send_sem,
+        recv_sem=recv_sem,
+        device_id=device,
+        device_id_type=MESH,
+    )
+    copy.start()
+    return copy
+
+
+def places():
+    group, share = lax.axis_index("dp"), lax.axis_index("vocab")
+    core = lax.rem(share, 2)
+    core_peer = (group, share + 1 - 2 * core)
+    side_peer = (group, lax.rem(share + 2, 4))
+    return group, share, core, core_peer, side_peer
+
+
+def group_peers(group, share, groups):
+    return [(lax.rem(group + step, groups), share) for step in range(1, groups)]
+
+
+def share_peers(group, share, shares):
+    return [(group, lax.rem(share + step, shares)) for step in range(1, shares)]
+
+
+def total_scratch(rows, width):
+    half = rows // 2
+    return [
+        pltpu.VMEM((rows, width), jnp.float32),
+        pltpu.VMEM((4, half, width), jnp.bfloat16),
+        pltpu.VMEM((rows, width), jnp.bfloat16),
+        pltpu.SemaphoreType.DMA((6,)),
+    ]
+
+
+class Total:
+    def __init__(self, refs):
+        self.part, self.bufs, self.total, self.sems = refs
+        _, _, core, self.core_peer, self.side_peer = places()
+        half = self.part.shape[0] // 2
+        self.mine = pl.ds(pl.multiple_of(core * half, half), half)
+        self.other = pl.ds(pl.multiple_of((1 - core) * half, half), half)
+
+    def begin(self, partial_rows):
+        self.part[...] = partial_rows
+        self.bufs[0] = lowered(self.part[self.other, :])
+        self.one = send(
+            self.bufs.at[0], self.bufs.at[1], self.sems.at[0], self.sems.at[1], self.core_peer
+        )
+
+    def middle(self):
+        self.one.wait_recv()
+        self.bufs[2] = lowered(self.part[self.mine, :] + self.bufs[1].astype(jnp.float32))
+        self.two = send(
+            self.bufs.at[2], self.bufs.at[3], self.sems.at[2], self.sems.at[3], self.side_peer
+        )
+
+    def last(self):
+        self.two.wait_recv()
+        self.total[self.mine, :] = lowered(
+            self.bufs[2].astype(jnp.float32) + self.bufs[3].astype(jnp.float32)
+        )
+        piece = self.total.at[self.mine, :]
+        self.three = send(piece, piece, self.sems.at[4], self.sems.at[5], self.core_peer)
+
+    def finish(self):
+        self.three.wait()
+        self.one.wait_send()
+        self.two.wait_send()
+        return self.total[...].astype(jnp.float32)
+
+    def rest(self):
+        self.middle()
+        self.last()
+        return self.finish()
+
+
+class Exchange:
+    def __init__(self, source_ref, target_ref, sems, groups, index):
+        group, share = lax.axis_index("dp"), lax.axis_index("vocab")
+        columns = target_ref.shape[2]
+        at = pl.ds(index * columns, columns)
+        self.copies = [
+            send(
+                source_ref.at[peer[0], :, at],
+                target_ref.at[group],
+                sems.at[0, step],
+                sems.at[1, step],
+                peer,
+            )
+            for step, peer in enumerate(group_peers(group, share, groups))
+        ]
+        self.keep = pltpu.make_async_copy(
+            source_ref.at[group, :, at], target_ref.at[group], sems.at[0, groups - 1]
+        )
+        self.keep.start()
+
+    def finish(self):
+        self.keep.wait()
+        for copy in self.copies:
+            copy.wait()
+
+
+def in_vmem(count, at_rest=()):
+    return [
+        pl.BlockSpec(memory_space=pl.ANY if index in at_rest else pltpu.VMEM)
+        for index in range(count)
+    ]
+
+
+def call(kernel, name, number, inputs, out_shape, scratch, flops, rest_in=(), rest_out=()):
+    moved = sum(math.prod(member.shape) * member.dtype.itemsize for member in (*inputs, *out_shape))
+    return pl.pallas_call(
+        kernel,
+        out_shape=tuple(out_shape),
+        in_specs=in_vmem(len(inputs), rest_in),
+        out_specs=tuple(in_vmem(len(out_shape), rest_out)),
+        scratch_shapes=scratch,
+        compiler_params=pltpu.CompilerParams(
+            collective_id=number, has_side_effects=True, vmem_limit_bytes=VMEM_BYTES
+        ),
+        cost_estimate=pl.CostEstimate(flops=flops, bytes_accessed=moved, transcendentals=0),
+        name=name,
+    )(*inputs)
+
+
+def shape_of(shape, dtype):
+    return jax.ShapeDtypeStruct(shape, dtype)
+
+
+def head_slice(ref, start, index):
+    low = start + index * HEAD_DIM
+    return ref[:, low : low + HEAD_DIM]
+
+
+def masked_scores(query, key, causal):
+    scores = times_transposed(query, key) * HEAD_DIM ** (-0.5)
+    if causal:
+        down = lax.broadcasted_iota(jnp.int32, scores.shape, 0)
+        across = lax.broadcasted_iota(jnp.int32, scores.shape, 1)
+        scores = jnp.where(down >= across, scores, -1e30)
+    return scores
+
+
+def heads_forward(q_ref, kv_ref, starts, context_ref, logs_ref, causal):
+    q_start, k_start, v_start = starts
+    for index in range(context_ref.shape[1] // HEAD_DIM):
+        query = head_slice(q_ref, q_start, index)
+        key = head_slice(kv_ref, k_start, index)
+        value = head_slice(kv_ref, v_start, index)
+        scores = masked_scores(query, key, causal)
+        row_top = jnp.max(scores, axis=-1, keepdims=True)
+        exponent = jnp.exp(scores - row_top)
+        row_total = jnp.sum(exponent, axis=-1, keepdims=True)
+        context = lowered(matmul(lowered(exponent / row_total), value))
+        context_ref[:, index * HEAD_DIM : (index + 1) * HEAD_DIM] = context
+        logs_ref[:, index : index + 1] = row_top + jnp.log(row_total)
+
+
+def heads_backward(q_ref, kv_ref, starts, logs_ref, grad_ref, gq_ref, gkv_ref, g_starts, causal):
+    q_start, k_start, v_start = starts
+    gq_start, gk_start, gv_start = g_starts
+    scale = HEAD_DIM ** (-0.5)
+    for index in range(grad_ref.shape[1] // HEAD_DIM):
+        low, high = index * HEAD_DIM, (index + 1) * HEAD_DIM
+        query = head_slice(q_ref, q_start, index)
+        key = head_slice(kv_ref, k_start, index)
+        value = head_slice(kv_ref, v_start, index)
+        grad = grad_ref[:, low:high]
+        softmax_out = jnp.exp(
+            masked_scores(query, key, causal) - logs_ref[:, index : index + 1]
+        )
+        gkv_ref[:, gv_start + low : gv_start + high] = lowered(
+            contract_rows(lowered(softmax_out), grad)
+        )
+        grad_softmax = times_transposed(grad, value)
+        inner = jnp.sum(grad_softmax * softmax_out, axis=-1, keepdims=True)
+        grad_scores = lowered(softmax_out * (grad_softmax - inner))
+        gq_ref[:, gq_start + low : gq_start + high] = lowered(matmul(grad_scores, key) * scale)
+        gkv_ref[:, gk_start + low : gk_start + high] = lowered(
+            contract_rows(grad_scores, query) * scale
+        )
+
+
+def norm_backward(grad_out, saved_parts, gain_row):
+    normed, scale_inv = saved_parts
+    grad_normed = grad_out * gain_row
+    grad_in = scale_inv * (
+        grad_normed
+        - jnp.mean(grad_normed, axis=-1, keepdims=True)
+        - normed * jnp.mean(grad_normed * normed, axis=-1, keepdims=True)
+    )
+    return (
+        grad_in,
+        jnp.sum(grad_out * normed, axis=0, keepdims=True),
+        jnp.sum(grad_out, axis=0, keepdims=True),
+    )
+
+
+def gain_of(norms_ref, row):
+    return norms_ref[row : row + 1, :], norms_ref[row + 7 : row + 8, :]
+
+
+def stream_of(looked_ref, start, place_ref):
+    rows, width = place_ref.shape
+    looked = looked_ref[start : start + rows, :].astype(jnp.float32)
+    return looked * math.sqrt(width) + place_ref[...]
+
+
+def first_kernel(
+    shares,
+    looked_ref, place_enc_ref, place_dec_ref, w_ref,
+    qkv_enc_ref, context_enc_ref, logs_enc_ref, stream_enc_ref,
+    qkv_dec_ref, context_dec_ref, logs_dec_ref, stream_dec_ref,
+    out_rows_ref, norms_ref,
+    blocks_ref, block_sems, local_sem, *total_refs,
+):
+    group, share, _, _, _ = places()
+    peers = share_peers(group, share, shares)
+    meet(peers)
+    _, rows, wide = blocks_ref.shape
+    own = qkv_enc_ref.shape[1] // 3
+    padded = w_ref.shape[1] - wide
+    enc_start, dec_start, out_start = 0, padded // 2, padded
+    window = pl.ds(out_start, wide)
+    copies = []
+    for step, (_, peer) in enumerate(peers):
+        source = w_ref.at[pl.ds(pl.multiple_of(peer * rows, 64), rows), window]
+        copies.append(
+            send(source, blocks_ref.at[share], block_sems.at[0, step], block_sems.at[1, step], (group, peer))
+        )
+    keep = pltpu.make_async_copy(
+        w_ref.at[pl.ds(pl.multiple_of(share * rows, 64), rows), window], blocks_ref.at[share], local_sem
+    )
+    keep.start()
+
+    turned = jnp.transpose(w_ref[:, w_ref.shape[1] - 128 :].astype(jnp.float32))
+    norms_ref[...] = turned[64:80]
+
+    enc_total, dec_total = Total(total_refs[:4]), Total(total_refs[4:])
+    enc_len, dec_len = place_enc_ref.shape[0], place_dec_ref.shape[0]
+    stream = stream_of(looked_ref, 0, place_enc_ref)
+    normed, _ = norm_forward(stream, *gain_of(norms_ref, 0))
+    qkv_enc_ref[...] = lowered(matmul(lowered(normed), w_ref[:, enc_start : enc_start + 3 * own]))
+    stream_enc_ref[...] = stream
+    starts = (0, own, 2 * own)
+    logs_enc_ref[...] = jnp.zeros_like(logs_enc_ref)
+    heads_forward(qkv_enc_ref, qkv_enc_ref, starts, context_enc_ref, logs_enc_ref, False)
+    keep.wait()
+    for copy in copies:
+        copy.wait()
+    for matrix in range(3):
+        for piece in range(shares):
+            out_rows_ref[matrix, :, piece * own : (piece + 1) * own] = blocks_ref[
+                piece, :, matrix * own : (matrix + 1) * own
+            ]
+    enc_total.begin(matmul(context_enc_ref[...], out_rows_ref[0]))
+    stream = stream_of(looked_ref, enc_len, place_dec_ref)
+    stream_dec_ref[...] = stream
+    normed, _ = norm_forward(stream, *gain_of(norms_ref, 3))
+    enc_total.middle()
+    qkv_dec_ref[...] = lowered(matmul(lowered(normed), w_ref[:, dec_start : dec_start + 3 * own]))
+    logs_dec_ref[...] = jnp.zeros_like(logs_dec_ref)
+    heads_forward(qkv_dec_ref, qkv_dec_ref, starts, context_dec_ref, logs_dec_ref, True)
+    enc_total.last()
+    dec_total.begin(matmul(context_dec_ref[...], out_rows_ref[1]))
+    dec_total.middle()
+    stream_enc_ref[...] += enc_total.finish()
+    dec_total.last()
+    stream_dec_ref[...] += dec_total.finish()
+
+
+def enc_feed_kernel(stream_in_ref, norms_ref, w_ref, pre_ref, stream_ref, memory_ref, *total_refs):
+    group, share, _, core_peer, side_peer = places()
+    meet([core_peer, side_peer])
+    width = stream_in_ref.shape[1]
+    total = Total(total_refs)
+    normed, _ = norm_forward(stream_in_ref[...], *gain_of(norms_ref, 1))
+    hidden = w_ref.shape[1] - width
+    pre_ref[...] = matmul(lowered(normed), w_ref[:, :hidden])
+    activated = lowered(jax.nn.silu(pre_ref[...]))
+    total.begin(matmul(activated, w_ref[:, hidden:]))
+    stream_ref[...] = stream_in_ref[...] + total.rest()
+    memory, _ = norm_forward(stream_ref[...], *gain_of(norms_ref, 2))
+    memory_ref[...] = lowered(memory)
+
+
+def dec_kernel(
+    groups,
+    stream_in_ref, memory_ref, norms_ref, w_ref, out_rows_ref, positions_ref,
+    q_ref, kv_ref, context_ref, logs_ref, stream_mid_ref, pre_ref, stream_ref, selected_ref,
+    own_ref, select_sems, *total_refs,
+):
+    group, share, _, core_peer, side_peer = places()
+    peers = group_peers(group, share, groups)
+    meet([core_peer, side_peer] + peers)
+    width = stream_in_ref.shape[1]
+    own = q_ref.shape[1]
+    hidden = pre_ref.shape[1]
+    in_start = hidden + width
+    cross_total, feed_total = Total(total_refs[:4]), Total(total_refs[4:])
+    kv_ref[...] = lowered(matmul(memory_ref[...], w_ref[:, in_start + own : in_start + 3 * own]))
+    normed, _ = norm_forward(stream_in_ref[...], *gain_of(norms_ref, 4))
+    q_ref[...] = lowered(matmul(lowered(normed), w_ref[:, in_start : in_start + own]))
+    logs_ref[...] = jnp.zeros_like(logs_ref)
+    heads_forward(q_ref, kv_ref, (0, 0, own), context_ref, logs_ref, False)
+    cross_total.begin(matmul(context_ref[...], out_rows_ref[2]))
+    stream_mid_ref[...] = stream_in_ref[...] + cross_total.rest()
+    normed, _ = norm_forward(stream_mid_ref[...], *gain_of(norms_ref, 5))
+    pre_ref[...] = matmul(lowered(normed), w_ref[:, :hidden])
+    activated = lowered(jax.nn.silu(pre_ref[...]))
+    feed_total.begin(matmul(activated, w_ref[:, hidden : hidden + width]))
+    stream_ref[...] = stream_mid_ref[...] + feed_total.rest()
+    final, _ = norm_forward(stream_ref[...], *gain_of(norms_ref, 6))
+    places_down = lax.broadcasted_iota(jnp.int32, (own_ref.shape[0], stream_ref.shape[0]), 1)
+    chosen = lowered(jnp.where(places_down == positions_ref[...], 1.0, 0.0))
+    own_ref[...] = lowered(matmul(chosen, lowered(final)))
+    selected_ref[group] = own_ref[...]
+    copies = [
+        send(own_ref, selected_ref.at[group], select_sems.at[0, step], select_sems.at[1, step], peer)
+        for step, peer in enumerate(peers)
+    ]
+    for copy in copies:
+        copy.wait()
+
+
+def combine_stats(stats):
+    row_max = stats[0][0:1]
+    for member in stats[1:]:
+        row_max = jnp.maximum(row_max, member[0:1])
+    exp_total = smooth = target = 0.0
+    for member in stats:
+        exp_total = exp_total + member[1:2] * jnp.exp(member[0:1] - row_max)
+        smooth = smooth + member[2:3]
+        target = target + member[3:4]
+    return row_max, exp_total, smooth, target
+
+
+def head_kernel(
+    groups, shares, shard_rows,
+    selected_ref, table_ref, targets_ref, weights_ref, counted_ref,
+    loss_ref, grad_out_ref, head_ref,
+    logits_ref, dz_ref, stats_ref, turned_ref, share_stats_ref, group_stats_ref, stat_sems,
+    part_ref, core_ref, side_ref, group_ref, sum_ref, sems,
+):
+    group, share, core, core_peer, side_peer = places()
+    side = share // 2
+    near, far = share_peers(group, share, shares), group_peers(group, share, groups)
+    meet(near + far)
+    rows, width = selected_ref.shape
+    chunk = table_ref.shape[1]
+    vocab_total = shard_rows * shares
+    first = group * chunk
+    limit = jnp.minimum(shard_rows - first, vocab_total - 1 - share * shard_rows - first)
+    block = 512
+    step_rows = 32
+
+    for part in range(chunk // block):
+        logits_ref[:, part * block : (part + 1) * block] = matmul(
+            selected_ref[...], table_ref[:, part * block : (part + 1) * block]
+        )
+    stats_ref[...] = jnp.zeros_like(stats_ref)
+
+    def gather_stats(step, carry):
+        at = pl.ds(pl.multiple_of(step * step_rows, step_rows), step_rows)
+        logits = logits_ref[at, :]
+        column = lax.broadcasted_iota(jnp.int32, logits.shape, 1)
+        real = column < limit
+        masked = jnp.where(real, logits, -1e30)
+        top = jnp.max(masked, axis=1, keepdims=True)
+        stats_ref[at, 0:1] = top
+        stats_ref[at, 1:2] = jnp.sum(jnp.exp(masked - top), axis=1, keepdims=True)
+        stats_ref[at, 2:3] = jnp.sum(jnp.where(real, logits, 0.0), axis=1, keepdims=True)
+        hit = column == targets_ref[at, :]
+        stats_ref[at, 3:4] = jnp.sum(jnp.where(hit, logits, 0.0), axis=1, keepdims=True)
+        return carry
+
+    lax.fori_loop(0, rows // step_rows, gather_stats, 0)
+    share_stats_ref[share] = jnp.transpose(stats_ref[...])[0:8]
+    copies = [
+        send(share_stats_ref.at[share], share_stats_ref.at[share], stat_sems.at[0, step], stat_sems.at[1, step], peer)
+        for step, peer in enumerate(near)
+    ]
+    for copy in copies:
+        copy.wait()
+    merged = combine_stats([share_stats_ref[index] for index in range(shares)])
+    group_stats_ref[group] = jnp.concatenate(merged + (jnp.zeros((4, rows), jnp.float32),), axis=0)
+    copies = [
+        send(group_stats_ref.at[group], group_stats_ref.at[group], stat_sems.at[2, step], stat_sems.at[3, step], peer)
+        for step, peer in enumerate(far)
+    ]
+    for copy in copies:
+        copy.wait()
+    row_max, exp_total, smooth, target = combine_stats(
+        [group_stats_ref[index] for index in range(groups)]
+    )
+    log_total = row_max + jnp.log(exp_total)
+    per_row = log_total - (1.0 - SMOOTH) * target - SMOOTH * smooth / (vocab_total - 1)
+    loss = jnp.sum(counted_ref[...] * per_row, axis=1, keepdims=True)
+    loss_ref[...] = jnp.broadcast_to(loss, loss_ref.shape)
+    turned_ref[...] = jnp.zeros_like(turned_ref)
+    turned_ref[0:1, :] = log_total
+    stats_ref[...] = jnp.transpose(turned_ref[...])
+
+    def make_dz(step, carry):
+        at = pl.ds(pl.multiple_of(step * step_rows, step_rows), step_rows)
+        logits = logits_ref[at, :]
+        column = lax.broadcasted_iota(jnp.int32, logits.shape, 1)
+        softmax_rows = jnp.exp(logits - stats_ref[at, 0:1])
+        hit = jnp.where(column == targets_ref[at, :], 1.0 - SMOOTH, 0.0)
+        grad = weights_ref[at, :] * (softmax_rows - hit - SMOOTH / (vocab_total - 1))
+        dz_ref[at, :] = lowered(jnp.where(column < limit, grad, 0.0))
+        return carry
+
+    lax.fori_loop(0, rows // step_rows, make_dz, 0)
+    loss_rows = rows // groups
+    half, quarter = loss_rows // 2, loss_rows // 4
+    part_ref[...] = lowered(times_transposed(dz_ref[...], table_ref[...])).reshape(part_ref.shape)
+    mine = pl.ds(pl.multiple_of(core * half, 16), half)
+    other = pl.ds(pl.multiple_of((1 - core) * half, 16), half)
+    copy = send(part_ref.at[:, other, :], core_ref, sems.at[0, 0], sems.at[1, 0], core_peer)
+
+    def head_part(index):
+        at = slice(index * block, (index + 1) * block)
+        head_ref[:, at] = lowered(contract_rows(selected_ref[...], dz_ref[:, at]))
+
+    parts = chunk // block
+    head_part(0)
+    copy.wait()
+    part_ref[:, mine, :] = lowered(
+        part_ref[:, mine, :].astype(jnp.float32) + core_ref[...].astype(jnp.float32)
+    )
+    base = core * half
+    my_quarter = pl.ds(pl.multiple_of(base + side * quarter, 16), quarter)
+    other_quarter = pl.ds(pl.multiple_of(base + (1 - side) * quarter, 16), quarter)
+    copy = send(part_ref.at[:, other_quarter, :], side_ref, sems.at[0, 1], sems.at[1, 1], side_peer)
+    for index in range(1, parts // 2):
+        head_part(index)
+    copy.wait()
+    side_ref[...] = lowered(
+        part_ref[:, my_quarter, :].astype(jnp.float32) + side_ref[...].astype(jnp.float32)
+    )
+    group_ref[group] = side_ref[group]
+    copies = [
+        send(side_ref.at[peer[0]], group_ref.at[group], sems.at[0, 2 + step], sems.at[1, 2 + step], peer)
+        for step, peer in enumerate(far)
+    ]
+    for index in range(parts // 2, parts):
+        head_part(index)
+    for copy in copies:
+        copy.wait()
+    summed = group_ref[0].astype(jnp.float32)
+    for index in range(1, groups):
+        summed = summed + group_ref[index].astype(jnp.float32)
+    sum_ref[...] = lowered(summed)
+    grad_out_ref[my_quarter, :] = sum_ref[...]
+    base_sem = 1 + groups
+    copies = [
+        send(sum_ref, grad_out_ref.at[my_quarter, :], sems.at[0, base_sem + step], sems.at[1, base_sem + step], peer)
+        for step, peer in enumerate(near)
+    ]
+    for copy in copies:
+        copy.wait()
+
+
+def feed_grads(grad_ref, stream_ref, pre_ref, norms_ref, row, w_ref, grads_ref, total):
+    width = stream_ref.shape[1]
+    hidden = pre_ref.shape[1]
+    normed, _ = norm_forward(stream_ref[...], *gain_of(norms_ref, row))
+    grad_low = lowered(grad_ref[...])
+    pre = pre_ref[...]
+    sigmoid_pre = jax.nn.sigmoid(pre)
+    grad_pre = lowered(
+        times_transposed(grad_low, w_ref[:, hidden : hidden + width])
+        * sigmoid_pre
+        * (1.0 + pre * (1.0 - sigmoid_pre))
+    )
+    total.begin(times_transposed(grad_pre, w_ref[:, :hidden]))
+    activated = lowered(pre * sigmoid_pre)
+    grads_ref[:, hidden : hidden + width] = lowered(contract_rows(activated, grad_low))
+    total.middle()
+    grads_ref[:, :hidden] = lowered(contract_rows(lowered(normed), grad_pre))
+
+
+def norm_step(grad_ref, stream_ref, norms_ref, row, summed, rows_ref, slot):
+    gain, shift = gain_of(norms_ref, row)
+    _, kept = norm_forward(stream_ref[...], gain, shift)
+    grad_in, grad_gain, grad_shift = norm_backward(summed, kept, gain)
+    rows_ref[slot : slot + 1, :] = grad_gain
+    rows_ref[slot + 1 : slot + 2, :] = grad_shift
+    if grad_ref is None:
+        return grad_in
+    return grad_ref[...] + grad_in
+
+
+def dec_back_kernel(
+    groups,
+    grad_selected_ref, positions_ref, stream_in_ref, stream_mid_ref, stream_ref, pre_ref, memory_ref,
+    norms_ref, w_ref, out_rows_ref, q_ref, kv_ref, context_ref, logs_ref, head_in_ref,
+    grads_ref, grad_out_rows_ref, grad_ref, grad_memory_ref, rows_ref, head_out_ref,
+    head_sems, grad_context_ref, gq_ref, gkv_ref, *total_refs,
+):
+    group, share, _, core_peer, side_peer = places()
+    meet([core_peer, side_peer] + group_peers(group, share, groups))
+    exchange = Exchange(head_in_ref, head_out_ref, head_sems, groups, 0)
+    width = stream_ref.shape[1]
+    own = q_ref.shape[1]
+    hidden = pre_ref.shape[1]
+    in_start = hidden + width
+    feed_total, cross_total, memory_total = [Total(total_refs[4 * k : 4 * k + 4]) for k in range(3)]
+    rows_ref[...] = jnp.zeros_like(rows_ref)
+    down = lax.broadcasted_iota(jnp.int32, (stream_ref.shape[0], grad_selected_ref.shape[0]), 0)
+    chosen = lowered(jnp.where(down == positions_ref[...], 1.0, 0.0))
+    grad_final = matmul(chosen, grad_selected_ref[...])
+    grad_ref[...] = norm_step(None, stream_ref, norms_ref, 6, grad_final, rows_ref, 0)
+    feed_grads(grad_ref, stream_mid_ref, pre_ref, norms_ref, 5, w_ref, grads_ref, feed_total)
+    feed_total.last()
+    grad_ref[...] = norm_step(
+        grad_ref, stream_mid_ref, norms_ref, 5, feed_total.finish(), rows_ref, 2
+    )
+    grad_low = lowered(grad_ref[...])
+    grad_context_ref[...] = lowered(times_transposed(grad_low, out_rows_ref[2]))
+    heads_backward(
+        q_ref, kv_ref, (0, 0, own), logs_ref, grad_context_ref, gq_ref, gkv_ref, (0, 0, own), False
+    )
+    memory_total.begin(
+        times_transposed(gkv_ref[...], w_ref[:, in_start + own : in_start + 3 * own])
+    )
+    cross_total.begin(times_transposed(gq_ref[...], w_ref[:, in_start : in_start + own]))
+    grad_out_rows_ref[...] = lowered(contract_rows(context_ref[...], grad_low))
+    memory_total.middle()
+    cross_total.middle()
+    normed, _ = norm_forward(stream_in_ref[...], *gain_of(norms_ref, 4))
+    grads_ref[:, in_start:] = jnp.zeros((width, grads_ref.shape[1] - in_start), jnp.bfloat16)
+    grads_ref[:, in_start : in_start + own] = lowered(contract_rows(lowered(normed), gq_ref[...]))
+    grads_ref[:, in_start + own : in_start + 3 * own] = lowered(
+        contract_rows(memory_ref[...], gkv_ref[...])
+    )
+    memory_total.last()
+    cross_total.last()
+    grad_memory_ref[...] = memory_total.finish()
+    grad_ref[...] = norm_step(
+        grad_ref, stream_in_ref, norms_ref, 4, cross_total.finish(), rows_ref, 4
+    )
+    exchange.finish()
+
+
+def mid_back_kernel(
+    groups,
+    grad_memory_ref, stream_enc_ref, stream_mid_ref, pre_ref, norms_ref, w_ref,
+    grad_dec_in_ref, looked_ref, place_dec_ref, w_first_ref, out_rows_ref, qkv_ref, context_ref, logs_ref, head_in_ref,
+    grads_ref, grad_out_rows_ref, grad_enc_ref, tokens_ref, rows_ref, head_out_ref,
+    head_sems, stream_dec_ref, grad_context_ref, gqkv_ref, *total_refs,
+):
+    group, share, _, core_peer, side_peer = places()
+    meet([core_peer, side_peer] + group_peers(group, share, groups))
+    exchange = Exchange(head_in_ref, head_out_ref, head_sems, groups, 1)
+    width = stream_enc_ref.shape[1]
+    own = context_ref.shape[1]
+    hidden = pre_ref.shape[1]
+    in_start = hidden + width
+    w_start = w_first_ref.shape[1] // 3
+    dec_start = looked_ref.shape[0] - place_dec_ref.shape[0]
+    feed_total, self_total = Total(total_refs[:4]), Total(total_refs[4:])
+    rows_ref[...] = jnp.zeros_like(rows_ref)
+    grad_enc_ref[...] = norm_step(
+        None, stream_enc_ref, norms_ref, 2, grad_memory_ref[...], rows_ref, 0
+    )
+    feed_grads(grad_enc_ref, stream_mid_ref, pre_ref, norms_ref, 1, w_ref, grads_ref, feed_total)
+    grad_low = lowered(grad_dec_in_ref[...])
+    grad_context_ref[...] = lowered(times_transposed(grad_low, out_rows_ref[1]))
+    starts = (0, own, 2 * own)
+    heads_backward(
+        qkv_ref, qkv_ref, starts, logs_ref, grad_context_ref, gqkv_ref, gqkv_ref, starts, True
+    )
+    feed_total.last()
+    self_total.begin(times_transposed(gqkv_ref[...], w_first_ref[:, w_start : w_start + 3 * own]))
+    grad_out_rows_ref[...] = lowered(contract_rows(context_ref[...], grad_low))
+    self_total.middle()
+    stream_dec_ref[...] = stream_of(looked_ref, dec_start, place_dec_ref)
+    normed, _ = norm_forward(stream_dec_ref[...], *gain_of(norms_ref, 3))
+    grads_ref[:, in_start:] = jnp.zeros((width, grads_ref.shape[1] - in_start), jnp.bfloat16)
+    grads_ref[:, in_start : in_start + 3 * own] = lowered(
+        contract_rows(lowered(normed), gqkv_ref[...])
+    )
+    grad_enc_ref[...] = norm_step(
+        grad_enc_ref, stream_mid_ref, norms_ref, 1, feed_total.finish(), rows_ref, 2
+    )
+    self_total.last()
+    grad_dec = norm_step(
+        grad_dec_in_ref, stream_dec_ref, norms_ref, 3, self_total.finish(), rows_ref, 4
+    )
+    tokens_ref[...] = lowered(grad_dec * math.sqrt(width))
+    exchange.finish()
+
+
+def last_back_kernel(
+    groups, shares,
+    grad_in_ref, looked_ref, place_enc_ref, norms_ref, w_ref, out_rows_ref, qkv_ref, context_ref, logs_ref,
+    g_self_ref, g_cross_ref, rows_dec_ref, rows_mid_ref, head_in_ref,
+    grads_ref, tokens_ref, head_out_ref,
+    head_sems, stream_ref, grad_context_ref, gqkv_ref, g_rows_ref, norm_rows_ref, turned_ref, blocks_ref, rows_ref, block_sems, local_sem, *total_refs,
+):
+    group, share, _, core_peer, side_peer = places()
+    peers = share_peers(group, share, shares)
+    meet(peers + group_peers(group, share, groups))
+    exchange = Exchange(head_in_ref, head_out_ref, head_sems, groups, 2)
+    width = stream_ref.shape[1]
+    own = context_ref.shape[1]
+    wide = blocks_ref.shape[2]
+    total = Total(total_refs)
+    grad_low = lowered(grad_in_ref[...])
+    grad_context_ref[...] = lowered(times_transposed(grad_low, out_rows_ref[0]))
+    starts = (0, own, 2 * own)
+    heads_backward(
+        qkv_ref, qkv_ref, starts, logs_ref, grad_context_ref, gqkv_ref, gqkv_ref, starts, False
+    )
+    total.begin(times_transposed(gqkv_ref[...], w_ref[:, : 3 * own]))
+    g_rows_ref[...] = lowered(contract_rows(context_ref[...], grad_low))
+    total.middle()
+    stream_ref[...] = stream_of(looked_ref, 0, place_enc_ref)
+    normed, _ = norm_forward(stream_ref[...], *gain_of(norms_ref, 0))
+    in_wide = grads_ref.shape[1] - wide
+    grads_ref[:, :in_wide] = jnp.zeros((width, in_wide), jnp.bfloat16)
+    grads_ref[:, : 3 * own] = lowered(contract_rows(lowered(normed), gqkv_ref[...]))
+    blocks_ref[...] = jnp.zeros_like(blocks_ref)
+    for piece in range(shares):
+        at = slice(piece * own, (piece + 1) * own)
+        for matrix, source in enumerate((g_rows_ref, g_self_ref, g_cross_ref)):
+            blocks_ref[piece, :, matrix * own : (matrix + 1) * own] = source[:, at]
+    total.last()
+    rows_ref[...] = jnp.zeros_like(rows_ref)
+    grad_enc = norm_step(grad_in_ref, stream_ref, norms_ref, 0, total.finish(), rows_ref, 0)
+    tokens_ref[...] = lowered(grad_enc * math.sqrt(width))
+    norm_rows_ref[...] = jnp.zeros_like(norm_rows_ref)
+    order = (
+        (0, rows_ref, 0),
+        (1, rows_mid_ref, 2),
+        (2, rows_mid_ref, 0),
+        (3, rows_mid_ref, 4),
+        (4, rows_dec_ref, 4),
+        (5, rows_dec_ref, 2),
+        (6, rows_dec_ref, 0),
+    )
+    for row, source, slot in order:
+        norm_rows_ref[64 + row : 65 + row, :] = source[slot : slot + 1, :]
+        norm_rows_ref[71 + row : 72 + row, :] = source[slot + 1 : slot + 2, :]
+    turned_ref[...] = jnp.transpose(norm_rows_ref[...])
+    own_rows = turned_ref[pl.ds(pl.multiple_of(share * own, 64), own), :]
+    for piece in range(shares):
+        tail = blocks_ref[piece, :, wide - 128 :].astype(jnp.float32)
+        blocks_ref[piece, :, wide - 128 :] = lowered(tail + own_rows)
+    target = grads_ref.at[pl.ds(pl.multiple_of(share * own, 64), own), pl.ds(in_wide, wide)]
+    copies = [
+        send(blocks_ref.at[peer[1]], target, block_sems.at[0, step], block_sems.at[1, step], peer)
+        for step, peer in enumerate(peers)
+    ]
+    keep = pltpu.make_async_copy(blocks_ref.at[share], target, local_sem)
+    keep.start()
+    keep.wait()
+    for copy in copies:
+        copy.wait()
+    exchange.finish()
+
+
+def numbers_kernel(groups, own_ref, out_ref, sems, local_sem):
+    group, share, _, _, _ = places()
+    peers = group_peers(group, share, groups)
+    meet(peers)
+    copies = [
+        send(own_ref, out_ref.at[group], sems.at[0, step], sems.at[1, step], peer)
+        for step, peer in enumerate(peers)
+    ]
+    keep = pltpu.make_async_copy(own_ref, out_ref.at[group], local_sem)
+    keep.start()
+    keep.wait()
+    for copy in copies:
+        copy.wait()
+
+
+def look_kernel(groups, picked_ref, looked_ref, send_ref, core_ref, side_ref, group_ref, sems):
+    group, share, core, core_peer, side_peer = places()
+    side = share // 2
+    far = group_peers(group, share, groups)
+    meet([core_peer, side_peer] + far)
+    _, tokens, width = picked_ref.shape
+    half, quarter = tokens // 2, tokens // 4
+    mine = pl.ds(pl.multiple_of(core * half, 16), half)
+    other = pl.ds(pl.multiple_of((1 - core) * half, 16), half)
+    send(picked_ref.at[:, other, :], core_ref, sems.at[0, 0], sems.at[1, 0], core_peer).wait()
+    core_ref[...] = core_ref[...] + picked_ref[:, mine, :]
+    own_quarter = pl.ds(pl.multiple_of(side * quarter, 16), quarter)
+    other_quarter = pl.ds(pl.multiple_of((1 - side) * quarter, 16), quarter)
+    send(core_ref.at[:, other_quarter, :], side_ref, sems.at[0, 1], sems.at[1, 1], side_peer).wait()
+    side_ref[...] = side_ref[...] + core_ref[:, own_quarter, :]
+    group_ref[group] = side_ref[group]
+    copies = [
+        send(side_ref.at[peer[0]], group_ref.at[group], sems.at[0, 2 + step], sems.at[1, 2 + step], peer)
+        for step, peer in enumerate(far)
+    ]
+    for copy in copies:
+        copy.wait()
+    for index in range(groups):
+        send_ref[:, index * width : (index + 1) * width] = group_ref[index]
+    at = pl.ds(pl.multiple_of(core * half + side * quarter, 16), quarter)
+    looked_ref[at, :] = send_ref[...]
+    end = 1 + groups
+    send(send_ref, looked_ref.at[at, :], sems.at[0, end], sems.at[1, end], side_peer).wait()
+    end = end + 1
+    both = looked_ref.at[mine, :]
+    send(both, both, sems.at[0, end], sems.at[1, end], core_peer).wait()
+
+
+def squares_kernel(
+    groups, shares, norm_start, norm_count,
+    embedding_ref, one_ref, two_ref, three_ref, out_ref, share_ref, group_ref, sems,
+):
+    group, share, _, _, _ = places()
+    near, far = share_peers(group, share, shares), group_peers(group, share, groups)
+    meet(near + far)
+    total = 0.0
+    for ref in (one_ref, two_ref, three_ref):
+        value = ref[...].astype(jnp.float32)
+        value = value * value
+        if ref is three_ref:
+            column = lax.broadcasted_iota(jnp.int32, value.shape, 1)
+            norm_part = (column >= norm_start) & (column < norm_start + norm_count)
+            value = jnp.where(norm_part, value / shares, value)
+        total = total + jnp.sum(value)
+    lane = lax.broadcasted_iota(jnp.int32, (8, 128), 1)
+    down = lax.broadcasted_iota(jnp.int32, (8, 128), 0)
+    share_ref[share] = jnp.where((lane == 0) & (down == 0), total, 0.0) + jnp.where(
+        down == 1, embedding_ref[...], 0.0
+    )
+    copies = [
+        send(share_ref.at[share], share_ref.at[share], sems.at[0, step], sems.at[1, step], peer)
+        for step, peer in enumerate(near)
+    ]
+    for copy in copies:
+        copy.wait()
+    summed = share_ref[0]
+    for index in range(1, shares):
+        summed = summed + share_ref[index]
+    group_ref[group] = summed
+    copies = [
+        send(group_ref.at[group], group_ref.at[group], sems.at[2, step], sems.at[3, step], peer)
+        for step, peer in enumerate(far)
+    ]
+    for copy in copies:
+        copy.wait()
+    summed = group_ref[0]
+    for index in range(1, groups):
+        summed = summed + group_ref[index]
+    out_ref[...] = jnp.broadcast_to(jnp.sum(summed), out_ref.shape)
+
+
+def share_of_columns(array, groups, shares, index):
+    lead, columns = array.shape[:-1], array.shape[-1]
+    cut = array.reshape(lead + (groups, shares, columns // groups // shares))
+    own = lax.dynamic_index_in_dim(cut, index, axis=len(lead) + 1, keepdims=False)
+    return own.reshape(lead + (columns // shares,))
+
+
+def whole_of_shares(shares_first, groups):
+    shares, rows, columns = shares_first.shape
+    cut = shares_first.reshape(shares, rows, groups, columns // groups)
+    return cut.transpose(1, 2, 0, 3).reshape(rows, shares * columns)
+
+
+def local(
+    enc_ids,
+    labels,
+    target_lengths,
+    loss_positions,
+    embedding,
+    attn_in,
+    attn_out,
+    ffn_up,
+    ffn_down,
+    norms,
+    embedding_first,
+    attn_in_first,
+    attn_out_first,
+    ffn_up_first,
+    ffn_down_first,
+    norms_first,
+    embedding_second,
+    attn_in_second,
+    attn_out_second,
+    ffn_up_second,
+    ffn_down_second,
+    norms_second,
+):
+    groups, shares = lax.axis_size("dp"), lax.axis_size("vocab")
+    group, share = lax.axis_index("dp"), lax.axis_index("vocab")
+    enc_len, dec_len = enc_ids.shape[1], labels.shape[1]
+    loss_count = loss_positions.shape[1]
+    shard_rows, part_width = embedding.shape
+    model_width = part_width * groups
+    vocab_total = shard_rows * shares
+    row_start = share * shard_rows
+    root_width = math.sqrt(model_width)
+    tokens = enc_len + dec_len
+
+    bf16, f32 = jnp.bfloat16, jnp.float32
+    sems = pltpu.SemaphoreType.DMA
+    numbers = jnp.concatenate(
+        [enc_ids, labels, loss_positions, target_lengths[:, None]], axis=1
+    )
+    number_count = numbers.shape[1]
+    number_lanes = -(-number_count // 1024) * 128
+    numbers = jnp.pad(numbers, ((0, 0), (0, 8 * number_lanes - number_count)))
+    (numbers,) = call(
+        partial(numbers_kernel, groups),
+        "numbers",
+        1,
+        [numbers.reshape(8, number_lanes)],
+        [shape_of((groups, 8, number_lanes), jnp.int32)],
+        [sems((2, groups - 1)), sems],
+        0,
+    )
+    numbers = numbers.reshape(groups, 8 * number_lanes)
+    all_enc = numbers[:, :enc_len]
+    all_labels = numbers[:, enc_len:tokens]
+    all_positions = numbers[:, tokens : tokens + loss_count]
+    all_lengths = numbers[:, tokens + loss_count : number_count]
+    all_tokens = jnp.concatenate(
+        [all_enc, jnp.zeros((groups, 1), jnp.int32), all_labels[:, :-1]], axis=1
+    )
+    all_targets = jnp.take_along_axis(all_labels, all_positions, axis=1).reshape(-1)
+    all_counted = (all_positions < all_lengths).reshape(-1).astype(f32)
+    token_count = jnp.sum(all_counted)
+
+    local_ids = all_tokens.reshape(-1) - row_start
+    picked, hit_list, hit_count = pick_rows(local_ids, embedding)
+    (looked,) = call(
+        partial(look_kernel, groups),
+        "look",
+        2,
+        [picked.reshape(groups, tokens, part_width)],
+        [shape_of((tokens, model_width), bf16)],
+        [
+            pltpu.VMEM((tokens // 4, model_width), bf16),
+            pltpu.VMEM((groups, tokens // 2, part_width), bf16),
+            pltpu.VMEM((groups, tokens // 4, part_width), bf16),
+            pltpu.VMEM((groups, tokens // 4, part_width), bf16),
+            sems((2, groups + 3)),
+        ],
+        0,
+    )
+
+    mine_in = share_of_columns(lowered(attn_in), 3, shares, share)
+    mine_out = share_of_columns(lowered(attn_out), 1, shares, share)
+    mine_up = share_of_columns(lowered(ffn_up), groups, shares, share)
+    down_rows = ffn_down.shape[1] // shares
+    mine_down = lax.dynamic_slice_in_dim(ffn_down, share * down_rows, down_rows, axis=1)
+    mine_down = lowered(mine_down)
+    norm_rows = norms.shape[0]
+    own_in, own, own_up = mine_in.shape[2], mine_out.shape[2], mine_up.shape[2]
+    gap = -own_in % 128
+
+    def wider(array, columns):
+        return jnp.pad(array, ((0, 0), (0, columns)))
+
+    mine_first = jnp.concatenate(
+        [wider(mine_in[0], gap), wider(mine_in[1], gap), mine_out[0], mine_out[1], mine_out[2]]
+        + [wider(lowered(norms).T, gap - norm_rows)],
+        axis=1,
+    )
+    mine_enc = jnp.concatenate([mine_up[0], mine_down[0]], axis=1)
+    mine_dec = jnp.concatenate([mine_up[1], mine_down[1], wider(mine_in[2], gap)], axis=1)
+    mine_first, mine_enc, mine_dec, _ = lax.optimization_barrier(
+        (mine_first, mine_enc, mine_dec, all_lengths)
+    )
+    w_first = lax.all_gather(mine_first, "dp", axis=0, tiled=True)
+    w_enc = lax.all_gather(mine_enc, "dp", axis=0, tiled=True)
+    w_dec = lax.all_gather(mine_dec, "dp", axis=0, tiled=True)
+    in_wide = own_in + gap
+
+    chunk = -(-shard_rows // (groups * 512)) * 512
+    across = jnp.pad(lowered(embedding.T), ((0, 0), (0, groups * chunk - shard_rows)))
+    across = across.reshape(part_width, groups, chunk).transpose(1, 0, 2)
+    across, looked = lax.optimization_barrier((across, looked))
+    table = lax.all_to_all(across, "dp", 0, 0).reshape(model_width, chunk)
+
+    place_enc = positions_numpy(enc_len, model_width)
+    place_dec = positions_numpy(dec_len, model_width)
+    enc_macs, dec_macs = enc_len * model_width, dec_len * model_width
+    total_enc, total_dec = total_scratch(enc_len, model_width), total_scratch(dec_len, model_width)
+    (
+        qkv_enc, context_enc, logs_enc, stream_enc,
+        qkv_dec, context_dec, logs_dec, stream_dec,
+        out_rows, norm_values,
+    ) = call(
+        partial(first_kernel, shares),
+        "first",
+        3,
+        [looked, place_enc, place_dec, w_first],
+        [
+            shape_of((enc_len, 3 * own), bf16),
+            shape_of((enc_len, own), bf16),
+            shape_of((enc_len, 128), f32),
+            shape_of((enc_len, model_width), f32),
+            shape_of((dec_len, 3 * own), bf16),
+            shape_of((dec_len, own), bf16),
+            shape_of((dec_len, 128), f32),
+            shape_of((dec_len, model_width), f32),
+            shape_of((3, own, model_width), bf16),
+            shape_of((16, model_width), f32),
+        ],
+        [
+            pltpu.VMEM((shares, own, in_wide), bf16),
+            sems((2, shares - 1)),
+            sems,
+        ]
+        + total_enc
+        + total_dec,
+        8 * (enc_macs + dec_macs) * own,
+    )
+    pre_enc, stream_two, memory = call(
+        enc_feed_kernel,
+        "enc_feed",
+        4,
+        [stream_enc, norm_values, w_enc],
+        [
+            shape_of((enc_len, own_up), f32),
+            shape_of((enc_len, model_width), f32),
+            shape_of((enc_len, model_width), bf16),
+        ],
+        total_enc,
+        4 * enc_macs * own_up,
+    )
+    (
+        q_cross, kv_cross, context_cross, logs_cross, stream_mid, pre_dec, stream_out, selected
+    ) = call(
+        partial(dec_kernel, groups),
+        "dec",
+        5,
+        [stream_dec, memory, norm_values, w_dec, out_rows, loss_positions.reshape(-1, 1)],
+        [
+            shape_of((dec_len, own), bf16),
+            shape_of((enc_len, 2 * own), bf16),
+            shape_of((dec_len, own), bf16),
+            shape_of((dec_len, 128), f32),
+            shape_of((dec_len, model_width), f32),
+            shape_of((dec_len, own_up), f32),
+            shape_of((dec_len, model_width), f32),
+            shape_of((groups, loss_count, model_width), bf16),
+        ],
+        [pltpu.VMEM((loss_count, model_width), bf16), sems((2, groups - 1))] + total_dec + total_dec,
+        4 * dec_macs * own_up + 8 * enc_macs * own,
+    )
+
+    rows_all = groups * loss_count
+    first_row = row_start + group * chunk
+    targets = all_targets - first_row
+    inside = (targets >= 0) & (targets < jnp.minimum(chunk, shard_rows - group * chunk))
+    targets = jnp.where(inside, targets, -1)[:, None]
+    loss, grad_selected, head_grad = call(
+        partial(head_kernel, groups, shares, shard_rows),
+        "head",
+        6,
+        [
+            selected.reshape(rows_all, model_width),
+            table,
+            targets,
+            (all_counted / token_count)[:, None],
+            all_counted[None, :],
+        ],
+        [
+            shape_of((1, 128), f32),
+            shape_of((loss_count, model_width), bf16),
+            shape_of((model_width, chunk), bf16),
+        ],
+        [
+            pltpu.VMEM((rows_all, chunk), f32),
+            pltpu.VMEM((rows_all, chunk), bf16),
+            pltpu.VMEM((rows_all, 128), f32),
+            pltpu.VMEM((128, rows_all), f32),
+            pltpu.VMEM((shares, 8, rows_all), f32),
+            pltpu.VMEM((groups, 8, rows_all), f32),
+            sems((4, max(groups, shares))),
+            pltpu.VMEM((groups, loss_count, model_width), bf16),
+            pltpu.VMEM((groups, loss_count // 2, model_width), bf16),
+            pltpu.VMEM((groups, loss_count // 4, model_width), bf16),
+            pltpu.VMEM((groups, loss_count // 4, model_width), bf16),
+            pltpu.VMEM((loss_count // 4, model_width), bf16),
+            sems((2, groups + shares)),
+        ],
+        6 * rows_all * chunk * model_width,
+    )
+    loss_sum = loss[0, 0]
+    head_grad = head_grad.reshape(groups, part_width, chunk)
+    pieces = chunk // 3
+
+    dec_grads, g_out_cross, grad_dec, grad_memory, rows_dec, head_zero = call(
+        partial(dec_back_kernel, groups),
+        "dec_back",
+        7,
+        [
+            grad_selected, loss_positions.reshape(1, -1), stream_dec, stream_mid, stream_out, pre_dec,
+            memory, norm_values, w_dec, out_rows, q_cross, kv_cross, context_cross, logs_cross,
+            head_grad,
+        ],
+        [
+            shape_of((model_width, own_up + model_width + in_wide), bf16),
+            shape_of((own, model_width), bf16),
+            shape_of((dec_len, model_width), f32),
+            shape_of((enc_len, model_width), f32),
+            shape_of((8, model_width), f32),
+            shape_of((groups, part_width, pieces), bf16),
+        ],
+        [
+            sems((2, groups)),
+            pltpu.VMEM((dec_len, own), bf16),
+            pltpu.VMEM((dec_len, own), bf16),
+            pltpu.VMEM((enc_len, 2 * own), bf16),
+        ]
+        + total_dec
+        + total_dec
+        + total_enc,
+        8 * dec_macs * own_up + 16 * enc_macs * own,
+        (14,),
+        (5,),
+    )
+    dec_own = lax.psum_scatter(dec_grads, "dp", scatter_dimension=0, tiled=True)
+    mid_grads, g_out_self, grad_enc, tokens_dec, rows_mid, head_one = call(
+        partial(mid_back_kernel, groups),
+        "mid_back",
+        8,
+        [
+            grad_memory, stream_two, stream_enc, pre_enc, norm_values, w_enc,
+            grad_dec, looked, place_dec, w_first, out_rows, qkv_dec, context_dec, logs_dec,
+            head_grad,
+        ],
+        [
+            shape_of((model_width, own_up + model_width + in_wide), bf16),
+            shape_of((own, model_width), bf16),
+            shape_of((enc_len, model_width), f32),
+            shape_of((dec_len, model_width), bf16),
+            shape_of((8, model_width), f32),
+            shape_of((groups, part_width, pieces), bf16),
+        ],
+        [
+            sems((2, groups)),
+            pltpu.VMEM((dec_len, model_width), f32),
+            pltpu.VMEM((dec_len, own), bf16),
+            pltpu.VMEM((dec_len, 3 * own), bf16),
+        ]
+        + total_enc
+        + total_dec,
+        8 * enc_macs * own_up + 16 * dec_macs * own,
+        (14,),
+        (5,),
+    )
+    mid_own = lax.psum_scatter(mid_grads, "dp", scatter_dimension=0, tiled=True)
+    last_grads, tokens_enc, head_two = call(
+        partial(last_back_kernel, groups, shares),
+        "last_back",
+        9,
+        [
+            grad_enc, looked, place_enc, norm_values, w_first, out_rows, qkv_enc, context_enc, logs_enc,
+            g_out_self, g_out_cross, rows_dec, rows_mid, head_grad,
+        ],
+        [
+            shape_of((model_width, 2 * in_wide), bf16),
+            shape_of((enc_len, model_width), bf16),
+            shape_of((groups, part_width, pieces), bf16),
+        ],
+        [
+            sems((2, groups)),
+            pltpu.VMEM((enc_len, model_width), f32),
+            pltpu.VMEM((enc_len, own), bf16),
+            pltpu.VMEM((enc_len, 3 * own), bf16),
+            pltpu.VMEM((own, model_width), bf16),
+            pltpu.VMEM((128, model_width), f32),
+            pltpu.VMEM((model_width, 128), f32),
+            pltpu.VMEM((shares, own, in_wide), bf16),
+            pltpu.VMEM((8, model_width), f32),
+            sems((2, shares - 1)),
+            sems,
+        ]
+        + total_enc,
+        16 * enc_macs * own,
+        (13,),
+        (2,),
+    )
+    last_own = lax.psum_scatter(last_grads, "dp", scatter_dimension=0, tiled=True)
+
+    grad_tokens = jnp.concatenate([tokens_enc, tokens_dec], axis=0)
+    grad_tokens = grad_tokens.reshape(tokens, groups, part_width).transpose(1, 0, 2)
+    grad_tokens = lax.all_to_all(grad_tokens, "dp", 0, 0).reshape(groups * tokens, part_width)
+    g_embedding, embedding_squares = spread_rows(
+        local_ids, hit_list, hit_count, grad_tokens, (head_zero, head_one, head_two)
+    )
+    g_embedding = g_embedding[:, :shard_rows].T
+    norm_start = in_wide + own_in
+    (squares,) = call(
+        partial(squares_kernel, groups, shares, norm_start, norm_rows),
+        "squares",
+        10,
+        [embedding_squares, dec_own, mid_own, last_own],
+        [shape_of((1, 128), f32)],
+        [
+            pltpu.VMEM((shares, 8, 128), f32),
+            pltpu.VMEM((groups, 8, 128), f32),
+            sems((4, max(groups, shares))),
+        ],
+        0,
+    )
+    grad_norm = jnp.sqrt(squares[0, 0])
+    factor = jnp.minimum(1.0, CLIP / (grad_norm + 1e-06))
+    dec_shares = lax.all_gather(dec_own, "vocab", axis=0, tiled=False)
+    mid_shares = lax.all_gather(mid_own, "vocab", axis=0, tiled=False)
+    last_shares = lax.all_gather(last_own, "vocab", axis=0, tiled=False)
+
+    def shares_cut(array, *sizes):
+        edges = np.cumsum((0,) + sizes)
+        return [array[:, :, low:high].astype(f32) for low, high in zip(edges[:-1], edges[1:])]
+
+    s_up_dec, s_down_dec, s_in_cross = shares_cut(dec_shares, own_up, model_width, own_in)
+    s_up_enc, s_down_enc, s_in_self = shares_cut(mid_shares, own_up, model_width, own_in)
+    s_in_enc, _, s_out_enc, s_out_self, s_out_cross = shares_cut(
+        last_shares, own_in, gap, own, own, own
+    )
+    gradients = (
+        g_embedding,
+        jnp.stack([whole_of_shares(member, 3) for member in (s_in_enc, s_in_self, s_in_cross)]),
+        jnp.stack([whole_of_shares(member, 1) for member in (s_out_enc, s_out_self, s_out_cross)]),
+        jnp.stack([whole_of_shares(member, groups) for member in (s_up_enc, s_up_dec)]),
+        jnp.stack([member.reshape(-1, model_width) for member in (s_down_enc, s_down_dec)]),
+        last_own[:, norm_start : norm_start + norm_rows].astype(f32).T,
+    )
+    params = (embedding, attn_in, attn_out, ffn_up, ffn_down, norms)
+    firsts = (
+        embedding_first,
+        attn_in_first,
+        attn_out_first,
+        ffn_up_first,
+        ffn_down_first,
+        norms_first,
+    )
+    seconds = (
+        embedding_second,
+        attn_in_second,
+        attn_out_second,
+        ffn_up_second,
+        ffn_down_second,
+        norms_second,
+    )
+    updated = [
+        adam_update(params[slot], firsts[slot], seconds[slot], gradients[slot], factor, RATES[slot])
+        for slot in range(6)
+    ]
+    return (loss_sum, token_count, grad_norm) + tuple(
+        updated[slot][kind] for kind in range(3) for slot in range(6)
+    )
+
+
+def splits_evenly(mesh):
+    return HEADS % mesh.shape["vocab"] == 0
+
+
 def solution(mesh):
     placed = (
         P("dp", None),
@@ -433,7 +1719,7 @@
         P(None, "dp"),
     )
     return jax.shard_map(
-        local,
+        local if splits_evenly(mesh) else local_copied,
         mesh=mesh,
         in_specs=placed,
         out_specs=(

time: 2950 us -> 833 us (0.28)
  waiting for transfers between devices: 2020 us -> 169 us
  Pallas kernels: 0 us -> 430 us
  other arithmetic: 310 us -> 60.2 us
  matrix products: 231 us -> 0 us
  local copies, waits for them, and re-layouts: 242 us -> 99.5 us
  blocking collectives: 103 us -> 10 us
  starting transfers between devices: 1.18 us -> 35 us
    all_gather x5, waiting for transfers between devices: 1040 us -> 64.6 us  [the longest x1 64.6 us: local(): w_dec = lax.all_gather(mine_dec, 'dp', axis=0, tiled=True)]
    unnamed x15 -> x8, waiting for transfers between devices: 592 us -> 2.64 us
    pallas_call x0 -> x12, Pallas kernels: none -> 430 us  [the longest x10 373 us: call(): pl.pallas_call(kernel, out_shape=tuple(out_shape), in_specs=in_vmem(len(i...]
    reduce_scatter x4 -> x3, waiting for transfers between devices: 329 us -> 63.6 us  [the longest x1 57.4 us: local(): mid_own = lax.psum_scatter(mid_grads, 'dp', scatter_dimension=0, tiled=True)]
    dot_general x54 -> x0, matrix products: 231 us -> none  [the longest x12 67.7 us: contract_rows(): lax.dot_general(left_side, right_side, (((0,), (0,)), ((), ())), preferre...]
    scatter-add x2 -> x0, other arithmetic: 125 us -> none  [the longest x1 123 us: local(): lookup_term = jnp.zeros((shard_rows, model_width), jnp.float32).at[safe_r...]
    unnamed x442 -> x73, local copies, waits for them, and re-layouts: 146 us -> 25.4 us
    psum x3 -> x0, blocking collectives: 66 us -> none  [the longest x1 39.5 us: local(): lax.psum(dense_squares / lax.axis_size('vocab') + jnp.sum(g_embedding * g...]
  transfers between devices with their start and end apart: 13 -> 10, of which waited for: 10 -> 4; matrix products, arithmetic and copies ran while one was open for 16% -> 11% of each run, Pallas kernels for 0% -> 41%
where the time goes in v1:
time: 833 us; the launch traced here: 823 us
  Pallas kernels  430 us (52%)
  waiting for transfers between devices  169 us (20%)
  local copies, waits for them, and re-layouts  99.5 us (12%)
  other arithmetic  60.2 us (7%)
  starting transfers between devices  35 us (4%)
  between operations  19.3 us (2%)
  blocking collectives  10 us (1%)
    pallas_call x10, Pallas kernels, call(): pl.pallas_call(kernel, out_shape=tuple(out_shape), in_specs=in_vmem(len(i...  373 us
    all_gather x1, waiting for transfers between devices, local(): w_dec = lax.all_gather(mine_dec, 'dp', axis=0, tiled=True)  64.6 us
    reduce_scatter x1, waiting for transfers between devices, local(): mid_own = lax.psum_scatter(mid_grads, 'dp', scatter_dimension=0, tiled=True)  57.4 us
    sub x6, other arithmetic, adam_update(): return (weight - rate * (corrected + DECAY * weight), new_first, new_second)  44.4 us
    all_to_all x1, waiting for transfers between devices, local(): lax.all_to_all(grad_tokens, 'dp', 0, 0).reshape(groups * tokens, part_width)  37.7 us
    pallas_call x1, Pallas kernels, pick_rows(): pl.pallas_call(pick_kernel, out_shape=(jax.ShapeDtypeStruct((count, width...  31 us
    pallas_call x1, Pallas kernels, spread_rows(): pl.pallas_call(spread_kernel, out_shape=(jax.ShapeDtypeStruct((width, chu...  26.2 us
    unnamed x73, local copies, waits for them, and re-layouts  25.4 us
  transfers between devices with their start and end apart: 10, of which 4 were waited for; matrix products, arithmetic and copies ran while one was open for 11% of the time, Pallas kernels for 41%

profile of v1, /device:TPU:0, one launch (start us, length us, event | category | flops | bytes accessed | tf_op | source)
XLA Modules:
  0.0 822.7 jit_solution(16013092485171903474)
XLA Ops:
  7.2 1.9 convert_element_type.61
  9.1 1.7 reshape.217
  10.9 1.6 constant_dynamic-slice_fusion.5
  15.4 1.6 reshape.218
  19.3 1.1 dynamic-slice_convert_fusion
  21.3 2.5 reshape.219
  23.8 4.0 dynamic-slice_reduce_fusion
  28.0 1.2 copy.187
  31.8 1.7 fusion.7
  33.5 1.7 concatenate.20
  36.0 6.2 convert_bitcast_fusion
  43.5 9.9 %numbers.1 = s32[8,8,128]{2,1,0:T(8,128)} custom-call(s32[8,128]{1,0:T(8,128)} %bitcast.134), custom_call_target="tpu_custom_call" | custom-call | bytes 36864 | tf_op jit(solution)/shard_map/numbers/pallas_call | solution.py:645
  54.3 11.7 %copy.143.table_ref = f32[24026,96]{1,0:T(8,128)} copy(f32[24026,96]{0,1:T(8,128)} %param.28) | data formatting | bytes 18451968 | tf_op args[4]
  66.0 3.1 pad.22
  69.1 2.6 copy.200
  72.4 31.0 %pick_rows.1 = (bf16[6144,96]{1,0:T(8,128)(2,1)}, s32[6152]{0:T(1024)}, s32[1]{0:T(128)}) custom-call(s32[6144]{0:T(1024)} %sub.47.ids_ref, f32[24026,96]{1,0:T(8,128)} %copy.143.table_ref), custom_call_target="tpu_custom_call" | custom-call | tf_op jit(solution)/shard_map/pick_rows/pallas_call | solution.py:443
  103.3 37.9 %look.1.looked_ref = bf16[768,768]{1,0:T(8,128)(2,1)} custom-call(bf16[8,768,96]{2,1,0:T(8,128)(2,1)} %bitcast.120), custom_call_target="tpu_custom_call" | custom-call | bytes 2359296 | tf_op jit(solution)/shard_map/look/pallas_call | solution.py:645
  141.3 12.1 %all-to-all-start = ((bf16[8,96,3072]{2,1,0:T(8,128)(2,1)}), bf16[8,96,3072]{2,1,0:T(8,128)(2,1)}, u32[]{:S(2)}, u32[]{:S(2)}) async-start(bf16[8,96,3072]{2,1,0:T(8,128)(2,1)} %bitcast.104), calls=%async_computation | async-start | bytes 9437184 | tf_op jit(solution)/shard_map/all_to_all | solution.py:1416
  155.0 3.6 gather_fusion
  162.7 40.5 %first.1 = (bf16[512,576]{1,0:T(8,128)(2,1)}, bf16[512,192]{1,0:T(8,128)(2,1)}, f32[512,128]{1,0:T(8,128)}, f32[512,768]{1,0:T(8,128)}, bf16[256,576]{1,0:T(8,12...) custom-call(bf16[768,768]{1,0:T(8,128)(2,1)} %look.1.looked_ref, ...), custom_call_target="tpu_custom_call" | custom-call | flops 905969664 | bytes 11354112 | tf_op jit(solution)/shard_map/first/pallas_call | solution.py:645
  203.3 20.7 %enc_feed.1 = (f32[512,768]{1,0:T(8,128)}, f32[512,768]{1,0:T(8,128)}, bf16[512,768]{1,0:T(8,128)(2,1)}) custom-call(f32[512,768]{1,0:T(8,128)} %get-tuple-element.74.stream_in_ref.stream_mid_ref, f32[16,768]{1,0:T(8,128)} %get-tuple-element.75.norms_ref, bf16[768,1536]{1,0:T(8,128)(2,1)} %all-gather.11.cloned.1.call-done.w_ref), custom_call_target="tpu_custom_call" | custom-call | flops 1207959552 | bytes 7913472 | tf_op jit(solution)/shard_map/enc_feed/pallas_call | solution.py:645
  224.0 64.6 %all-gather.13.cloned.1.call-done.w_ref = bf16[768,2176]{1,0:T(8,128)(2,1)} async-done(((bf16[96,2176]{1,0:T(8,128)(2,1)}), bf16[768,2176]{1,0:T(8,128)(2,1)}) %all-gather.13.cloned.1.call-update) | async-done | bytes 3342352 | tf_op jit(solution)/shard_map/all_gather | solution.py:1409
  288.5 42.3 %dec.1 = (bf16[256,192]{1,0:T(8,128)(2,1)}, bf16[512,384]{1,0:T(8,128)(2,1)}, bf16[256,192]{1,0:T(8,128)(2,1)}, f32[256,128]{1,0:T(8,128)}, f32[256,768]{1,0:T(8...) custom-call(f32[256,768]{1,0:T(8,128)} %get-tuple-element.73.stream_in_ref, ...), custom_call_target="tpu_custom_call" | custom-call | flops 1207959552 | bytes 9715968 | tf_op jit(solution)/shard_map/dec/pallas_call | solution.py:645
  330.9 53.0 %head.1 = (f32[1,128]{1,0:T(1,128)}, bf16[64,768]{1,0:T(8,128)(2,1)}, bf16[768,3072]{1,0:T(8,128)(2,1)}) custom-call(bf16[512,768]{1,0:T(8,128)(2,1)} %bitcast.137, bf16[768,3072]{1,0:T(8,128)(2,1)} %bitcast.16.table_ref, s32[512,1]{1,0:T(8,128)} %and_select_fusion.targets_ref, f32[512,1]{1,0:T(8,128)} %div.135.weights_ref, f32[1,512]{1,0:T(1,128)} %reshape.235.counted_ref), custom_call_target="tpu_custom_call" | custom-call | flops 7247757312 | bytes 10328576 | tf_op jit(solution)/shard_map/head/pallas_call | solution.py:645
  383.9 41.5 %dec_back.1 = (bf16[768,2176]{1,0:T(8,128)(2,1)}, bf16[192,768]{1,0:T(8,128)(2,1)}, f32[256,768]{1,0:T(8,128)}, f32[512,768]{1,0:T(8,128)}, f32[8,768]{1,0:T(8,128)}, /*index=5*/bf16[8,96,1024]{2,1,0:T(8,128)(2,1)}) custom-call(bf16[64,768]{1,0:T(8,128)(2,1)} %get-tuple-element.85.grad_selected_ref, s32[1,64]{1,0:T(1,128)} %positions_ref.1, ...), custom_call_target="tpu_custom_call" | custom-call | flops 2415919104 | bytes 21340416 | tf_op jit(solution)/shard_map/dec_back/pallas_call | solution.py:645
  425.5 50.6 %mid_back.1 = (bf16[768,2176]{1,0:T(8,128)(2,1)}, bf16[192,768]{1,0:T(8,128)(2,1)}, f32[512,768]{1,0:T(8,128)}, bf16[256,768]{1,0:T(8,128)(2,1)}, f32[8,768]{1,0:T(8,128)}, /*index=5*/bf16[8,96,1024]{2,1,0:T(8,128)(2,1)}) custom-call(f32[512,768]{1,0:T(8,128)} %get-tuple-element.94.grad_memory_ref, f32[512,768]{1,0:T(8,128)} %get-tuple-element.95.stream_enc_ref, ...), custom_call_target="tpu_custom_call" | custom-call | flops 3019898880 | bytes 27729920 | tf_op jit(solution)/shard_map/mid_back/pallas_call | solution.py:645
  476.1 64.4 %last_back.1 = (bf16[768,1280]{1,0:T(8,128)(2,1)}, bf16[512,768]{1,0:T(8,128)(2,1)}, bf16[8,96,1024]{2,1,0:T(8,128)(2,1)}) custom-call(f32[512,768]{1,0:T(8,128)} %get-tuple-element.101.grad_in_ref, bf16[768,768]{1,0:T(8,128)(2,1)} %look.1.looked_ref, f32[512,768]{1,0:T(8,128)} %constant.61.clone.place_enc_ref, f32[16,768]{1,0:T(8,128)} %get-tuple-element.75.norms_ref, ...), custom_call_target="tpu_custom_call" | custom-call | flops 1207959552 | bytes 18939904 | tf_op jit(solution)/shard_map/last_back/pallas_call | solution.py:645
  541.1 1.3 pad_maximum_fusion.1
  542.5 1.5 copy.156
  543.9 22.6 %all-to-all-start.1 = ((bf16[8,768,96]{1,2,0:T(8,128)(2,1)}), bf16[8,768,96]{1,2,0:T(8,128)(2,1)S(1)}, u32[]{:S(2)}, u32[]{:S(2)}) async-start(bf16[8,768,96]{1,2,0:T(8,128)(2,1)} %bitcast.21), calls=%async_computation.1 | async-start | bytes 2359296 | tf_op jit(solution)/shard_map/all_to_all | solution.py:1624
  571.7 37.7 %all-to-all-done.1 = bf16[8,768,96]{1,2,0:T(8,128)(2,1)S(1)} async-done(((bf16[8,768,96]{1,2,0:T(8,128)(2,1)}), bf16[8,768,96]{1,2,0:T(8,128)(2,1)S(1)}, u32[]{:S(2)}, u32[]{:S(2)}) %all-to-all-start.1) | async-done | bytes 1179680 | tf_op jit(solution)/shard_map/all_to_all | solution.py:1624
  609.3 1.5 copy.157
  610.9 26.2 %spread_rows.1 = (f32[96,24576]{1,0:T(8,128)}, f32[1,128]{1,0:T(1,128)}) custom-call(s32[6144]{0:T(1024)} %sub.47.ids_ref, s32[6152]{0:T(1024)} %get-tuple-element.83.list_ref, s32[1]{0:T(128)} %get-tuple-element.84.count_ref, bf16[6144,96]{1,0:T(8,128)(2,1)} %bitcast.106, bf16[8,96,1024]{2,1,0:T(8,128)(2,1)} %get-tuple-element.111.zero_ref, ...), custom_call_target="tpu_custom_call" | custom-call | tf_op jit(solution)/shard_map/spread_rows/pallas_call | solution.py:498
  637.0 6.2 reduce-scatter.8.cloned.1.call-done.three_ref
  643.2 10.0 %all-gather = bf16[384,1280]{1,0:T(8,128)(2,1)S(1)} all-gather(bf16[96,1280]{1,0:T(8,128)(2,1)} %reduce-scatter.8.cloned.1.call-done.three_ref), channel_id=2, replica_groups=mesh['dp'=8,'vocab'=4] {'vocab'}, dimensions={0}, use_global_device_ids=true | all-gather | bytes 1228800 | tf_op jit(solution)/shard_map/all_gather | solution.py:1647
  654.0 2.1 copy.188
  656.1 2.1 copy.159
  658.2 2.4 stack_reshape.40
  662.4 1.1 copy.165
  665.4 57.4 %reduce-scatter.6.cloned.1.call-done.two_ref = bf16[96,2176]{1,0:T(8,128)(2,1)} async-done(((bf16[768,2176]{1,0:T(8,128)(2,1)}), bf16[96,2176]{1,0:T(8,128)(2,1)}) %reduce-scatter.6.cloned.1.call-update) | async-done | bytes 417808 | tf_op jit(solution)/shard_map/reduce_scatter | solution.py:1588
  722.8 12.0 %squares.1 = f32[1,128]{1,0:T(1,128)} custom-call(f32[1,128]{1,0:T(1,128)} %get-tuple-element.114.embedding_ref, bf16[96,2176]{1,0:T(8,128)(2,1)} %reduce-scatter.4.cloned.1.call-done.one_ref, bf16[96,2176]{1,0:T(8,128)(2,1)} %reduce-scatter.6.cloned.1.call-done.two_ref, bf16[96,1280]{1,0:T(8,128)(2,1)} %reduce-scatter.8.cloned.1.call-done.three_ref), custom_call_target="tpu_custom_call" | custom-call | bytes 1082368 | tf_op jit(solution)/shard_map/squares/pallas_call | solution.py:645
  735.6 23.9 %multiply_subtract_fusion = (f32[24026,96]{0,1:T(8,128)}, f32[24026,96]{0,1:T(8,128)}, f32[24026,96]{0,1:T(8,128)}) fusion(f32[24026,96]{0,1:T(8,128)} %param.28, f32[]{:T(128)S(6)} %min_shard_map.3, f32[96,24576]{1,0:T(8,128)} %get-tuple-element.118, f32[24026,96]{0,1:T(8,128)} %param.34, f32[24026,96]{0,1:T(8,128)} %param.40), kind=kLoop, calls=%fused_computation.5 | loop fusion | flops 36903936 | bytes 64581892 | tf_op jit(solution)/shard_map/sub | solution.py:214
  759.5 1.5 multiply_subtract_fusion.5
  761.0 1.5 copy.174
  762.5 1.5 copy.175
  764.0 1.5 copy.176
  765.4 3.4 multiply_subtract_fusion.4
  768.9 1.1 slice.136
  770.0 2.3 fusion.20
  772.3 1.9 slice.135
  774.1 2.3 fusion.19
  777.6 1.3 stack_reshape.42
  778.8 1.3 copy.189
  780.9 1.3 stack_reshape.41
  782.2 1.9 reshape.234
  784.2 1.9 copy.201
  786.1 3.4 stack_reshape.47
  789.4 1.9 reshape.233
  791.4 1.9 copy.202
  793.3 2.5 stack_reshape.46
  795.9 7.0 multiply_subtract_fusion.3
  802.9 4.4 multiply_subtract_fusion.2
  807.3 1.5 copy-done.6
  809.0 4.3 multiply_subtract_fusion.1
  (138 shorter events, 29.3 us)
Async XLA Ops:
  7.2 155.5 %all-gather.9.cloned.1.call-start = ((), (), s32[]{:S(2)}) async-start(), calls=%async_computation.5 | async-start | bytes 3317760 | tf_op jit(solution)/shard_map/all_gather | solution.py:1407
  12.5 2.1 copy-start.2
  12.7 5.9 copy-start.25
  13.9 7.3 copy-start.1
  23.8 6.3 copy-start.20
  23.8 7.2 copy-start.17
  23.8 8.0 copy-start.16
  23.8 9.7 %copy-start.18 = (bf16[96,640]{1,0:T(8,128)(2,1)S(1)}, bf16[96,640]{1,0:T(8,128)(2,1)}, u32[]{:S(2)}) copy-start(bf16[96,640]{1,0:T(8,128)(2,1)} %pad.24) | copy-start | bytes 368644
  23.8 9.7 %copy-start.19 = (bf16[96,640]{1,0:T(8,128)(2,1)S(1)}, bf16[96,640]{1,0:T(8,128)(2,1)}, u32[]{:S(2)}) copy-start(bf16[96,640]{1,0:T(8,128)(2,1)} %pad.25) | copy-start | bytes 368644
  35.2 168.1 %all-gather.11.cloned.1.call-start = ((), (), s32[]{:S(2)}) async-start(), calls=%async_computation.6 | async-start | bytes 2654208 | tf_op jit(solution)/shard_map/all_gather | solution.py:1408
  35.9 6.9 copy-start.26
  35.9 6.9 copy-start.27
  35.9 6.9 copy-start.28
  141.3 189.6 %all-to-all-start = ((bf16[8,96,3072]{2,1,0:T(8,128)(2,1)}), bf16[8,96,3072]{2,1,0:T(8,128)(2,1)}, u32[]{:S(2)}, u32[]{:S(2)}) async-start(bf16[8,96,3072]{2,1,0:T(8,128)(2,1)} %bitcast.104), calls=%async_computation | async-start | bytes 9437184 | tf_op jit(solution)/shard_map/all_to_all | solution.py:1416
  153.4 135.2 %all-gather.13.cloned.1.call-start = ((), (), s32[]{:S(2)}) async-start(), calls=%async_computation.7 | async-start | bytes 3760128 | tf_op jit(solution)/shard_map/all_gather | solution.py:1409
  154.1 412.5 %reduce-scatter.4.cloned.1.call-start = ((), (), s32[]{:S(2)}) async-start(), calls=%async_computation.8 | async-start | bytes 3760128 | tf_op jit(solution)/shard_map/reduce_scatter | solution.py:1558
  425.5 217.7 %reduce-scatter.8.cloned.1.call-start = ((), (), s32[]{:S(2)}) async-start(), calls=%async_computation.10 | async-start | bytes 2211840 | tf_op jit(solution)/shard_map/reduce_scatter | solution.py:1620
  540.6 182.2 %reduce-scatter.6.cloned.1.call-start = ((), (), s32[]{:S(2)}) async-start(), calls=%async_computation.9 | async-start | bytes 3760128 | tf_op jit(solution)/shard_map/reduce_scatter | solution.py:1588
  543.9 65.4 %all-to-all-start.1 = ((bf16[8,768,96]{1,2,0:T(8,128)(2,1)}), bf16[8,768,96]{1,2,0:T(8,128)(2,1)S(1)}, u32[]{:S(2)}, u32[]{:S(2)}) async-start(bf16[8,768,96]{1,2,0:T(8,128)(2,1)} %bitcast.21), calls=%async_computation.1 | async-start | bytes 2359296 | tf_op jit(solution)/shard_map/all_to_all | solution.py:1624
  566.6 202.3 %all-gather.17.cloned.1.call-start = ((), (), s32[]{:S(2)}) async-start(), calls=%async_computation.12 | async-start | bytes 2088960 | tf_op jit(solution)/shard_map/all_gather | solution.py:1645
  567.3 205.0 %all-gather.15.cloned.1.call-start = ((), (), s32[]{:S(2)}) async-start(), calls=%async_computation.11 | async-start | bytes 2088960 | tf_op jit(solution)/shard_map/all_gather | solution.py:1646
  735.6 24.0 %copy-start.21 = (f32[14,96]{0,1:T(8,128)S(1)}, f32[14,96]{0,1:T(8,128)}, u32[]{:S(2)}) copy-start(f32[14,96]{0,1:T(8,128)} %copy.173) | copy-start | bytes 16132
  735.6 23.9 %copy-start.22 = (f32[14,96]{0,1:T(8,128)S(1)}, f32[14,96]{0,1:T(8,128)}, u32[]{:S(2)}) copy-start(f32[14,96]{0,1:T(8,128)} %copy.172) | copy-start | bytes 16132
  735.6 23.9 %copy-start.23 = (f32[14,96]{0,1:T(8,128)S(1)}, f32[14,96]{0,1:T(8,128)}, u32[]{:S(2)}) copy-start(f32[14,96]{0,1:T(8,128)} %copy.170) | copy-start | bytes 16132
  735.6 23.9 %copy-start.24 = (f32[14,96]{0,1:T(8,128)S(1)}, f32[14,96]{0,1:T(8,128)}, u32[]{:S(2)}) copy-start(f32[14,96]{0,1:T(8,128)} %copy.171) | copy-start | bytes 16132
  735.6 29.8 %copy-start.3 = (f32[3,96,768]{2,1,0:T(8,128)S(1)}, f32[3,96,768]{2,1,0:T(8,128)}, u32[]{:S(2)}) copy-start(f32[3,96,768]{2,1,0:T(8,128)} %param.30) | copy-start | bytes 2654212
  735.6 29.8 %copy-start.14 = (bf16[1,96,768]{2,1,0:T(8,128)(2,1)S(1)}, bf16[1,96,768]{2,1,0:T(8,128)(2,1)}, u32[]{:S(2)}) copy-start(bf16[1,96,768]{2,1,0:T(8,128)(2,1)} %stack_reshape.45) | copy-start | bytes 442372
  735.6 29.8 %copy-start.15 = (bf16[1,96,768]{2,1,0:T(8,128)(2,1)S(1)}, bf16[1,96,768]{2,1,0:T(8,128)(2,1)}, u32[]{:S(2)}) copy-start(bf16[1,96,768]{2,1,0:T(8,128)(2,1)} %stack_reshape.44) | copy-start | bytes 442372
  795.8 7.0 copy-start.4
  795.8 7.0 copy-start.7
  795.9 7.0 copy-start.8
  795.9 7.0 copy-start.9
  795.9 7.0 copy-start.10
  802.9 4.4 copy-start
  802.9 4.4 copy-start.5
  802.9 5.9 copy-start.6
  802.9 5.9 copy-start.11
  802.9 6.0 copy-start.12
  802.9 6.1 copy-start.13
  809.0 4.3 copy-start.29
Sparse Core Ops, SparseCore 0:
  35.3 61.0 all-gather.8
  99.1 52.1 all-gather.10
  157.0 131.5 all-gather.12
  425.6 131.2 reduce-scatter.3
  560.6 82.5 reduce-scatter.7
  646.7 76.0 reduce-scatter.5
  724.4 19.4 all-gather.16
  745.5 20.1 all-gather.14

commit v2 on v1

--- a/solution.py
+++ b/solution.py
@@ -420,32 +420,76 @@
     return np.concatenate([np.sin(angles), np.cos(angles)], axis=1).astype(np.float32)
 
 
-def pick_kernel(ids_ref, table_ref, out_ref, list_ref, count_ref, wide_ref):
-    count, rows = wide_ref.shape[0], table_ref.shape[0]
-
+def hits_kernel(rows, span, ids_ref, list_ref):
     def one(step, found):
         for inner in range(8):
             slot = step * 8 + inner
             row = ids_ref[slot]
-            hit = (row >= 0) & (row < rows)
-            safe = jnp.where(hit, row, 0)
-            wide_ref[pl.ds(slot, 1), :] = table_ref[pl.ds(safe, 1), :] * jnp.where(hit, 1.0, 0.0)
-            list_ref[found] = slot
-            found = found + jnp.where(hit, 1, 0)
+            list_ref[found] = row * span + slot
+            found = found + jnp.where((row >= 0) & (row < rows), 1, 0)
         return found
 
-    count_ref[0] = lax.fori_loop(0, count // 8, one, 0)
+    list_ref[list_ref.shape[0] - 1] = lax.fori_loop(0, ids_ref.shape[0] // 8, one, 0)
+
+
+def list_hits(local_ids, rows, span):
+    return pl.pallas_call(
+        partial(hits_kernel, rows, span),
+        out_shape=jax.ShapeDtypeStruct((span,), jnp.int32),
+        in_specs=[pl.BlockSpec(memory_space=pltpu.SMEM)],
+        out_specs=pl.BlockSpec(memory_space=pltpu.SMEM),
+        name="list_hits",
+    )(local_ids)
+
+
+def over_hits(lists_ref, visit):
+    groups, span = lists_ref.shape
+    for group in range(groups):
+
+        def one(step, carry):
+            entry = lists_ref[group, step]
+            visit(group, entry // span, lax.rem(entry, span))
+            return carry
+
+        lax.fori_loop(0, lists_ref[group, span - 1], one, 0)
+
+
+def pick_kernel(lists_ref, table_ref, out_ref, across_ref, wide_ref, turned_ref):
+    tokens = wide_ref.shape[0] // lists_ref.shape[0]
+    width, rows = table_ref.shape
+    total = across_ref.shape[1]
+    wide_ref[...] = jnp.zeros_like(wide_ref)
+    step = 1024
+    for low in range(0, total, step):
+        high = max(min(low + step, rows), low)
+        if high > low:
+            across_ref[:, low:high] = lowered(table_ref[:, low:high])
+        if high < low + step:
+            across_ref[:, high : low + step] = jnp.zeros((width, low + step - high), jnp.bfloat16)
+
+    def turn(piece, carry):
+        for part in range(8):
+            start = pl.multiple_of(piece * step + part * 128, 128)
+            block = across_ref[:, pl.ds(start, 128)].astype(jnp.float32)
+            turned_ref[pl.ds(start, 128), :] = jnp.transpose(block)
+        return carry
+
+    lax.fori_loop(0, total // step, turn, 0)
+
+    def visit(group, row, slot):
+        wide_ref[pl.ds(group * tokens + slot, 1), :] = turned_ref[pl.ds(row, 1), :]
+
+    over_hits(lists_ref, visit)
     out_ref[...] = wide_ref[...].astype(jnp.bfloat16)
 
 
-def pick_rows(local_ids, table):
-    count, width = local_ids.shape[0], table.shape[1]
+def pick_rows(lists, count, table, total):
+    width = table.shape[0]
     return pl.pallas_call(
         pick_kernel,
         out_shape=(
             jax.ShapeDtypeStruct((count, width), jnp.bfloat16),
-            jax.ShapeDtypeStruct((count + 8,), jnp.int32),
-            jax.ShapeDtypeStruct((1,), jnp.int32),
+            jax.ShapeDtypeStruct((width, total), jnp.bfloat16),
         ),
         in_specs=[
             pl.BlockSpec(memory_space=pltpu.SMEM),
@@ -453,35 +497,38 @@
         ],
         out_specs=(
             pl.BlockSpec(memory_space=pltpu.VMEM),
-            pl.BlockSpec(memory_space=pltpu.SMEM),
-            pl.BlockSpec(memory_space=pltpu.SMEM),
+            pl.BlockSpec(memory_space=pltpu.VMEM),
         ),
-        scratch_shapes=[pltpu.VMEM((count, width), jnp.float32)],
+        scratch_shapes=[
+            pltpu.VMEM((count, width), jnp.float32),
+            pltpu.VMEM((total, width), jnp.float32),
+        ],
         compiler_params=pltpu.CompilerParams(vmem_limit_bytes=VMEM_BYTES),
         name="pick_rows",
-    )(local_ids, table)
-
-
-def spread_kernel(ids_ref, list_ref, count_ref, grads_ref, zero_ref, one_ref, two_ref, out_ref, squares_ref, wide_ref, rows_ref):
-    width = grads_ref.shape[1]
-    chunks, _, piece_columns = zero_ref.shape
-    chunk = 3 * piece_columns
-    rows_ref[...] = grads_ref[...].astype(jnp.float32)
+    )(lists, table)
+
+
+def spread_kernel(
+    lists_ref, grads_ref, head_ref, out_ref, squares_ref, wide_ref, rows_ref
+):
+    shares, groups, quarter, width = grads_ref.shape
+    tokens = shares * quarter
+    chunks, _, chunk = head_ref.shape
+    for index in range(shares):
+        for number in range(groups):
+            start = number * tokens + index * quarter
+            rows_ref[start : start + quarter, :] = grads_ref[index, number].astype(jnp.float32)
     wide_ref[...] = jnp.zeros_like(wide_ref)
 
-    def one(step, carry):
-        slot = list_ref[step]
-        row = ids_ref[slot]
-        wide_ref[pl.ds(row, 1), 0:width] += rows_ref[pl.ds(slot, 1), :]
-        return carry
-
-    lax.fori_loop(0, count_ref[0], one, 0)
+    def visit(group, row, slot):
+        wide_ref[pl.ds(row, 1), 0:width] += rows_ref[pl.ds(group * tokens + slot, 1), :]
+
+    over_hits(lists_ref, visit)
 
     def turn(piece, total):
         for part in range(chunk // 128):
+            column = part * 128
             start = pl.multiple_of(piece * chunk + part * 128, 128)
-            head_ref = (zero_ref, one_ref, two_ref)[part * 128 // piece_columns]
-            column = part * 128 % piece_columns
             block = jnp.transpose(wide_ref[pl.ds(start, 128), :])[:width]
             block = block + head_ref[piece, :, column : column + 128].astype(jnp.float32)
             out_ref[:, pl.ds(start, 128)] = block
@@ -492,28 +539,28 @@
     squares_ref[...] = jnp.sum(total, axis=0, keepdims=True)
 
 
-def spread_rows(local_ids, hit_list, hit_count, grads, head):
-    chunks, width, piece_columns = head[0].shape
-    chunk = 3 * piece_columns
+def spread_rows(lists, grads, head):
+    chunks, width, chunk = head.shape
+    shares, groups, quarter, _ = grads.shape
     return pl.pallas_call(
         spread_kernel,
         out_shape=(
             jax.ShapeDtypeStruct((width, chunks * chunk), jnp.float32),
             jax.ShapeDtypeStruct((1, 128), jnp.float32),
         ),
-        in_specs=[pl.BlockSpec(memory_space=pltpu.SMEM)] * 3
-        + [pl.BlockSpec(memory_space=pltpu.VMEM)] * 4,
+        in_specs=[pl.BlockSpec(memory_space=pltpu.SMEM)]
+        + [pl.BlockSpec(memory_space=pltpu.VMEM)] * 2,
         out_specs=(
             pl.BlockSpec(memory_space=pltpu.VMEM),
             pl.BlockSpec(memory_space=pltpu.VMEM),
         ),
         scratch_shapes=[
             pltpu.VMEM((chunks * chunk, 128), jnp.float32),
-            pltpu.VMEM(grads.shape, jnp.float32),
+            pltpu.VMEM((shares * groups * quarter, width), jnp.float32),
         ],
         compiler_params=pltpu.CompilerParams(vmem_limit_bytes=VMEM_BYTES),
         name="spread_rows",
-    )(local_ids, hit_list, hit_count, grads, *head)
+    )(lists, grads, head)
 
 
 MESH = pl.DeviceIdType.MESH
@@ -608,28 +655,131 @@
 
 
 class Exchange:
-    def __init__(self, source_ref, target_ref, sems, groups, index):
+    def __init__(self, block_of, target_ref, sems, groups):
         group, share = lax.axis_index("dp"), lax.axis_index("vocab")
-        columns = target_ref.shape[2]
-        at = pl.ds(index * columns, columns)
         self.copies = [
             send(
-                source_ref.at[peer[0], :, at],
-                target_ref.at[group],
-                sems.at[0, step],
-                sems.at[1, step],
-                peer,
+                block_of(peer[0]), target_ref.at[group], sems.at[0, step], sems.at[1, step], peer
             )
             for step, peer in enumerate(group_peers(group, share, groups))
         ]
         self.keep = pltpu.make_async_copy(
-            source_ref.at[group, :, at], target_ref.at[group], sems.at[0, groups - 1]
+            block_of(group), target_ref.at[group], sems.at[0, groups - 1]
         )
         self.keep.start()
 
     def finish(self):
         self.keep.wait()
         for copy in self.copies:
+            copy.wait()
+
+
+def head_blocks(source_ref, start, columns):
+    return lambda group: source_ref.at[group, :, pl.ds(start, columns)]
+
+
+def table_blocks(source_ref, chunk, start, columns):
+    return lambda group: source_ref.at[:, pl.ds(pl.multiple_of(group * chunk + start, 128), columns)]
+
+
+def pair_of(group, share):
+    place = lax.rem(group, 2)
+    return (group + 1 - 2 * place, share), place
+
+
+def line_places(group):
+    pair, place = group // 2, lax.rem(group, 2)
+    high, low = pair // 2, lax.rem(pair, 2)
+    far = ((1 - high) * 2 + low) * 2 + place
+    near = (high * 2 + 1 - low) * 2 + place
+    return high, low, far, near
+
+
+def line_scratch(width, columns):
+    return [
+        pltpu.VMEM((2, 2, width, columns), jnp.bfloat16),
+        pltpu.VMEM((2, width, columns), jnp.bfloat16),
+        pltpu.VMEM((width, columns), jnp.bfloat16),
+        pltpu.SemaphoreType.DMA((6,)),
+    ]
+
+
+class Owned:
+    def __init__(self, blocks, refs):
+        group, self.share = lax.axis_index("dp"), lax.axis_index("vocab")
+        self.high, self.low, self.far, self.near = line_places(group)
+        self.pair, self.place = pair_of(group, self.share)
+        self.blocks = blocks
+        self.pair_in, self.near_in, self.far_in, self.sems = refs
+
+    def begin(self):
+        source = self.blocks.at[:, :, 1 - self.place]
+        self.zero = send(source, self.pair_in, self.sems.at[0], self.sems.at[1], self.pair)
+
+    def beside(self):
+        self.zero.wait()
+        self.blocks[:, :, self.place] = lowered(
+            self.blocks[:, :, self.place].astype(jnp.float32) + self.pair_in[...].astype(jnp.float32)
+        )
+        self.one = send(
+            self.blocks.at[:, 1 - self.low, self.place],
+            self.near_in,
+            self.sems.at[2],
+            self.sems.at[3],
+            (self.near, self.share),
+        )
+
+    def beyond(self):
+        self.one.wait()
+        self.blocks[:, self.low, self.place] = lowered(
+            self.blocks[:, self.low, self.place].astype(jnp.float32)
+            + self.near_in[...].astype(jnp.float32)
+        )
+        self.two = send(
+            self.blocks.at[1 - self.high, self.low, self.place],
+            self.far_in,
+            self.sems.at[4],
+            self.sems.at[5],
+            (self.far, self.share),
+        )
+
+    def finish(self):
+        self.two.wait()
+        return lowered(
+            self.blocks[self.high, self.low, self.place].astype(jnp.float32)
+            + self.far_in[...].astype(jnp.float32)
+        )
+
+
+class Late:
+    def __init__(self, source, buffer, sem):
+        self.copy, self.buffer, self.waiting = pltpu.make_async_copy(source, buffer, sem), buffer, True
+        self.copy.start()
+
+    def __call__(self):
+        if self.waiting:
+            self.copy.wait()
+            self.waiting = False
+        return self.buffer
+
+
+class ShareGather:
+    def __init__(self, target_ref, sems):
+        _, self.share, _, self.core_peer, self.side_peer = places()
+        self.target, self.sems = target_ref, sems
+        block = target_ref.at[self.share]
+        self.one = send(block, block, sems.at[0, 0], sems.at[1, 0], self.side_peer)
+
+    def middle(self):
+        self.one.wait()
+        both = [self.target.at[index] for index in (self.share, self.side_peer[1])]
+        self.two = [
+            send(block, block, self.sems.at[0, 1 + step], self.sems.at[1, 1 + step], self.core_peer)
+            for step, block in enumerate(both)
+        ]
+
+    def finish(self):
+        for copy in self.two:
             copy.wait()
 
 
@@ -740,19 +890,23 @@
 
 
 def first_kernel(
-    shares,
-    looked_ref, place_enc_ref, place_dec_ref, w_ref,
+    groups, shares, start, first_wide,
+    looked_ref, place_enc_ref, place_dec_ref, w_ref, across_ref,
     qkv_enc_ref, context_enc_ref, logs_enc_ref, stream_enc_ref,
     qkv_dec_ref, context_dec_ref, logs_dec_ref, stream_dec_ref,
-    out_rows_ref, norms_ref,
-    blocks_ref, block_sems, local_sem, *total_refs,
+    out_rows_ref, norms_ref, table_ref,
+    table_sems, blocks_ref, block_sems, local_sem, *total_refs,
 ):
     group, share, _, _, _ = places()
     peers = share_peers(group, share, shares)
-    meet(peers)
+    meet(peers + group_peers(group, share, groups))
+    chunk, columns = across_ref.shape[1] // groups, table_ref.shape[2]
+    exchange = Exchange(
+        table_blocks(across_ref, chunk, start, columns), table_ref, table_sems, groups
+    )
     _, rows, wide = blocks_ref.shape
     own = qkv_enc_ref.shape[1] // 3
-    padded = w_ref.shape[1] - wide
+    padded = first_wide - wide
     enc_start, dec_start, out_start = 0, padded // 2, padded
     window = pl.ds(out_start, wide)
     copies = []
@@ -766,7 +920,7 @@
     )
     keep.start()
 
-    turned = jnp.transpose(w_ref[:, w_ref.shape[1] - 128 :].astype(jnp.float32))
+    turned = jnp.transpose(w_ref[:, first_wide - 128 : first_wide].astype(jnp.float32))
     norms_ref[...] = turned[64:80]
 
     enc_total, dec_total = Total(total_refs[:4]), Total(total_refs[4:])
@@ -800,32 +954,49 @@
     stream_enc_ref[...] += enc_total.finish()
     dec_total.last()
     stream_dec_ref[...] += dec_total.finish()
-
-
-def enc_feed_kernel(stream_in_ref, norms_ref, w_ref, pre_ref, stream_ref, memory_ref, *total_refs):
+    exchange.finish()
+
+
+def enc_feed_kernel(
+    groups, start, first_wide,
+    stream_in_ref, norms_ref, w_early_ref, across_ref,
+    pre_ref, stream_ref, memory_ref, table_ref,
+    table_sems, w_ref, w_sem, *total_refs,
+):
     group, share, _, core_peer, side_peer = places()
-    meet([core_peer, side_peer])
+    load = Late(w_early_ref.at[:, pl.ds(first_wide, w_ref.shape[1])], w_ref, w_sem)
+    meet([core_peer, side_peer] + group_peers(group, share, groups))
+    chunk, columns = across_ref.shape[1] // groups, table_ref.shape[2]
+    exchange = Exchange(
+        table_blocks(across_ref, chunk, start, columns), table_ref, table_sems, groups
+    )
     width = stream_in_ref.shape[1]
     total = Total(total_refs)
     normed, _ = norm_forward(stream_in_ref[...], *gain_of(norms_ref, 1))
     hidden = w_ref.shape[1] - width
+    load()
     pre_ref[...] = matmul(lowered(normed), w_ref[:, :hidden])
     activated = lowered(jax.nn.silu(pre_ref[...]))
     total.begin(matmul(activated, w_ref[:, hidden:]))
     stream_ref[...] = stream_in_ref[...] + total.rest()
     memory, _ = norm_forward(stream_ref[...], *gain_of(norms_ref, 2))
     memory_ref[...] = lowered(memory)
+    exchange.finish()
 
 
 def dec_kernel(
-    groups,
-    stream_in_ref, memory_ref, norms_ref, w_ref, out_rows_ref, positions_ref,
-    q_ref, kv_ref, context_ref, logs_ref, stream_mid_ref, pre_ref, stream_ref, selected_ref,
-    own_ref, select_sems, *total_refs,
+    groups, start,
+    stream_in_ref, memory_ref, norms_ref, w_ref, out_rows_ref, positions_ref, across_ref,
+    q_ref, kv_ref, context_ref, logs_ref, stream_mid_ref, pre_ref, stream_ref, selected_ref, table_ref,
+    own_ref, select_sems, table_sems, *total_refs,
 ):
     group, share, _, core_peer, side_peer = places()
     peers = group_peers(group, share, groups)
     meet([core_peer, side_peer] + peers)
+    chunk, columns = across_ref.shape[1] // groups, table_ref.shape[2]
+    exchange = Exchange(
+        table_blocks(across_ref, chunk, start, columns), table_ref, table_sems, groups
+    )
     width = stream_in_ref.shape[1]
     own = q_ref.shape[1]
     hidden = pre_ref.shape[1]
@@ -852,6 +1023,7 @@
         send(own_ref, selected_ref.at[group], select_sems.at[0, step], select_sems.at[1, step], peer)
         for step, peer in enumerate(peers)
     ]
+    exchange.finish()
     for copy in copies:
         copy.wait()
 
@@ -870,7 +1042,7 @@
 
 def head_kernel(
     groups, shares, shard_rows,
-    selected_ref, table_ref, targets_ref, weights_ref, counted_ref,
+    selected_ref, zero_ref, one_ref, two_ref, three_ref, targets_ref, weights_ref, counted_ref,
     loss_ref, grad_out_ref, head_ref,
     logits_ref, dz_ref, stats_ref, turned_ref, share_stats_ref, group_stats_ref, stat_sems,
     part_ref, core_ref, side_ref, group_ref, sum_ref, sems,
@@ -880,17 +1052,21 @@
     near, far = share_peers(group, share, shares), group_peers(group, share, groups)
     meet(near + far)
     rows, width = selected_ref.shape
-    chunk = table_ref.shape[1]
+    chunk = logits_ref.shape[1]
+    tables = (zero_ref, one_ref, two_ref, three_ref)
+    starts = np.cumsum([0] + [ref.shape[1] for ref in tables])
     vocab_total = shard_rows * shares
     first = group * chunk
     limit = jnp.minimum(shard_rows - first, vocab_total - 1 - share * shard_rows - first)
-    block = 512
+    block = 384
     step_rows = 32
 
-    for part in range(chunk // block):
-        logits_ref[:, part * block : (part + 1) * block] = matmul(
-            selected_ref[...], table_ref[:, part * block : (part + 1) * block]
-        )
+    for ref, start in zip(tables, starts):
+        step = 512 if ref.shape[1] % 512 == 0 else 384
+        for low in range(0, ref.shape[1], step):
+            logits_ref[:, start + low : start + low + step] = matmul(
+                selected_ref[...], ref[:, low : low + step]
+            )
     stats_ref[...] = jnp.zeros_like(stats_ref)
 
     def gather_stats(step, carry):
@@ -947,7 +1123,10 @@
     lax.fori_loop(0, rows // step_rows, make_dz, 0)
     loss_rows = rows // groups
     half, quarter = loss_rows // 2, loss_rows // 4
-    part_ref[...] = lowered(times_transposed(dz_ref[...], table_ref[...])).reshape(part_ref.shape)
+    grad_rows = 0.0
+    for ref, start in zip(tables, starts):
+        grad_rows = grad_rows + times_transposed(dz_ref[:, start : start + ref.shape[1]], ref[...])
+    part_ref[...] = lowered(grad_rows).reshape(part_ref.shape)
     mine = pl.ds(pl.multiple_of(core * half, 16), half)
     other = pl.ds(pl.multiple_of((1 - core) * half, 16), half)
     copy = send(part_ref.at[:, other, :], core_ref, sems.at[0, 0], sems.at[1, 0], core_peer)
@@ -995,6 +1174,11 @@
         copy.wait()
 
 
+def put_grads(grads_ref, start, value):
+    shape = grads_ref.shape[:4] + (value.shape[1],)
+    grads_ref[:, :, :, :, start : start + value.shape[1]] = lowered(value).reshape(shape)
+
+
 def feed_grads(grad_ref, stream_ref, pre_ref, norms_ref, row, w_ref, grads_ref, total):
     width = stream_ref.shape[1]
     hidden = pre_ref.shape[1]
@@ -1009,9 +1193,9 @@
     )
     total.begin(times_transposed(grad_pre, w_ref[:, :hidden]))
     activated = lowered(pre * sigmoid_pre)
-    grads_ref[:, hidden : hidden + width] = lowered(contract_rows(activated, grad_low))
+    put_grads(grads_ref, hidden, contract_rows(activated, grad_low))
     total.middle()
-    grads_ref[:, :hidden] = lowered(contract_rows(lowered(normed), grad_pre))
+    put_grads(grads_ref, 0, contract_rows(lowered(normed), grad_pre))
 
 
 def norm_step(grad_ref, stream_ref, norms_ref, row, summed, rows_ref, slot):
@@ -1025,145 +1209,178 @@
     return grad_ref[...] + grad_in
 
 
-def dec_back_kernel(
-    groups,
-    grad_selected_ref, positions_ref, stream_in_ref, stream_mid_ref, stream_ref, pre_ref, memory_ref,
-    norms_ref, w_ref, out_rows_ref, q_ref, kv_ref, context_ref, logs_ref, head_in_ref,
-    grads_ref, grad_out_rows_ref, grad_ref, grad_memory_ref, rows_ref, head_out_ref,
-    head_sems, grad_context_ref, gq_ref, gkv_ref, *total_refs,
+def back_kernel(
+    groups, shares, first_wide, norm_start, norm_count, refs_in, refs_out, *refs
 ):
-    group, share, _, core_peer, side_peer = places()
-    meet([core_peer, side_peer] + group_peers(group, share, groups))
-    exchange = Exchange(head_in_ref, head_out_ref, head_sems, groups, 0)
-    width = stream_ref.shape[1]
+    inputs, outputs, scratch = refs[:refs_in], refs[refs_in : refs_in + refs_out], refs[refs_in + refs_out :]
+    (
+        grad_selected_ref, positions_ref, stream_out_ref, stream_mid_ref, pre_dec_ref, norms_ref, w_dec_hbm,
+        out_rows_hbm, memory_hbm, stream_dec_hbm, q_ref, kv_ref, context_cross_ref, logs_cross_ref,
+        stream_two_hbm, stream_enc_hbm, pre_enc_hbm, w_early_hbm, looked_hbm, place_enc_hbm, place_dec_ref,
+        qkv_dec_ref, context_dec_ref, logs_dec_ref, qkv_enc_ref, context_enc_ref, logs_enc_ref,
+        head_in_ref,
+    ) = inputs
+    head_out_ref, own_tokens_ref, dec_shares_ref, own_ref, squares_ref = outputs
+    (
+        head_sems, load_sems, w_ref, w_enc_ref, out_rows_ref, memory_ref, stream_dec_ref, stream_two_ref,
+        stream_enc_ref, pre_enc_ref, looked_ref,
+        dec_grads_ref, mid_grads_ref, last_grads_ref,
+        grad_ref, grad_enc_ref,
+        context_ref, gq_ref, gkv_ref, gqkv_ref, gqkv_enc_ref, context_enc_grad_ref,
+        g_enc_ref, g_self_ref, g_cross_ref, rows_dec_ref, rows_mid_ref, rows_ref,
+        norm_rows_ref, turned_ref, blocks_ref, block_sems, cut_ref, token_sems, share_sems, dec_sems, dec_own_ref,
+        local_sems,
+    ) = scratch[:38]
+    rest = scratch[38:]
+    stream_ref = pre_enc_ref
+    small_one, large_one = rest[:4], rest[4:8]
+    small_two, large_two = small_one[:1] + rest[8:11], large_one[:1] + rest[11:14]
+    dec_line = Owned(dec_grads_ref, rest[14:18])
+    mid_line = Owned(mid_grads_ref, rest[18:22])
+    last_line = Owned(last_grads_ref, rest[22:26])
+    group, share, core, core_peer, side_peer = places()
+    peers = share_peers(group, share, shares)
+    load_w_dec = Late(w_dec_hbm, w_ref, load_sems.at[0])
+    load_rows = Late(out_rows_hbm, out_rows_ref, load_sems.at[1])
+    load_memory = Late(memory_hbm, memory_ref, load_sems.at[2])
+    load_dec = Late(stream_dec_hbm, stream_dec_ref, load_sems.at[3])
+    load_two = Late(stream_two_hbm, stream_two_ref, load_sems.at[4])
+    load_enc = Late(stream_enc_hbm, stream_enc_ref, load_sems.at[5])
+    load_pre = Late(pre_enc_hbm, pre_enc_ref, load_sems.at[6])
+    load_w_enc = Late(
+        w_early_hbm.at[:, pl.ds(first_wide, w_enc_ref.shape[1])], w_enc_ref, load_sems.at[7]
+    )
+    load_looked = Late(looked_hbm, looked_ref, load_sems.at[8])
+    meet(peers + group_peers(group, share, groups))
+    exchange = Exchange(
+        head_blocks(head_in_ref, 0, head_out_ref.shape[2]), head_out_ref, head_sems, groups
+    )
+    width = stream_out_ref.shape[1]
     own = q_ref.shape[1]
-    hidden = pre_ref.shape[1]
+    hidden = pre_dec_ref.shape[1]
     in_start = hidden + width
-    feed_total, cross_total, memory_total = [Total(total_refs[4 * k : 4 * k + 4]) for k in range(3)]
-    rows_ref[...] = jnp.zeros_like(rows_ref)
-    down = lax.broadcasted_iota(jnp.int32, (stream_ref.shape[0], grad_selected_ref.shape[0]), 0)
+    starts = (0, own, 2 * own)
+    for rows in (rows_dec_ref, rows_mid_ref, rows_ref):
+        rows[...] = jnp.zeros_like(rows)
+
+    total = Total(small_one)
+    down = lax.broadcasted_iota(jnp.int32, (stream_out_ref.shape[0], grad_selected_ref.shape[0]), 0)
     chosen = lowered(jnp.where(down == positions_ref[...], 1.0, 0.0))
     grad_final = matmul(chosen, grad_selected_ref[...])
-    grad_ref[...] = norm_step(None, stream_ref, norms_ref, 6, grad_final, rows_ref, 0)
-    feed_grads(grad_ref, stream_mid_ref, pre_ref, norms_ref, 5, w_ref, grads_ref, feed_total)
-    feed_total.last()
+    grad_ref[...] = norm_step(None, stream_out_ref, norms_ref, 6, grad_final, rows_dec_ref, 0)
+    load_w_dec()
+    feed_grads(grad_ref, stream_mid_ref, pre_dec_ref, norms_ref, 5, w_ref, dec_grads_ref, total)
+    total.last()
     grad_ref[...] = norm_step(
-        grad_ref, stream_mid_ref, norms_ref, 5, feed_total.finish(), rows_ref, 2
-    )
+        grad_ref, stream_mid_ref, norms_ref, 5, total.finish(), rows_dec_ref, 2
+    )
+
+    cross_total, memory_total = Total(small_two), Total(large_one)
     grad_low = lowered(grad_ref[...])
-    grad_context_ref[...] = lowered(times_transposed(grad_low, out_rows_ref[2]))
+    load_rows()
+    context_ref[...] = lowered(times_transposed(grad_low, out_rows_ref[2]))
     heads_backward(
-        q_ref, kv_ref, (0, 0, own), logs_ref, grad_context_ref, gq_ref, gkv_ref, (0, 0, own), False
+        q_ref, kv_ref, (0, 0, own), logs_cross_ref, context_ref, gq_ref, gkv_ref, (0, 0, own), False
     )
     memory_total.begin(
         times_transposed(gkv_ref[...], w_ref[:, in_start + own : in_start + 3 * own])
     )
     cross_total.begin(times_transposed(gq_ref[...], w_ref[:, in_start : in_start + own]))
-    grad_out_rows_ref[...] = lowered(contract_rows(context_ref[...], grad_low))
+    load_w_first = Late(
+        w_early_hbm.at[:, pl.ds(0, first_wide)], w_ref.at[:, pl.ds(0, first_wide)], load_sems.at[9]
+    )
+    g_cross_ref[...] = lowered(contract_rows(context_cross_ref[...], grad_low))
     memory_total.middle()
     cross_total.middle()
-    normed, _ = norm_forward(stream_in_ref[...], *gain_of(norms_ref, 4))
-    grads_ref[:, in_start:] = jnp.zeros((width, grads_ref.shape[1] - in_start), jnp.bfloat16)
-    grads_ref[:, in_start : in_start + own] = lowered(contract_rows(lowered(normed), gq_ref[...]))
-    grads_ref[:, in_start + own : in_start + 3 * own] = lowered(
-        contract_rows(memory_ref[...], gkv_ref[...])
-    )
+    load_dec()
+    load_memory()
+    normed, _ = norm_forward(stream_dec_ref[...], *gain_of(norms_ref, 4))
+    gap = dec_grads_ref.shape[4] - in_start - 3 * own
+    put_grads(dec_grads_ref, in_start, contract_rows(lowered(normed), gq_ref[...]))
+    put_grads(dec_grads_ref, in_start + own, contract_rows(memory_ref[...], gkv_ref[...]))
+    put_grads(dec_grads_ref, in_start + 3 * own, jnp.zeros((width, gap), jnp.float32))
+    dec_line.begin()
     memory_total.last()
     cross_total.last()
-    grad_memory_ref[...] = memory_total.finish()
+    summed = memory_total.finish()
+    load_two()
+    grad_enc_ref[...] = norm_step(None, stream_two_ref, norms_ref, 2, summed, rows_mid_ref, 0)
+    load_place = Late(place_enc_hbm, stream_two_ref, load_sems.at[10])
     grad_ref[...] = norm_step(
-        grad_ref, stream_in_ref, norms_ref, 4, cross_total.finish(), rows_ref, 4
-    )
-    exchange.finish()
-
-
-def mid_back_kernel(
-    groups,
-    grad_memory_ref, stream_enc_ref, stream_mid_ref, pre_ref, norms_ref, w_ref,
-    grad_dec_in_ref, looked_ref, place_dec_ref, w_first_ref, out_rows_ref, qkv_ref, context_ref, logs_ref, head_in_ref,
-    grads_ref, grad_out_rows_ref, grad_enc_ref, tokens_ref, rows_ref, head_out_ref,
-    head_sems, stream_dec_ref, grad_context_ref, gqkv_ref, *total_refs,
-):
-    group, share, _, core_peer, side_peer = places()
-    meet([core_peer, side_peer] + group_peers(group, share, groups))
-    exchange = Exchange(head_in_ref, head_out_ref, head_sems, groups, 1)
-    width = stream_enc_ref.shape[1]
-    own = context_ref.shape[1]
-    hidden = pre_ref.shape[1]
-    in_start = hidden + width
-    w_start = w_first_ref.shape[1] // 3
-    dec_start = looked_ref.shape[0] - place_dec_ref.shape[0]
-    feed_total, self_total = Total(total_refs[:4]), Total(total_refs[4:])
-    rows_ref[...] = jnp.zeros_like(rows_ref)
+        grad_ref, stream_dec_ref, norms_ref, 4, cross_total.finish(), rows_dec_ref, 4
+    )
+
+    feed_total, self_total = Total(large_two), Total(small_one)
+    load_enc()
+    load_pre()
+    load_w_enc()
+    feed_grads(
+        grad_enc_ref, stream_enc_ref, pre_enc_ref, norms_ref, 1, w_enc_ref, mid_grads_ref, feed_total
+    )
+    grad_low = lowered(grad_ref[...])
+    context_ref[...] = lowered(times_transposed(grad_low, out_rows_ref[1]))
+    feed_total.last()
+    heads_backward(
+        qkv_dec_ref, qkv_dec_ref, starts, logs_dec_ref, context_ref, gqkv_ref, gqkv_ref, starts, True
+    )
+    load_w_first()
+    w_start = first_wide // 3
+    self_total.begin(times_transposed(gqkv_ref[...], w_ref[:, w_start : w_start + 3 * own]))
+    g_self_ref[...] = lowered(contract_rows(context_dec_ref[...], grad_low))
+    self_total.middle()
+    load_looked()
+    enc_len = stream_enc_ref.shape[0]
+    stream_dec_ref[...] = stream_of(looked_ref, enc_len, place_dec_ref)
+    normed, _ = norm_forward(stream_dec_ref[...], *gain_of(norms_ref, 3))
+    put_grads(mid_grads_ref, in_start, contract_rows(lowered(normed), gqkv_ref[...]))
+    put_grads(mid_grads_ref, in_start + 3 * own, jnp.zeros((width, gap), jnp.float32))
+    mid_line.begin()
     grad_enc_ref[...] = norm_step(
-        None, stream_enc_ref, norms_ref, 2, grad_memory_ref[...], rows_ref, 0
-    )
-    feed_grads(grad_enc_ref, stream_mid_ref, pre_ref, norms_ref, 1, w_ref, grads_ref, feed_total)
-    grad_low = lowered(grad_dec_in_ref[...])
-    grad_context_ref[...] = lowered(times_transposed(grad_low, out_rows_ref[1]))
-    starts = (0, own, 2 * own)
+        grad_enc_ref, stream_enc_ref, norms_ref, 1, feed_total.finish(), rows_mid_ref, 2
+    )
+    self_total.last()
+    tokens = cut_ref.shape[1]
+    part = cut_ref.shape[2]
+    grad_dec = norm_step(
+        grad_ref, stream_dec_ref, norms_ref, 3, self_total.finish(), rows_mid_ref, 4
+    )
+    grad_low = lowered(grad_dec * math.sqrt(width))
+    for index in range(groups):
+        cut_ref[index, enc_len:tokens] = grad_low[:, index * part : (index + 1) * part]
+
+    total = Total(large_one)
+    grad_low = lowered(grad_enc_ref[...])
+    context_enc_grad_ref[...] = lowered(times_transposed(grad_low, out_rows_ref[0]))
     heads_backward(
-        qkv_ref, qkv_ref, starts, logs_ref, grad_context_ref, gqkv_ref, gqkv_ref, starts, True
-    )
-    feed_total.last()
-    self_total.begin(times_transposed(gqkv_ref[...], w_first_ref[:, w_start : w_start + 3 * own]))
-    grad_out_rows_ref[...] = lowered(contract_rows(context_ref[...], grad_low))
-    self_total.middle()
-    stream_dec_ref[...] = stream_of(looked_ref, dec_start, place_dec_ref)
-    normed, _ = norm_forward(stream_dec_ref[...], *gain_of(norms_ref, 3))
-    grads_ref[:, in_start:] = jnp.zeros((width, grads_ref.shape[1] - in_start), jnp.bfloat16)
-    grads_ref[:, in_start : in_start + 3 * own] = lowered(
-        contract_rows(lowered(normed), gqkv_ref[...])
-    )
-    grad_enc_ref[...] = norm_step(
-        grad_enc_ref, stream_mid_ref, norms_ref, 1, feed_total.finish(), rows_ref, 2
-    )
-    self_total.last()
-    grad_dec = norm_step(
-        grad_dec_in_ref, stream_dec_ref, norms_ref, 3, self_total.finish(), rows_ref, 4
-    )
-    tokens_ref[...] = lowered(grad_dec * math.sqrt(width))
-    exchange.finish()
-
-
-def last_back_kernel(
-    groups, shares,
-    grad_in_ref, looked_ref, place_enc_ref, norms_ref, w_ref, out_rows_ref, qkv_ref, context_ref, logs_ref,
-    g_self_ref, g_cross_ref, rows_dec_ref, rows_mid_ref, head_in_ref,
-    grads_ref, tokens_ref, head_out_ref,
-    head_sems, stream_ref, grad_context_ref, gqkv_ref, g_rows_ref, norm_rows_ref, turned_ref, blocks_ref, rows_ref, block_sems, local_sem, *total_refs,
-):
-    group, share, _, core_peer, side_peer = places()
-    peers = share_peers(group, share, shares)
-    meet(peers + group_peers(group, share, groups))
-    exchange = Exchange(head_in_ref, head_out_ref, head_sems, groups, 2)
-    width = stream_ref.shape[1]
-    own = context_ref.shape[1]
+        qkv_enc_ref, qkv_enc_ref, starts, logs_enc_ref, context_enc_grad_ref, gqkv_enc_ref, gqkv_enc_ref, starts,
+        False,
+    )
+    total.begin(times_transposed(gqkv_enc_ref[...], w_ref[:, : 3 * own]))
+    dec_line.beside()
+    g_enc_ref[...] = lowered(contract_rows(context_enc_ref[...], grad_low))
+    total.middle()
+    load_place()
+    stream_ref[...] = stream_of(looked_ref, 0, stream_two_ref)
+    normed, _ = norm_forward(stream_ref[...], *gain_of(norms_ref, 0))
     wide = blocks_ref.shape[2]
-    total = Total(total_refs)
-    grad_low = lowered(grad_in_ref[...])
-    grad_context_ref[...] = lowered(times_transposed(grad_low, out_rows_ref[0]))
-    starts = (0, own, 2 * own)
-    heads_backward(
-        qkv_ref, qkv_ref, starts, logs_ref, grad_context_ref, gqkv_ref, gqkv_ref, starts, False
-    )
-    total.begin(times_transposed(gqkv_ref[...], w_ref[:, : 3 * own]))
-    g_rows_ref[...] = lowered(contract_rows(context_ref[...], grad_low))
-    total.middle()
-    stream_ref[...] = stream_of(looked_ref, 0, place_enc_ref)
-    normed, _ = norm_forward(stream_ref[...], *gain_of(norms_ref, 0))
-    in_wide = grads_ref.shape[1] - wide
-    grads_ref[:, :in_wide] = jnp.zeros((width, in_wide), jnp.bfloat16)
-    grads_ref[:, : 3 * own] = lowered(contract_rows(lowered(normed), gqkv_ref[...]))
+    in_wide = last_grads_ref.shape[4] - wide
+    put_grads(last_grads_ref, 0, contract_rows(lowered(normed), gqkv_enc_ref[...]))
+    put_grads(last_grads_ref, 3 * own, jnp.zeros((width, in_wide - 3 * own), jnp.float32))
     blocks_ref[...] = jnp.zeros_like(blocks_ref)
     for piece in range(shares):
         at = slice(piece * own, (piece + 1) * own)
-        for matrix, source in enumerate((g_rows_ref, g_self_ref, g_cross_ref)):
+        for matrix, source in enumerate((g_enc_ref, g_self_ref, g_cross_ref)):
             blocks_ref[piece, :, matrix * own : (matrix + 1) * own] = source[:, at]
     total.last()
-    rows_ref[...] = jnp.zeros_like(rows_ref)
-    grad_enc = norm_step(grad_in_ref, stream_ref, norms_ref, 0, total.finish(), rows_ref, 0)
-    tokens_ref[...] = lowered(grad_enc * math.sqrt(width))
+    grad_enc = norm_step(grad_enc_ref, stream_ref, norms_ref, 0, total.finish(), rows_ref, 0)
+    grad_low = lowered(grad_enc * math.sqrt(width))
+    for index in range(groups):
+        cut_ref[index, 0:enc_len] = grad_low[:, index * part : (index + 1) * part]
+    quarter = tokens // shares
+    own_rows = pl.ds(pl.multiple_of(share * quarter, 64), quarter)
+    to_groups = Exchange(
+        lambda index: cut_ref.at[index, own_rows, :], own_tokens_ref.at[share], token_sems, groups
+    )
     norm_rows_ref[...] = jnp.zeros_like(norm_rows_ref)
     order = (
         (0, rows_ref, 0),
@@ -1178,39 +1395,71 @@
         norm_rows_ref[64 + row : 65 + row, :] = source[slot : slot + 1, :]
         norm_rows_ref[71 + row : 72 + row, :] = source[slot + 1 : slot + 2, :]
     turned_ref[...] = jnp.transpose(norm_rows_ref[...])
-    own_rows = turned_ref[pl.ds(pl.multiple_of(share * own, 64), own), :]
+    own_norms = turned_ref[pl.ds(pl.multiple_of(share * own, 64), own), :]
     for piece in range(shares):
         tail = blocks_ref[piece, :, wide - 128 :].astype(jnp.float32)
-        blocks_ref[piece, :, wide - 128 :] = lowered(tail + own_rows)
-    target = grads_ref.at[pl.ds(pl.multiple_of(share * own, 64), own), pl.ds(in_wide, wide)]
-    copies = [
-        send(blocks_ref.at[peer[1]], target, block_sems.at[0, step], block_sems.at[1, step], peer)
-        for step, peer in enumerate(peers)
-    ]
-    keep = pltpu.make_async_copy(blocks_ref.at[share], target, local_sem)
+        blocks_ref[piece, :, wide - 128 :] = lowered(tail + own_norms)
+    copies = []
+    for half in range(2):
+        target = last_grads_ref.at[share // 2, lax.rem(share, 2), half, :, pl.ds(in_wide, wide)]
+        source_rows = pl.ds(half * part, part)
+        for step, peer in enumerate(peers):
+            copies.append(
+                send(
+                    blocks_ref.at[peer[1], source_rows, :],
+                    target,
+                    block_sems.at[half, 0, step],
+                    block_sems.at[half, 1, step],
+                    peer,
+                )
+            )
+        keep = pltpu.make_async_copy(
+            blocks_ref.at[share, source_rows, :], target, local_sems.at[half]
+        )
+        keep.start()
+        copies.append(keep)
+    for copy in copies:
+        copy.wait()
+    last_line.begin()
+    mid_line.beside()
+    dec_line.beyond()
+    to_groups.finish()
+    token_gather = ShareGather(own_tokens_ref, share_sems)
+    last_line.beside()
+    mid_line.beyond()
+    dec_own_ref[...] = dec_line.finish()
+    keep = pltpu.make_async_copy(dec_own_ref, dec_shares_ref.at[share], local_sems.at[2])
     keep.start()
     keep.wait()
-    for copy in copies:
-        copy.wait()
+    dec_gather = ShareGather(dec_shares_ref, dec_sems)
+    token_gather.middle()
+    last_line.beyond()
+    middle = mid_grads_ref.shape[4]
+    own_ref[:, :middle] = mid_line.finish()
+    dec_gather.middle()
+    token_gather.finish()
+    own_ref[:, middle:] = last_line.finish()
+    squares = 0.0
+    for ref in (dec_own_ref, own_ref):
+        value = ref[...].astype(jnp.float32)
+        value = value * value
+        if ref is own_ref:
+            column = lax.broadcasted_iota(jnp.int32, value.shape, 1)
+            norm_part = (column >= norm_start) & (column < norm_start + norm_count)
+            value = jnp.where(norm_part, value / shares, value)
+        squares = squares + jnp.sum(jnp.sum(value, axis=0, keepdims=True), axis=1, keepdims=True)
+    lane = lax.broadcasted_iota(jnp.int32, squares_ref.shape, 1)
+    squares_ref[...] = jnp.where(lane == 0, squares, 0.0)
+    dec_gather.finish()
     exchange.finish()
 
 
-def numbers_kernel(groups, own_ref, out_ref, sems, local_sem):
-    group, share, _, _, _ = places()
-    peers = group_peers(group, share, groups)
-    meet(peers)
-    copies = [
-        send(own_ref, out_ref.at[group], sems.at[0, step], sems.at[1, step], peer)
-        for step, peer in enumerate(peers)
-    ]
-    keep = pltpu.make_async_copy(own_ref, out_ref.at[group], local_sem)
-    keep.start()
-    keep.wait()
-    for copy in copies:
-        copy.wait()
-
-
-def look_kernel(groups, picked_ref, looked_ref, send_ref, core_ref, side_ref, group_ref, sems):
+def look_kernel(
+    groups,
+    picked_ref, across_ref,
+    looked_ref, table_ref,
+    send_ref, core_ref, side_ref, group_ref, sems, table_sems,
+):
     group, share, core, core_peer, side_peer = places()
     side = share // 2
     far = group_peers(group, share, groups)
@@ -1232,6 +1481,10 @@
     ]
     for copy in copies:
         copy.wait()
+    chunk, columns = across_ref.shape[1] // groups, table_ref.shape[2]
+    exchange = Exchange(
+        table_blocks(across_ref, chunk, 0, columns), table_ref, table_sems, groups
+    )
     for index in range(groups):
         send_ref[:, index * width : (index + 1) * width] = group_ref[index]
     at = pl.ds(pl.multiple_of(core * half + side * quarter, 16), quarter)
@@ -1241,29 +1494,20 @@
     end = end + 1
     both = looked_ref.at[mine, :]
     send(both, both, sems.at[0, end], sems.at[1, end], core_peer).wait()
+    exchange.finish()
 
 
 def squares_kernel(
-    groups, shares, norm_start, norm_count,
-    embedding_ref, one_ref, two_ref, three_ref, out_ref, share_ref, group_ref, sems,
+    groups, shares,
+    embedding_ref, dense_ref,
+    out_ref,
+    share_ref, group_ref, sems,
 ):
     group, share, _, _, _ = places()
     near, far = share_peers(group, share, shares), group_peers(group, share, groups)
     meet(near + far)
-    total = 0.0
-    for ref in (one_ref, two_ref, three_ref):
-        value = ref[...].astype(jnp.float32)
-        value = value * value
-        if ref is three_ref:
-            column = lax.broadcasted_iota(jnp.int32, value.shape, 1)
-            norm_part = (column >= norm_start) & (column < norm_start + norm_count)
-            value = jnp.where(norm_part, value / shares, value)
-        total = total + jnp.sum(value)
-    lane = lax.broadcasted_iota(jnp.int32, (8, 128), 1)
     down = lax.broadcasted_iota(jnp.int32, (8, 128), 0)
-    share_ref[share] = jnp.where((lane == 0) & (down == 0), total, 0.0) + jnp.where(
-        down == 1, embedding_ref[...], 0.0
-    )
+    share_ref[share] = jnp.where(down == 0, embedding_ref[...] + dense_ref[...], 0.0)
     copies = [
         send(share_ref.at[share], share_ref.at[share], sems.at[0, step], sems.at[1, step], peer)
         for step, peer in enumerate(near)
@@ -1286,17 +1530,118 @@
     out_ref[...] = jnp.broadcast_to(jnp.sum(summed), out_ref.shape)
 
 
-def share_of_columns(array, groups, shares, index):
-    lead, columns = array.shape[:-1], array.shape[-1]
-    cut = array.reshape(lead + (groups, shares, columns // groups // shares))
-    own = lax.dynamic_index_in_dim(cut, index, axis=len(lead) + 1, keepdims=False)
-    return own.reshape(lead + (columns // shares,))
-
-
-def whole_of_shares(shares_first, groups):
-    shares, rows, columns = shares_first.shape
-    cut = shares_first.reshape(shares, rows, groups, columns // groups)
-    return cut.transpose(1, 2, 0, 3).reshape(rows, shares * columns)
+def dense_kernel(
+    rate, place_grads, factor_ref, *refs
+):
+    *grad_refs, w_ref, first_ref, second_ref, new_w_ref, new_first_ref, new_second_ref, wide_ref = refs
+    place_grads(wide_ref, *grad_refs)
+    updated = adam_update(
+        w_ref[0],
+        first_ref[0],
+        second_ref[0],
+        wide_ref[...].astype(jnp.float32),
+        factor_ref[0],
+        rate,
+    )
+    for out, value in zip((new_w_ref, new_first_ref, new_second_ref), updated):
+        out[0] = value
+
+
+def dense_update(name, rate, place_grads, factor, grads, w, first, second, parts):
+    matrices, rows, columns = w.shape
+    rows = rows // parts
+    own = pl.BlockSpec((1, rows, columns), lambda matrix, part: (matrix, part, 0))
+    shares, width = grads[0].shape[:2]
+    grad_specs = [
+        pl.BlockSpec((shares, width, member.shape[2]), lambda matrix, part: (0, 0, 0))
+        for member in grads
+    ]
+    return pl.pallas_call(
+        partial(dense_kernel, rate, place_grads),
+        grid=(matrices, parts),
+        out_shape=[jax.ShapeDtypeStruct(w.shape, w.dtype)] * 3,
+        in_specs=[pl.BlockSpec(memory_space=pltpu.SMEM)] + grad_specs + [own] * 3,
+        out_specs=[own] * 3,
+        scratch_shapes=[pltpu.VMEM((rows, columns), jnp.bfloat16)],
+        compiler_params=pltpu.CompilerParams(vmem_limit_bytes=VMEM_BYTES),
+        name=name,
+    )(factor, *grads, w, first, second)
+
+
+def place_columns(groups, matrix, source_ref, start):
+    def place(wide_ref):
+        @pl.when(pl.program_id(0) == matrix)
+        def _():
+            rows, columns = wide_ref.shape
+            shares = source_ref.shape[0]
+            piece = columns // groups // shares
+            at = pl.ds(pl.multiple_of(pl.program_id(1) * rows, 16), rows)
+            for number in range(groups):
+                for share in range(shares):
+                    low = (number * shares + share) * piece
+                    wide_ref[:, low : low + piece] = source_ref[
+                        share, at, start + number * piece : start + (number + 1) * piece
+                    ]
+
+    return place
+
+
+def prepare_kernel(
+    groups, shares, gap,
+    numbers_ref, hits_ref, in_ref, out_ref, up_ref, down_ref, norms_ref,
+    all_numbers_ref, all_hits_ref, early_ref, dec_ref,
+    square_ref, sems, local_sems,
+):
+    group, share, _, _, _ = places()
+    peers = group_peers(group, share, groups)
+    meet(peers)
+    copies = []
+    for number, (source, target) in enumerate(
+        ((numbers_ref, all_numbers_ref), (hits_ref, all_hits_ref))
+    ):
+        copies += [
+            send(source, target.at[group], sems.at[number, 0, step], sems.at[number, 1, step], peer)
+            for step, peer in enumerate(peers)
+        ]
+        keep = pltpu.make_async_copy(source, target.at[group], local_sems.at[number])
+        keep.start()
+        copies.append(keep)
+    width, model_width = in_ref.shape[1], out_ref.shape[2]
+    own = model_width // shares
+    piece = up_ref.shape[2] // groups // shares
+    hidden = groups * piece
+    early_ref[...] = jnp.zeros_like(early_ref)
+    dec_ref[...] = jnp.zeros_like(dec_ref)
+
+    def put(index):
+        def columns(target, start, source, groups_in, size):
+            step = shares * size
+            for number in range(groups_in):
+                low = number * step + index * size
+                target[:, start + number * size : start + (number + 1) * size] = lowered(
+                    source[:, low : low + size]
+                )
+
+        in_wide = 3 * own + gap
+        columns(early_ref, 0, in_ref.at[0], 3, own)
+        columns(early_ref, in_wide, in_ref.at[1], 3, own)
+        for matrix in range(3):
+            columns(early_ref, 2 * in_wide + matrix * own, out_ref.at[matrix], 1, own)
+        rows = slice(index * (down_ref.shape[1] // shares), (index + 1) * (down_ref.shape[1] // shares))
+        for matrix, (target, start) in enumerate(((early_ref, 3 * in_wide), (dec_ref, 0))):
+            columns(target, start, up_ref.at[matrix], groups, piece)
+            start = start + hidden
+            target[:, start : start + model_width] = lowered(down_ref[matrix, rows, :])
+        columns(dec_ref, hidden + model_width, in_ref.at[2], 3, own)
+
+    for index in range(shares):
+        pl.when(share == index)(partial(put, index))
+    square_ref[...] = jnp.zeros_like(square_ref)
+    square_ref[0 : norms_ref.shape[0], 0:width] = norms_ref[...]
+    end = 3 * (3 * own + gap)
+    early_ref[:, end - gap : end] = lowered(jnp.transpose(square_ref[...])[0:width, 0:gap])
+    for copy in copies:
+        copy.wait()
 
 
 def local(
@@ -1342,78 +1687,72 @@
     number_count = numbers.shape[1]
     number_lanes = -(-number_count // 1024) * 128
     numbers = jnp.pad(numbers, ((0, 0), (0, 8 * number_lanes - number_count)))
-    (numbers,) = call(
-        partial(numbers_kernel, groups),
-        "numbers",
+    span = 1 << tokens.bit_length()
+    own_tokens = jnp.concatenate([enc_ids[0], jnp.zeros((1,), jnp.int32), labels[0, :-1]])
+    hits = list_hits(own_tokens - row_start, shard_rows, span)
+    own = model_width // shares
+    own_in, own_up = 3 * own, ffn_up.shape[2] // shares
+    norm_rows = norms.shape[0]
+    gap = -own_in % 128
+    in_wide = own_in + gap
+    dec_wide = own_up + model_width + in_wide
+    first_wide = 3 * in_wide
+    early_wide = first_wide + own_up + model_width
+    chunk = -(-shard_rows // (groups * 3072)) * 3072
+    table_cuts = (chunk // 8, chunk // 3, chunk // 6, 3 * chunk // 8)
+    table_starts = np.cumsum((0,) + table_cuts).tolist()
+    numbers, hits, mine_early, mine_dec = call(
+        partial(prepare_kernel, groups, shares, gap),
+        "prepare",
         1,
-        [numbers.reshape(8, number_lanes)],
-        [shape_of((groups, 8, number_lanes), jnp.int32)],
-        [sems((2, groups - 1)), sems],
+        [
+            numbers.reshape(8, number_lanes), hits.reshape(8, span // 8),
+            attn_in, attn_out, ffn_up, ffn_down, norms,
+        ],
+        [
+            shape_of((groups, 8, number_lanes), jnp.int32),
+            shape_of((groups, 8, span // 8), jnp.int32),
+            shape_of((part_width, early_wide), bf16),
+            shape_of((part_width, dec_wide), bf16),
+        ],
+        [pltpu.VMEM((128, 128), f32), sems((2, 2, groups - 1)), sems((2,))],
         0,
     )
+    hits = hits.reshape(groups, span)
+    w_early = lax.all_gather(mine_early, "dp", axis=0, tiled=True)
+    w_dec = lax.all_gather(mine_dec, "dp", axis=0, tiled=True)
     numbers = numbers.reshape(groups, 8 * number_lanes)
-    all_enc = numbers[:, :enc_len]
     all_labels = numbers[:, enc_len:tokens]
     all_positions = numbers[:, tokens : tokens + loss_count]
     all_lengths = numbers[:, tokens + loss_count : number_count]
-    all_tokens = jnp.concatenate(
-        [all_enc, jnp.zeros((groups, 1), jnp.int32), all_labels[:, :-1]], axis=1
-    )
-    all_targets = jnp.take_along_axis(all_labels, all_positions, axis=1).reshape(-1)
+    at_place = all_positions[:, :, None] == jnp.arange(dec_len)
+    all_targets = jnp.sum(jnp.where(at_place, all_labels[:, None, :], 0), axis=2).reshape(-1)
     all_counted = (all_positions < all_lengths).reshape(-1).astype(f32)
     token_count = jnp.sum(all_counted)
 
-    local_ids = all_tokens.reshape(-1) - row_start
-    picked, hit_list, hit_count = pick_rows(local_ids, embedding)
-    (looked,) = call(
+    picked, across = pick_rows(hits, groups * tokens, embedding.T, groups * chunk)
+    looked, table_zero = call(
         partial(look_kernel, groups),
         "look",
         2,
-        [picked.reshape(groups, tokens, part_width)],
-        [shape_of((tokens, model_width), bf16)],
+        [picked.reshape(groups, tokens, part_width), across],
+        [
+            shape_of((tokens, model_width), bf16),
+            shape_of((groups, part_width, table_cuts[0]), bf16),
+        ],
         [
             pltpu.VMEM((tokens // 4, model_width), bf16),
             pltpu.VMEM((groups, tokens // 2, part_width), bf16),
             pltpu.VMEM((groups, tokens // 4, part_width), bf16),
             pltpu.VMEM((groups, tokens // 4, part_width), bf16),
             sems((2, groups + 3)),
+            sems((2, groups)),
         ],
         0,
-    )
-
-    mine_in = share_of_columns(lowered(attn_in), 3, shares, share)
-    mine_out = share_of_columns(lowered(attn_out), 1, shares, share)
-    mine_up = share_of_columns(lowered(ffn_up), groups, shares, share)
-    down_rows = ffn_down.shape[1] // shares
-    mine_down = lax.dynamic_slice_in_dim(ffn_down, share * down_rows, down_rows, axis=1)
-    mine_down = lowered(mine_down)
-    norm_rows = norms.shape[0]
-    own_in, own, own_up = mine_in.shape[2], mine_out.shape[2], mine_up.shape[2]
-    gap = -own_in % 128
-
-    def wider(array, columns):
-        return jnp.pad(array, ((0, 0), (0, columns)))
-
-    mine_first = jnp.concatenate(
-        [wider(mine_in[0], gap), wider(mine_in[1], gap), mine_out[0], mine_out[1], mine_out[2]]
-        + [wider(lowered(norms).T, gap - norm_rows)],
-        axis=1,
-    )
-    mine_enc = jnp.concatenate([mine_up[0], mine_down[0]], axis=1)
-    mine_dec = jnp.concatenate([mine_up[1], mine_down[1], wider(mine_in[2], gap)], axis=1)
-    mine_first, mine_enc, mine_dec, _ = lax.optimization_barrier(
-        (mine_first, mine_enc, mine_dec, all_lengths)
-    )
-    w_first = lax.all_gather(mine_first, "dp", axis=0, tiled=True)
-    w_enc = lax.all_gather(mine_enc, "dp", axis=0, tiled=True)
-    w_dec = lax.all_gather(mine_dec, "dp", axis=0, tiled=True)
-    in_wide = own_in + gap
-
-    chunk = -(-shard_rows // (groups * 512)) * 512
-    across = jnp.pad(lowered(embedding.T), ((0, 0), (0, groups * chunk - shard_rows)))
-    across = across.reshape(part_width, groups, chunk).transpose(1, 0, 2)
-    across, looked = lax.optimization_barrier((across, looked))
-    table = lax.all_to_all(across, "dp", 0, 0).reshape(model_width, chunk)
+        (1,),
+        (1,),
+    )
+
 
     place_enc = positions_numpy(enc_len, model_width)
     place_dec = positions_numpy(dec_len, model_width)
@@ -1422,12 +1761,12 @@
     (
         qkv_enc, context_enc, logs_enc, stream_enc,
         qkv_dec, context_dec, logs_dec, stream_dec,
-        out_rows, norm_values,
+        out_rows, norm_values, table_one,
     ) = call(
-        partial(first_kernel, shares),
+        partial(first_kernel, groups, shares, table_starts[1], first_wide),
         "first",
         3,
-        [looked, place_enc, place_dec, w_first],
+        [looked, place_enc, place_dec, w_early, across],
         [
             shape_of((enc_len, 3 * own), bf16),
             shape_of((enc_len, own), bf16),
@@ -1439,8 +1778,10 @@
             shape_of((dec_len, model_width), f32),
             shape_of((3, own, model_width), bf16),
             shape_of((16, model_width), f32),
+            shape_of((groups, part_width, table_cuts[1]), bf16),
         ],
         [
+            sems((2, groups)),
             pltpu.VMEM((shares, own, in_wide), bf16),
             sems((2, shares - 1)),
             sems,
@@ -1448,27 +1789,33 @@
         + total_enc
         + total_dec,
         8 * (enc_macs + dec_macs) * own,
-    )
-    pre_enc, stream_two, memory = call(
-        enc_feed_kernel,
+        (4,),
+        (10,),
+    )
+    pre_enc, stream_two, memory, table_two = call(
+        partial(enc_feed_kernel, groups, table_starts[2], first_wide),
         "enc_feed",
         4,
-        [stream_enc, norm_values, w_enc],
+        [stream_enc, norm_values, w_early, across],
         [
             shape_of((enc_len, own_up), f32),
             shape_of((enc_len, model_width), f32),
             shape_of((enc_len, model_width), bf16),
+            shape_of((groups, part_width, table_cuts[2]), bf16),
         ],
-        total_enc,
+        [sems((2, groups)), pltpu.VMEM((model_width, own_up + model_width), bf16), sems] + total_enc,
         4 * enc_macs * own_up,
+        (2, 3),
+        (3,),
     )
     (
-        q_cross, kv_cross, context_cross, logs_cross, stream_mid, pre_dec, stream_out, selected
+        q_cross, kv_cross, context_cross, logs_cross, stream_mid, pre_dec, stream_out, selected,
+        table_three,
     ) = call(
-        partial(dec_kernel, groups),
+        partial(dec_kernel, groups, table_starts[3]),
         "dec",
         5,
-        [stream_dec, memory, norm_values, w_dec, out_rows, loss_positions.reshape(-1, 1)],
+        [stream_dec, memory, norm_values, w_dec, out_rows, loss_positions.reshape(-1, 1), across],
         [
             shape_of((dec_len, own), bf16),
             shape_of((enc_len, 2 * own), bf16),
@@ -1478,9 +1825,18 @@
             shape_of((dec_len, own_up), f32),
             shape_of((dec_len, model_width), f32),
             shape_of((groups, loss_count, model_width), bf16),
+            shape_of((groups, part_width, table_cuts[3]), bf16),
         ],
-        [pltpu.VMEM((loss_count, model_width), bf16), sems((2, groups - 1))] + total_dec + total_dec,
+        [
+            pltpu.VMEM((loss_count, model_width), bf16),
+            sems((2, groups - 1)),
+            sems((2, groups)),
+        ]
+        + total_dec
+        + total_dec,
         4 * dec_macs * own_up + 8 * enc_macs * own,
+        (6,),
+        (8,),
     )
 
     rows_all = groups * loss_count
@@ -1494,7 +1850,10 @@
         6,
         [
             selected.reshape(rows_all, model_width),
-            table,
+            table_zero.reshape(model_width, -1),
+            table_one.reshape(model_width, -1),
+            table_two.reshape(model_width, -1),
+            table_three.reshape(model_width, -1),
             targets,
             (all_counted / token_count)[:, None],
             all_counted[None, :],
@@ -1523,115 +1882,91 @@
     )
     loss_sum = loss[0, 0]
     head_grad = head_grad.reshape(groups, part_width, chunk)
-    pieces = chunk // 3
-
-    dec_grads, g_out_cross, grad_dec, grad_memory, rows_dec, head_zero = call(
-        partial(dec_back_kernel, groups),
-        "dec_back",
+    late_wide = dec_wide + 2 * in_wide
+    norm_start = dec_wide + in_wide + own_in
+    quarter = tokens // shares
+    block_shape = (2, 2, 2, part_width)
+    back_inputs = [
+        grad_selected, loss_positions.reshape(1, -1), stream_out, stream_mid, pre_dec, norm_values, w_dec,
+        out_rows, memory, stream_dec, q_cross, kv_cross, context_cross, logs_cross,
+        stream_two, stream_enc, pre_enc, w_early, looked, place_enc, place_dec,
+        qkv_dec, context_dec, logs_dec, qkv_enc, context_enc, logs_enc,
+        head_grad,
+    ]
+
+    head_grad, grad_tokens, dec_shares, late_own, dense_squares = call(
+        partial(
+            back_kernel, groups, shares, first_wide, norm_start, norm_rows, len(back_inputs), 5
+        ),
+        "backward",
         7,
+        back_inputs,
         [
-            grad_selected, loss_positions.reshape(1, -1), stream_dec, stream_mid, stream_out, pre_dec,
-            memory, norm_values, w_dec, out_rows, q_cross, kv_cross, context_cross, logs_cross,
-            head_grad,
-        ],
-        [
-            shape_of((model_width, own_up + model_width + in_wide), bf16),
-            shape_of((own, model_width), bf16),
-            shape_of((dec_len, model_width), f32),
-            shape_of((enc_len, model_width), f32),
-            shape_of((8, model_width), f32),
-            shape_of((groups, part_width, pieces), bf16),
+            shape_of((groups, part_width, chunk), bf16),
+            shape_of((shares, groups, quarter, part_width), bf16),
+            shape_of((shares, part_width, dec_wide), bf16),
+            shape_of((part_width, late_wide), bf16),
+            shape_of((1, 128), f32),
         ],
         [
             sems((2, groups)),
+            sems((11,)),
+            pltpu.VMEM((model_width, dec_wide), bf16),
+            pltpu.VMEM((model_width, own_up + model_width), bf16),
+            pltpu.VMEM(out_rows.shape, bf16),
+            pltpu.VMEM((enc_len, model_width), bf16),
+            pltpu.VMEM((dec_len, model_width), f32),
+            pltpu.VMEM((enc_len, model_width), f32),
+            pltpu.VMEM((enc_len, model_width), f32),
+            pltpu.VMEM((enc_len, own_up), f32),
+            pltpu.VMEM((tokens, model_width), bf16),
+            pltpu.VMEM(block_shape + (dec_wide,), bf16),
+            pltpu.VMEM(block_shape + (dec_wide,), bf16),
+            pltpu.VMEM(block_shape + (2 * in_wide,), bf16),
+            pltpu.VMEM((dec_len, model_width), f32),
+            pltpu.VMEM((enc_len, model_width), f32),
             pltpu.VMEM((dec_len, own), bf16),
             pltpu.VMEM((dec_len, own), bf16),
             pltpu.VMEM((enc_len, 2 * own), bf16),
-        ]
-        + total_dec
-        + total_dec
-        + total_enc,
-        8 * dec_macs * own_up + 16 * enc_macs * own,
-        (14,),
-        (5,),
-    )
-    dec_own = lax.psum_scatter(dec_grads, "dp", scatter_dimension=0, tiled=True)
-    mid_grads, g_out_self, grad_enc, tokens_dec, rows_mid, head_one = call(
-        partial(mid_back_kernel, groups),
-        "mid_back",
-        8,
-        [
-            grad_memory, stream_two, stream_enc, pre_enc, norm_values, w_enc,
-            grad_dec, looked, place_dec, w_first, out_rows, qkv_dec, context_dec, logs_dec,
-            head_grad,
-        ],
-        [
-            shape_of((model_width, own_up + model_width + in_wide), bf16),
-            shape_of((own, model_width), bf16),
-            shape_of((enc_len, model_width), f32),
-            shape_of((dec_len, model_width), bf16),
-            shape_of((8, model_width), f32),
-            shape_of((groups, part_width, pieces), bf16),
-        ],
-        [
-            sems((2, groups)),
-            pltpu.VMEM((dec_len, model_width), f32),
-            pltpu.VMEM((dec_len, own), bf16),
             pltpu.VMEM((dec_len, 3 * own), bf16),
-        ]
-        + total_enc
-        + total_dec,
-        8 * enc_macs * own_up + 16 * dec_macs * own,
-        (14,),
-        (5,),
-    )
-    mid_own = lax.psum_scatter(mid_grads, "dp", scatter_dimension=0, tiled=True)
-    last_grads, tokens_enc, head_two = call(
-        partial(last_back_kernel, groups, shares),
-        "last_back",
-        9,
-        [
-            grad_enc, looked, place_enc, norm_values, w_first, out_rows, qkv_enc, context_enc, logs_enc,
-            g_out_self, g_out_cross, rows_dec, rows_mid, head_grad,
-        ],
-        [
-            shape_of((model_width, 2 * in_wide), bf16),
-            shape_of((enc_len, model_width), bf16),
-            shape_of((groups, part_width, pieces), bf16),
-        ],
-        [
-            sems((2, groups)),
-            pltpu.VMEM((enc_len, model_width), f32),
+            pltpu.VMEM((enc_len, 3 * own), bf16),
             pltpu.VMEM((enc_len, own), bf16),
-            pltpu.VMEM((enc_len, 3 * own), bf16),
             pltpu.VMEM((own, model_width), bf16),
+            pltpu.VMEM((own, model_width), bf16),
+            pltpu.VMEM((own, model_width), bf16),
+            pltpu.VMEM((8, model_width), f32),
+            pltpu.VMEM((8, model_width), f32),
+            pltpu.VMEM((8, model_width), f32),
             pltpu.VMEM((128, model_width), f32),
             pltpu.VMEM((model_width, 128), f32),
             pltpu.VMEM((shares, own, in_wide), bf16),
-            pltpu.VMEM((8, model_width), f32),
-            sems((2, shares - 1)),
-            sems,
-        ]
-        + total_enc,
-        16 * enc_macs * own,
-        (13,),
-        (2,),
-    )
-    last_own = lax.psum_scatter(last_grads, "dp", scatter_dimension=0, tiled=True)
-
-    grad_tokens = jnp.concatenate([tokens_enc, tokens_dec], axis=0)
-    grad_tokens = grad_tokens.reshape(tokens, groups, part_width).transpose(1, 0, 2)
-    grad_tokens = lax.all_to_all(grad_tokens, "dp", 0, 0).reshape(groups * tokens, part_width)
-    g_embedding, embedding_squares = spread_rows(
-        local_ids, hit_list, hit_count, grad_tokens, (head_zero, head_one, head_two)
-    )
+            sems((2, 2, shares - 1)),
+            pltpu.VMEM((groups, tokens, part_width), bf16),
+            sems((2, groups)),
+            sems((2, 3)),
+            sems((2, 3)),
+            pltpu.VMEM((part_width, dec_wide), bf16),
+            sems((3,)),
+            *total_dec,
+            *total_enc,
+            *total_dec[1:],
+            *total_enc[1:],
+            *line_scratch(part_width, dec_wide),
+            *line_scratch(part_width, dec_wide),
+            *line_scratch(part_width, 2 * in_wide),
+        ],
+        16 * (enc_macs + dec_macs) * own_up,
+        (6, 7, 8, 9, 14, 15, 16, 17, 18, 19, 27),
+        (0, 1, 2),
+    )
+    late_shares = lax.all_gather(late_own, "vocab", axis=0, tiled=False)
+    g_embedding, embedding_squares = spread_rows(hits, grad_tokens, head_grad)
     g_embedding = g_embedding[:, :shard_rows].T
-    norm_start = in_wide + own_in
     (squares,) = call(
-        partial(squares_kernel, groups, shares, norm_start, norm_rows),
+        partial(squares_kernel, groups, shares),
         "squares",
         10,
-        [embedding_squares, dec_own, mid_own, last_own],
+        [embedding_squares, dense_squares],
         [shape_of((1, 128), f32)],
         [
             pltpu.VMEM((shares, 8, 128), f32),
@@ -1642,55 +1977,55 @@
     )
     grad_norm = jnp.sqrt(squares[0, 0])
     factor = jnp.minimum(1.0, CLIP / (grad_norm + 1e-06))
-    dec_shares = lax.all_gather(dec_own, "vocab", axis=0, tiled=False)
-    mid_shares = lax.all_gather(mid_own, "vocab", axis=0, tiled=False)
-    last_shares = lax.all_gather(last_own, "vocab", axis=0, tiled=False)
-
-    def shares_cut(array, *sizes):
-        edges = np.cumsum((0,) + sizes)
-        return [array[:, :, low:high].astype(f32) for low, high in zip(edges[:-1], edges[1:])]
-
-    s_up_dec, s_down_dec, s_in_cross = shares_cut(dec_shares, own_up, model_width, own_in)
-    s_up_enc, s_down_enc, s_in_self = shares_cut(mid_shares, own_up, model_width, own_in)
-    s_in_enc, _, s_out_enc, s_out_self, s_out_cross = shares_cut(
-        last_shares, own_in, gap, own, own, own
-    )
-    gradients = (
-        g_embedding,
-        jnp.stack([whole_of_shares(member, 3) for member in (s_in_enc, s_in_self, s_in_cross)]),
-        jnp.stack([whole_of_shares(member, 1) for member in (s_out_enc, s_out_self, s_out_cross)]),
-        jnp.stack([whole_of_shares(member, groups) for member in (s_up_enc, s_up_dec)]),
-        jnp.stack([member.reshape(-1, model_width) for member in (s_down_enc, s_down_dec)]),
-        last_own[:, norm_start : norm_start + norm_rows].astype(f32).T,
-    )
-    params = (embedding, attn_in, attn_out, ffn_up, ffn_down, norms)
-    firsts = (
-        embedding_first,
-        attn_in_first,
-        attn_out_first,
-        ffn_up_first,
-        ffn_down_first,
-        norms_first,
-    )
-    seconds = (
-        embedding_second,
-        attn_in_second,
-        attn_out_second,
-        ffn_up_second,
-        ffn_down_second,
-        norms_second,
-    )
-    updated = [
-        adam_update(params[slot], firsts[slot], seconds[slot], gradients[slot], factor, RATES[slot])
-        for slot in range(6)
-    ]
+    grad_pair = [late_shares, dec_shares]
+    in_start, late_in, late_out = own_up + model_width, dec_wide, dec_wide + in_wide
+
+    def place_in(wide_ref, late_ref, dec_ref):
+        place_columns(3, 0, late_ref, late_in)(wide_ref)
+        place_columns(3, 1, late_ref, in_start)(wide_ref)
+        place_columns(3, 2, dec_ref, in_start)(wide_ref)
+
+    def place_out(wide_ref, late_ref):
+        for matrix in range(3):
+            place_columns(1, matrix, late_ref, late_out + matrix * own)(wide_ref)
+
+    def place_up(wide_ref, late_ref, dec_ref):
+        place_columns(groups, 0, late_ref, 0)(wide_ref)
+        place_columns(groups, 1, dec_ref, 0)(wide_ref)
+
+    def place_down(wide_ref, late_ref, dec_ref):
+        for matrix, ref in enumerate((late_ref, dec_ref)):
+
+            @pl.when(pl.program_id(0) == matrix)
+            def _(ref=ref):
+                wide_ref[...] = ref[pl.program_id(1), :, own_up : own_up + model_width]
+
+    scale = factor.reshape(1)
+    new_in = dense_update(
+        "adam_in", RATES[1], place_in, scale, grad_pair, attn_in, attn_in_first, attn_in_second, 2
+    )
+    new_out = dense_update(
+        "adam_out", RATES[2], place_out, scale, grad_pair[:1], attn_out, attn_out_first, attn_out_second, 1
+    )
+    new_up = dense_update(
+        "adam_up", RATES[3], place_up, scale, grad_pair, ffn_up, ffn_up_first, ffn_up_second, 2
+    )
+    new_down = dense_update(
+        "adam_down", RATES[4], place_down, scale, grad_pair, ffn_down, ffn_down_first, ffn_down_second, shares
+    )
+    g_norms = late_own[:, norm_start : norm_start + norm_rows].astype(f32).T
+    new_embedding = adam_update(
+        embedding, embedding_first, embedding_second, g_embedding, factor, RATES[0]
+    )
+    new_norms = adam_update(norms, norms_first, norms_second, g_norms, factor, RATES[5])
+    updated = (new_embedding, new_in, new_out, new_up, new_down, new_norms)
     return (loss_sum, token_count, grad_norm) + tuple(
         updated[slot][kind] for kind in range(3) for slot in range(6)
     )
 
 
 def splits_evenly(mesh):
-    return HEADS % mesh.shape["vocab"] == 0
+    return HEADS % mesh.shape["vocab"] == 0 and mesh.shape["dp"] == 8
 
 
 def solution(mesh):

time: 833 us -> 666 us (0.80)
  Pallas kernels: 430 us -> 578 us
  waiting for transfers between devices: 169 us -> 25.1 us
  local copies, waits for them, and re-layouts: 99.5 us -> 7.86 us
  starting transfers between devices: 35 us -> 0.12 us
  other arithmetic: 60.2 us -> 29.4 us
  blocking collectives: 10 us -> 0 us
    pallas_call x10 -> x8, Pallas kernels: 373 us -> 477 us  [call(): pl.pallas_call(kernel, out_shape=tuple(out_shape), in_specs=in_vmem(len(i...]
    reduce_scatter x3 -> x0, waiting for transfers between devices: 63.6 us -> none  [the longest x1 57.4 us: local(): mid_own = lax.psum_scatter(mid_grads, 'dp', scatter_dimension=0, tiled=True)]
    all_gather x1, waiting for transfers between devices: 64.6 us -> 12.5 us  [local(): w_dec = lax.all_gather(mine_dec, 'dp', axis=0, tiled=True)]
    all_to_all x2 -> x0, waiting for transfers between devices: 37.7 us -> none  [the longest x1 37.7 us: local(): lax.all_to_all(grad_tokens, 'dp', 0, 0).reshape(groups * tokens, part_width)]
    pallas_call x0 -> x5, Pallas kernels: none -> 37.2 us  [the longest x4 33.3 us: dense_update(): pl.pallas_call(partial(dense_kernel, rate, place_grads), grid=(matrices,...]
    all_to_all x2 -> x0, starting transfers between devices: 34.7 us -> none  [the longest x1 22.6 us: local(): lax.all_to_all(grad_tokens, 'dp', 0, 0).reshape(groups * tokens, part_width)]
    unnamed x73 -> x16, local copies, waits for them, and re-layouts: 25.4 us -> 4.3 us
    sub x6 -> x2, other arithmetic: 44.4 us -> 25.5 us  [adam_update(): return (weight - rate * (corrected + DECAY * weight), new_first, new_second)]
  transfers between devices with their start and end apart: 10 -> 3, of which waited for: 4 -> 2; matrix products, arithmetic and copies ran while one was open for 11% -> 5% of each run, Pallas kernels for 41% -> 27%
where the time goes in v2:
time: 666 us; the launch traced here: 659 us
  Pallas kernels  578 us (87%)
  other arithmetic  29.4 us (4%)
  waiting for transfers between devices  25.1 us (4%)
  between operations  18.6 us (3%)
  local copies, waits for them, and re-layouts  7.86 us (1%)
    pallas_call x8, Pallas kernels, call(): pl.pallas_call(kernel, out_shape=tuple(out_shape), in_specs=in_vmem(len(i...  477 us
    pallas_call x4, Pallas kernels, dense_update(): pl.pallas_call(partial(dense_kernel, rate, place_grads), grid=(matrices,...  33.3 us
    pallas_call x1, Pallas kernels, spread_rows(): pl.pallas_call(spread_kernel, out_shape=(jax.ShapeDtypeStruct((width, chu...  33 us
    pallas_call x1, Pallas kernels, pick_rows(): pl.pallas_call(pick_kernel, out_shape=(jax.ShapeDtypeStruct((count, width...  30.6 us
    sub x2, other arithmetic, adam_update(): return (weight - rate * (corrected + DECAY * weight), new_first, new_second)  25.5 us
  transfers between devices with their start and end apart: 3, of which 2 were waited for; matrix products, arithmetic and copies ran while one was open for 5% of the time, Pallas kernels for 27%

profile of v2, /device:TPU:0, one launch (start us, length us, event | category | flops | bytes accessed | tf_op | source)
XLA Modules:
  0.0 658.9 jit_solution(16544270791468145755)
XLA Ops:
  7.2 0.0 copy-start.3
  7.2 0.0 copy-start
  7.2 0.0 copy-start.1
  7.2 0.0 copy-start.2
  7.2 0.0 all-gather.5.cloned.1.call-start
  7.9 1.4 add_subtract_fusion.ids_ref
  9.3 3.9 list_hits.1
  13.2 0.8 pad_add_fusion
  14.0 0.6 pad.4
  14.6 13.5 %prepare.1 = (s32[8,8,128]{2,1,0:T(8,128)}, s32[8,8,128]{2,1,0:T(8,128)}, bf16[96,3456]{1,0:T(8,128)(2,1)}, bf16[96,2176]{1,0:T(8,128)(2,1)}) custom-call(s32[8,128]{1,0:T(8,128)} %bitcast.60, s32[8,128]{1,0:T(8,128)} %bitcast.59, f32[3,96,2304]{2,1,0:T(8,128)} %refs_2_.4, f32[3,96,768]{2,1,0:T(8,128)} %refs_1_.3, f32[2,96,3072]{2,1,0:T(8,128)} %refs_2_.6, ...), custom_call_target="tpu_custom_call" | custom-call | bytes 9417984 | tf_op jit(solution)/shard_map/prepare/pallas_call | solution.py:795
  28.1 0.0 all-gather.5.cloned.1.call-update
  28.1 0.0 all-gather.7.cloned.1.call-start
  28.2 0.7 all-gather.7.cloned.1.call-update
  28.9 0.0 all-gather.9.cloned.1.call-start
  28.9 0.8 copy.119
  29.7 0.0 copy-done
  29.7 0.1 copy.111
  29.9 1.4 copy.120
  31.2 0.0 copy-done.3
  31.2 0.7 copy.102.positions_ref
  31.9 0.3 select_reduce_fusion
  32.3 0.2 sub.39
  32.5 0.2 slice_reduce_fusion
  32.7 0.1 fusion.8
  32.8 0.6 convert_reduce_fusion
  34.1 0.9 div.55.weights_ref
  35.0 0.7 reshape.148.counted_ref
  35.6 0.1 copy.110
  35.7 0.0 copy-done.1
  35.7 0.1 copy.108
  35.8 0.0 copy-done.2
  35.9 0.1 copy.109
  36.0 30.6 %pick_rows.1 = (bf16[6144,96]{1,0:T(8,128)(2,1)}, bf16[96,24576]{1,0:T(8,128)(2,1)}) custom-call(s32[8,1024]{1,0:T(8,128)} %bitcast.51, f32[96,24026]{1,0:T(8,128)} %bitcast.48), custom_call_target="tpu_custom_call" | custom-call | tf_op jit(solution)/shard_map/pick_rows/pallas_call | solution.py:488
  66.5 55.6 %look.1 = (bf16[768,768]{1,0:T(8,128)(2,1)}, bf16[8,96,384]{2,1,0:T(8,128)(2,1)}) custom-call(bf16[8,768,96]{2,1,0:T(8,128)(2,1)} %bitcast.50, bf16[96,24576]{1,0:T(8,128)(2,1)} %get-tuple-element.77.across_ref), custom_call_target="tpu_custom_call" | custom-call | bytes 7667712 | tf_op jit(solution)/shard_map/look/pallas_call | solution.py:795
  122.2 0.7 and_select_fusion.targets_ref
  122.9 11.9 %all-gather.5.cloned.1.call-done.w_ref.w_early_ref.refs_17_ = bf16[768,3456]{1,0:T(8,128)(2,1)} async-done(((bf16[96,3456]{1,0:T(8,128)(2,1)}), bf16[768,3456]{1,0:T(8,128)(2,1)}) %all-gather.5.cloned.1.call-update) | async-done | bytes 5308432 | tf_op jit(solution)/shard_map/all_gather | solution.py:1722
  134.8 48.1 %first.1 = (bf16[512,576]{1,0:T(8,128)(2,1)}, bf16[512,192]{1,0:T(8,128)(2,1)}, f32[512,128]{1,0:T(8,128)}, f32[512,768]{1,0:T(8,128)}, bf16[256,576]{1,0:T(8,12...) custom-call(bf16[768,768]{1,0:T(8,128)(2,1)} %get-tuple-element.78.l, ...), custom_call_target="tpu_custom_call" | custom-call | flops 905969664 | bytes 20004864 | tf_op jit(solution)/shard_map/first/pallas_call | solution.py:795
  182.9 41.7 %enc_feed.1 = (f32[512,768]{1,0:T(8,128)}, f32[512,768]{1,0:T(8,128)}, bf16[512,768]{1,0:T(8,128)(2,1)}, bf16[8,96,512]{2,1,0:T(8,128)(2,1)}) custom-call(f32[512,768]{1,0:T(8,128)} %get-tuple-element.81.stream_in_ref.refs_15_, f32[16,768]{1,0:T(8,128)} %get-tuple-element.82.norms_ref.refs_5_, ...), custom_call_target="tpu_custom_call" | custom-call | flops 1207959552 | bytes 16367616 | tf_op jit(solution)/shard_map/enc_feed/pallas_call | solution.py:795
  224.6 12.5 %all-gather.7.cloned.1.call-done.w_ref.refs_6_ = bf16[768,2176]{1,0:T(8,128)(2,1)} async-done(((bf16[96,2176]{1,0:T(8,128)(2,1)}), bf16[768,2176]{1,0:T(8,128)(2,1)}) %all-gather.7.cloned.1.call-update) | async-done | bytes 3342352 | tf_op jit(solution)/shard_map/all_gather | solution.py:1723
  237.0 59.0 %dec.1 = (bf16[256,192]{1,0:T(8,128)(2,1)}, bf16[512,384]{1,0:T(8,128)(2,1)}, bf16[256,192]{1,0:T(8,128)(2,1)}, f32[256,128]{1,0:T(8,128)}, f32[256,768]{1,0:T(8...) custom-call(f32[256,768]{1,0:T(8,128)} %get-tuple-element.80.stream_, ...), custom_call_target="tpu_custom_call" | custom-call | flops 1207959552 | bytes 16204032 | tf_op jit(solution)/shard_map/dec/pallas_call | solution.py:795
  296.1 52.5 %head.1 = (f32[1,128]{1,0:T(1,128)}, bf16[64,768]{1,0:T(8,128)(2,1)}, bf16[768,3072]{1,0:T(8,128)(2,1)}) custom-call(bf16[512,768]{1,0:T(8,128)(2,1)} %bitcast.67, bf16[768,384]{1,0:T(8,128)(2,1)} %bitcast.68, bf16[768,1024]{1,0:T(8,128)(2,1)} %bitcast.65, bf16[768,512]{1,0:T(8,128)(2,1)} %bitcast.66, bf16[768,1152]{1,0:T(8,128)(2,1)} %bitcast.64, ...), custom_call_target="tpu_custom_call" | custom-call | flops 7247757312 | bytes 10328576 | tf_op jit(solution)/shard_map/head/pallas_call | solution.py:795
  348.6 193.8 %backward.1 = (bf16[8,96,3072]{2,1,0:T(8,128)(2,1)}, bf16[4,8,192,96]{3,2,1,0:T(8,128)(2,1)}, bf16[4,96,2176]{2,1,0:T(8,128)(2,1)}, bf16[96,3456]{1,0:T(8,128)(2,1)}, f32[1,128]{1,0:T(1,128)}) custom-call(bf16[64,768]{1,0:T(8,128)(2,1)} %get-tuple-element.93.refs_0_, s32[1,64]{1,0:T(1,128)} %refs_1_.2, f32[256,768]{1,0:T(8,128)} %get-tuple-element.94.refs_2_, ...), custom_call_target="tpu_custom_call" | custom-call | flops 7247757312 | bytes 37118720 | tf_op jit(solution)/shard_map/backward/pallas_call | solution.py:795
  542.4 33.0 %spread_rows.1 = (f32[96,24576]{1,0:T(8,128)}, f32[1,128]{1,0:T(1,128)}) custom-call(s32[8,1024]{1,0:T(8,128)} %bitcast.52, bf16[4,8,192,96]{3,2,1,0:T(8,128)(2,1)} %get-tuple-element.110.grads_ref, bf16[8,96,3072]{2,1,0:T(8,128)(2,1)} %get-tuple-element.111.head_ref), custom_call_target="tpu_custom_call" | custom-call | tf_op jit(solution)/shard_map/spread_rows/pallas_call | solution.py:545
  575.3 12.9 %squares.1 = f32[1,128]{1,0:T(1,128)} custom-call(f32[1,128]{1,0:T(1,128)} %get-tuple-element.112.embedding_ref, f32[1,128]{1,0:T(1,128)} %get-tuple-element.113.dense_ref), custom_call_target="tpu_custom_call" | custom-call | bytes 1536 | tf_op jit(solution)/shard_map/squares/pallas_call | solution.py:795
  589.0 0.0 all-gather.9.cloned.1.call-update
  589.0 0.9 multiply_subtract_fusion.1
  589.8 0.7 copy.112
  590.5 0.7 copy.113
  591.2 0.7 copy.114
  591.9 24.6 %multiply_subtract_fusion = (f32[24026,96]{0,1:T(8,128)}, f32[24026,96]{0,1:T(8,128)}, f32[24026,96]{0,1:T(8,128)}) fusion(f32[24026,96]{0,1:T(8,128)} %param.28, f32[]{:T(128)} %min_shard_map.3, f32[96,24576]{1,0:T(8,128)} %get-tuple-element.114, f32[24026,96]{0,1:T(8,128)} %param.34, f32[24026,96]{0,1:T(8,128)} %param.40), kind=kLoop, calls=%fused_computation.4 | loop fusion | flops 36903936 | bytes 64581892 | tf_op jit(solution)/shard_map/sub | solution.py:214
  616.5 0.0 all-gather.9.cloned.1.call-done
  616.5 5.2 adam_out.1
  621.7 9.7 %adam_in.1 = (f32[3,96,2304]{2,1,0:T(8,128)}, f32[3,96,2304]{2,1,0:T(8,128)}, f32[3,96,2304]{2,1,0:T(8,128)}) custom-call(f32[1]{0:T(128)} %bitcast.17.factor_ref, bf16[4,96,3456]{2,1,0:T(8,128)(2,1)} %bitcast.45, bf16[4,96,2176]{2,1,0:T(8,128)(2,1)} %get-tuple-element.116.refs_1_, f32[3,96,2304]{2,1,0:T(8,128)} %refs_2_.4, f32[3,96,2304]{2,1,0:T(8,128)} %refs_3_.4, ...), custom_call_target="tpu_custom_call" | custom-call | tf_op jit(solution)/shard_map/adam_in/pallas_call | solution.py:1559
  631.4 0.0 copy-start.4
  631.5 8.6 %adam_up.1 = (f32[2,96,3072]{2,1,0:T(8,128)}, f32[2,96,3072]{2,1,0:T(8,128)}, f32[2,96,3072]{2,1,0:T(8,128)}) custom-call(f32[1]{0:T(128)} %bitcast.17.factor_ref, bf16[4,96,3456]{2,1,0:T(8,128)(2,1)} %bitcast.46, bf16[4,96,2176]{2,1,0:T(8,128)(2,1)} %get-tuple-element.116.refs_1_, f32[2,96,3072]{2,1,0:T(8,128)} %refs_2_.6, f32[2,96,3072]{2,1,0:T(8,128)} %refs_3_.6, ...), custom_call_target="tpu_custom_call" | custom-call | tf_op jit(solution)/shard_map/adam_up/pallas_call | solution.py:1559
  640.1 9.7 %adam_down.1 = (f32[2,384,768]{2,1,0:T(8,128)}, f32[2,384,768]{2,1,0:T(8,128)}, f32[2,384,768]{2,1,0:T(8,128)}) custom-call(f32[1]{0:T(128)} %bitcast.17.factor_ref, bf16[4,96,3456]{2,1,0:T(8,128)(2,1)} %bitcast.47, bf16[4,96,2176]{2,1,0:T(8,128)(2,1)} %get-tuple-element.116.refs_1_, f32[2,384,768]{2,1,0:T(8,128)} %refs_2_.7, f32[2,384,768]{2,1,0:T(8,128)} %refs_3_.7, ...), custom_call_target="tpu_custom_call" | custom-call | tf_op jit(solution)/shard_map/adam_down/pallas_call | solution.py:1559
  649.8 0.0 copy-done.4
  (7 shorter events, 0.0 us)
Async XLA Ops:
  7.2 24.0 %copy-start.3 = (s32[1,64]{1,0:T(1,128)S(1)}, s32[1,64]{1,0:T(1,128)}, u32[]{:S(2)}) copy-start(s32[1,64]{1,0:T(1,128)} %refs_1_.2) | copy-start | bytes 772
  7.2 22.5 %copy-start = (f32[14,96]{1,0:T(8,128)S(1)}, f32[14,96]{1,0:T(8,128)}, u32[]{:S(2)}) copy-start(f32[14,96]{1,0:T(8,128)} %norms_ref.1) | copy-start | bytes 16132
  7.2 28.5 %copy-start.1 = (f32[14,96]{1,0:T(8,128)S(1)}, f32[14,96]{1,0:T(8,128)}, u32[]{:S(2)}) copy-start(f32[14,96]{1,0:T(8,128)} %param.39) | copy-start | bytes 16132
  7.2 28.6 %copy-start.2 = (f32[14,96]{1,0:T(8,128)S(1)}, f32[14,96]{1,0:T(8,128)}, u32[]{:S(2)}) copy-start(f32[14,96]{1,0:T(8,128)} %param.45) | copy-start | bytes 16132
  7.2 127.6 %all-gather.5.cloned.1.call-start = ((), (), s32[]{:S(2)}) async-start(), calls=%async_computation | async-start | bytes 5971968 | tf_op jit(solution)/shard_map/all_gather | solution.py:1722
  28.1 208.9 %all-gather.7.cloned.1.call-start = ((), (), s32[]{:S(2)}) async-start(), calls=%async_computation.1 | async-start | bytes 3760128 | tf_op jit(solution)/shard_map/all_gather | solution.py:1723
  28.9 587.6 %all-gather.9.cloned.1.call-start = ((), (), s32[]{:S(2)}) async-start(), calls=%async_computation.2 | async-start | bytes 3317760 | tf_op jit(solution)/shard_map/all_gather | solution.py:1962
  631.4 18.3 %copy-start.4 = (f32[1,128]{1,0:T(1,128)S(1)}, f32[1,128]{1,0:T(1,128)}, u32[]{:S(2)}) copy-start(f32[1,128]{1,0:T(1,128)} %get-tuple-element.92) | copy-start | bytes 1540
Sparse Core Ops, SparseCore 0:
  28.3 106.5 all-gather.4
  137.0 99.9 all-gather.6
  589.1 25.6 all-gather.8

commit v3 on v2

--- a/solution.py
+++ b/solution.py
@@ -509,15 +509,18 @@
 
 
 def spread_kernel(
-    lists_ref, grads_ref, head_ref, out_ref, squares_ref, wide_ref, rows_ref
+    lists_ref, grads_ref, zero_ref, one_ref, out_ref, squares_ref, wide_ref, rows_ref
 ):
-    shares, groups, quarter, width = grads_ref.shape
-    tokens = shares * quarter
-    chunks, _, chunk = head_ref.shape
+    shares, groups, _, width = grads_ref.shape
+    tokens = rows_ref.shape[0] // groups
+    quarter = tokens // shares
+    chunks = zero_ref.shape[0]
+    parts = [(ref, low) for ref in (zero_ref, one_ref) for low in range(0, ref.shape[2], 128)]
+    chunk = 128 * len(parts)
     for index in range(shares):
         for number in range(groups):
             start = number * tokens + index * quarter
-            rows_ref[start : start + quarter, :] = grads_ref[index, number].astype(jnp.float32)
+            rows_ref[start : start + quarter, :] = grads_ref[index, number, 0:quarter].astype(jnp.float32)
     wide_ref[...] = jnp.zeros_like(wide_ref)
 
     def visit(group, row, slot):
@@ -526,12 +529,11 @@
     over_hits(lists_ref, visit)
 
     def turn(piece, total):
-        for part in range(chunk // 128):
-            column = part * 128
+        for part, (head_ref, column) in enumerate(parts):
             start = pl.multiple_of(piece * chunk + part * 128, 128)
             block = jnp.transpose(wide_ref[pl.ds(start, 128), :])[:width]
             block = block + head_ref[piece, :, column : column + 128].astype(jnp.float32)
-            out_ref[:, pl.ds(start, 128)] = block
+            out_ref[:, pl.ds(start, 128)] = lowered(block)
             total = total + block * block
         return total
 
@@ -539,28 +541,28 @@
     squares_ref[...] = jnp.sum(total, axis=0, keepdims=True)
 
 
-def spread_rows(lists, grads, head):
-    chunks, width, chunk = head.shape
-    shares, groups, quarter, _ = grads.shape
+def spread_rows(lists, count, grads, head):
+    chunks, width, _ = head[0].shape
+    chunk = sum(member.shape[2] for member in head)
     return pl.pallas_call(
         spread_kernel,
         out_shape=(
-            jax.ShapeDtypeStruct((width, chunks * chunk), jnp.float32),
+            jax.ShapeDtypeStruct((width, chunks * chunk), jnp.bfloat16),
             jax.ShapeDtypeStruct((1, 128), jnp.float32),
         ),
         in_specs=[pl.BlockSpec(memory_space=pltpu.SMEM)]
-        + [pl.BlockSpec(memory_space=pltpu.VMEM)] * 2,
+        + [pl.BlockSpec(memory_space=pltpu.VMEM)] * 3,
         out_specs=(
             pl.BlockSpec(memory_space=pltpu.VMEM),
             pl.BlockSpec(memory_space=pltpu.VMEM),
         ),
         scratch_shapes=[
             pltpu.VMEM((chunks * chunk, 128), jnp.float32),
-            pltpu.VMEM((shares * groups * quarter, width), jnp.float32),
+            pltpu.VMEM((count, width), jnp.float32),
         ],
         compiler_params=pltpu.CompilerParams(vmem_limit_bytes=VMEM_BYTES),
         name="spread_rows",
-    )(lists, grads, head)
+    )(lists, grads, *head)
 
 
 MESH = pl.DeviceIdType.MESH
@@ -889,49 +891,77 @@
     return looked * math.sqrt(width) + place_ref[...]
 
 
-def first_kernel(
-    groups, shares, start, first_wide,
-    looked_ref, place_enc_ref, place_dec_ref, w_ref, across_ref,
-    qkv_enc_ref, context_enc_ref, logs_enc_ref, stream_enc_ref,
-    qkv_dec_ref, context_dec_ref, logs_dec_ref, stream_dec_ref,
-    out_rows_ref, norms_ref, table_ref,
-    table_sems, blocks_ref, block_sems, local_sem, *total_refs,
-):
-    group, share, _, _, _ = places()
-    peers = share_peers(group, share, shares)
-    meet(peers + group_peers(group, share, groups))
-    chunk, columns = across_ref.shape[1] // groups, table_ref.shape[2]
-    exchange = Exchange(
-        table_blocks(across_ref, chunk, start, columns), table_ref, table_sems, groups
-    )
-    _, rows, wide = blocks_ref.shape
+def forward_kernel(groups, shares, base, cuts, refs_in, refs_out, *refs):
+    inputs, outputs, scratch = refs[:refs_in], refs[refs_in : refs_in + refs_out], refs[refs_in + refs_out :]
+    looked_ref, place_enc_ref, place_dec_ref, w_early_hbm, across_ref = inputs
+    (
+        table_ref, out_rows_ref, norms_ref,
+        qkv_enc_ref, context_enc_ref, logs_enc_ref, stream_enc_hbm, pre_enc_hbm, stream_two_hbm, memory_ref,
+        qkv_dec_ref, context_dec_ref, logs_dec_ref, stream_dec_ref,
+    ) = outputs
+    (
+        table_sems, out_sems, load_sems, w_first_ref, w_enc_ref, stream_enc_ref, pre_enc_ref, stream_two_ref,
+        blocks_ref, block_sems, local_sem,
+    ) = scratch[:11]
+    rest = scratch[11:]
+    small_one, large_one = rest[:4], rest[4:8]
+    large_two = large_one[:1] + rest[8:11]
+    group, share, core, core_peer, side_peer = places()
+    peers, far = share_peers(group, share, shares), group_peers(group, share, groups)
+    first_wide = w_first_ref.shape[1]
+    load_first = Late(w_early_hbm.at[:, pl.ds(0, first_wide)], w_first_ref, load_sems.at[0])
+    load_enc = Late(
+        w_early_hbm.at[:, pl.ds(first_wide, w_enc_ref.shape[1])], w_enc_ref, load_sems.at[1]
+    )
+    meet(peers + far)
+    chunk = across_ref.shape[1] // groups
+    starts = np.cumsum((0,) + cuts).tolist()
+
+    def table_piece(index):
+        at = pl.ds(starts[index], cuts[index])
+        return Exchange(
+            table_blocks(across_ref, chunk, base + starts[index], cuts[index]),
+            table_ref.at[:, :, at],
+            table_sems.at[index],
+            groups,
+        )
+
+    outgoing = []
+
+    def put_out(source, target):
+        copy = pltpu.make_async_copy(source, target, out_sems.at[len(outgoing)])
+        copy.start()
+        outgoing.append(copy)
+
+    table_zero = table_piece(0)
+    load_first()
+
     own = qkv_enc_ref.shape[1] // 3
+    rows, wide = blocks_ref.shape[1:]
     padded = first_wide - wide
-    enc_start, dec_start, out_start = 0, padded // 2, padded
-    window = pl.ds(out_start, wide)
+    window = pl.ds(padded, wide)
     copies = []
     for step, (_, peer) in enumerate(peers):
-        source = w_ref.at[pl.ds(pl.multiple_of(peer * rows, 64), rows), window]
+        source = w_first_ref.at[pl.ds(pl.multiple_of(peer * rows, 64), rows), window]
         copies.append(
             send(source, blocks_ref.at[share], block_sems.at[0, step], block_sems.at[1, step], (group, peer))
         )
     keep = pltpu.make_async_copy(
-        w_ref.at[pl.ds(pl.multiple_of(share * rows, 64), rows), window], blocks_ref.at[share], local_sem
+        w_first_ref.at[pl.ds(pl.multiple_of(share * rows, 64), rows), window], blocks_ref.at[share], local_sem
     )
     keep.start()
-
-    turned = jnp.transpose(w_ref[:, first_wide - 128 : first_wide].astype(jnp.float32))
+    turned = jnp.transpose(w_first_ref[:, first_wide - 128 :].astype(jnp.float32))
     norms_ref[...] = turned[64:80]
-
-    enc_total, dec_total = Total(total_refs[:4]), Total(total_refs[4:])
+    enc_total, dec_total = Total(large_one), Total(small_one)
     enc_len, dec_len = place_enc_ref.shape[0], place_dec_ref.shape[0]
     stream = stream_of(looked_ref, 0, place_enc_ref)
     normed, _ = norm_forward(stream, *gain_of(norms_ref, 0))
-    qkv_enc_ref[...] = lowered(matmul(lowered(normed), w_ref[:, enc_start : enc_start + 3 * own]))
+    qkv_enc_ref[...] = lowered(matmul(lowered(normed), w_first_ref[:, : 3 * own]))
     stream_enc_ref[...] = stream
-    starts = (0, own, 2 * own)
+    head_starts = (0, own, 2 * own)
     logs_enc_ref[...] = jnp.zeros_like(logs_enc_ref)
-    heads_forward(qkv_enc_ref, qkv_enc_ref, starts, context_enc_ref, logs_enc_ref, False)
+    heads_forward(qkv_enc_ref, qkv_enc_ref, head_starts, context_enc_ref, logs_enc_ref, False)
+    table_one = table_piece(1)
     keep.wait()
     for copy in copies:
         copy.wait()
@@ -945,83 +975,80 @@
     stream_dec_ref[...] = stream
     normed, _ = norm_forward(stream, *gain_of(norms_ref, 3))
     enc_total.middle()
-    qkv_dec_ref[...] = lowered(matmul(lowered(normed), w_ref[:, dec_start : dec_start + 3 * own]))
+    dec_start = padded // 2
+    qkv_dec_ref[...] = lowered(
+        matmul(lowered(normed), w_first_ref[:, dec_start : dec_start + 3 * own])
+    )
     logs_dec_ref[...] = jnp.zeros_like(logs_dec_ref)
-    heads_forward(qkv_dec_ref, qkv_dec_ref, starts, context_dec_ref, logs_dec_ref, True)
+    heads_forward(qkv_dec_ref, qkv_dec_ref, head_starts, context_dec_ref, logs_dec_ref, True)
     enc_total.last()
     dec_total.begin(matmul(context_dec_ref[...], out_rows_ref[1]))
     dec_total.middle()
     stream_enc_ref[...] += enc_total.finish()
+    put_out(stream_enc_ref, stream_enc_hbm)
     dec_total.last()
+
+    total = Total(large_two)
+    normed, _ = norm_forward(stream_enc_ref[...], *gain_of(norms_ref, 1))
+    hidden, width = pre_enc_ref.shape[1], stream_enc_ref.shape[1]
+    load_enc()
+    pre_enc_ref[...] = matmul(lowered(normed), w_enc_ref[:, :hidden])
+    put_out(pre_enc_ref, pre_enc_hbm)
+    activated = lowered(jax.nn.silu(pre_enc_ref[...]))
+    total.begin(matmul(activated, w_enc_ref[:, hidden : hidden + width]))
     stream_dec_ref[...] += dec_total.finish()
-    exchange.finish()
-
-
-def enc_feed_kernel(
-    groups, start, first_wide,
-    stream_in_ref, norms_ref, w_early_ref, across_ref,
-    pre_ref, stream_ref, memory_ref, table_ref,
-    table_sems, w_ref, w_sem, *total_refs,
+    stream_two_ref[...] = stream_enc_ref[...] + total.rest()
+    put_out(stream_two_ref, stream_two_hbm)
+    memory, _ = norm_forward(stream_two_ref[...], *gain_of(norms_ref, 2))
+    memory_ref[...] = lowered(memory)
+    for piece in (table_zero, table_one):
+        piece.finish()
+    for copy in outgoing:
+        copy.wait()
+
+
+def dec_kernel(
+    groups, start,
+    stream_dec_ref, memory_ref, norms_ref, out_rows_ref, positions_ref, w_dec_hbm, across_ref,
+    table_ref, q_ref, kv_ref, context_ref, logs_ref, stream_mid_ref, pre_dec_ref, stream_out_ref, selected_ref,
+    w_dec_ref, load_sem, table_sems, own_ref, select_sems, *rest,
 ):
-    group, share, _, core_peer, side_peer = places()
-    load = Late(w_early_ref.at[:, pl.ds(first_wide, w_ref.shape[1])], w_ref, w_sem)
-    meet([core_peer, side_peer] + group_peers(group, share, groups))
+    small_one, small_two = rest[:4], rest[:1] + rest[4:7]
+    group, share, core, core_peer, side_peer = places()
+    far = group_peers(group, share, groups)
+    load_dec = Late(w_dec_hbm, w_dec_ref, load_sem)
+    meet([core_peer, side_peer] + far)
     chunk, columns = across_ref.shape[1] // groups, table_ref.shape[2]
     exchange = Exchange(
         table_blocks(across_ref, chunk, start, columns), table_ref, table_sems, groups
     )
-    width = stream_in_ref.shape[1]
-    total = Total(total_refs)
-    normed, _ = norm_forward(stream_in_ref[...], *gain_of(norms_ref, 1))
-    hidden = w_ref.shape[1] - width
-    load()
-    pre_ref[...] = matmul(lowered(normed), w_ref[:, :hidden])
-    activated = lowered(jax.nn.silu(pre_ref[...]))
-    total.begin(matmul(activated, w_ref[:, hidden:]))
-    stream_ref[...] = stream_in_ref[...] + total.rest()
-    memory, _ = norm_forward(stream_ref[...], *gain_of(norms_ref, 2))
-    memory_ref[...] = lowered(memory)
-    exchange.finish()
-
-
-def dec_kernel(
-    groups, start,
-    stream_in_ref, memory_ref, norms_ref, w_ref, out_rows_ref, positions_ref, across_ref,
-    q_ref, kv_ref, context_ref, logs_ref, stream_mid_ref, pre_ref, stream_ref, selected_ref, table_ref,
-    own_ref, select_sems, table_sems, *total_refs,
-):
-    group, share, _, core_peer, side_peer = places()
-    peers = group_peers(group, share, groups)
-    meet([core_peer, side_peer] + peers)
-    chunk, columns = across_ref.shape[1] // groups, table_ref.shape[2]
-    exchange = Exchange(
-        table_blocks(across_ref, chunk, start, columns), table_ref, table_sems, groups
-    )
-    width = stream_in_ref.shape[1]
-    own = q_ref.shape[1]
-    hidden = pre_ref.shape[1]
+    own, hidden = q_ref.shape[1], pre_dec_ref.shape[1]
+    dec_len, width = stream_dec_ref.shape
+    cross_total, feed_total = Total(small_two), Total(small_one)
     in_start = hidden + width
-    cross_total, feed_total = Total(total_refs[:4]), Total(total_refs[4:])
-    kv_ref[...] = lowered(matmul(memory_ref[...], w_ref[:, in_start + own : in_start + 3 * own]))
-    normed, _ = norm_forward(stream_in_ref[...], *gain_of(norms_ref, 4))
-    q_ref[...] = lowered(matmul(lowered(normed), w_ref[:, in_start : in_start + own]))
+    normed, _ = norm_forward(stream_dec_ref[...], *gain_of(norms_ref, 4))
+    load_dec()
+    kv_ref[...] = lowered(
+        matmul(memory_ref[...], w_dec_ref[:, in_start + own : in_start + 3 * own])
+    )
+    q_ref[...] = lowered(matmul(lowered(normed), w_dec_ref[:, in_start : in_start + own]))
     logs_ref[...] = jnp.zeros_like(logs_ref)
     heads_forward(q_ref, kv_ref, (0, 0, own), context_ref, logs_ref, False)
     cross_total.begin(matmul(context_ref[...], out_rows_ref[2]))
-    stream_mid_ref[...] = stream_in_ref[...] + cross_total.rest()
+    stream_mid_ref[...] = stream_dec_ref[...] + cross_total.rest()
     normed, _ = norm_forward(stream_mid_ref[...], *gain_of(norms_ref, 5))
-    pre_ref[...] = matmul(lowered(normed), w_ref[:, :hidden])
-    activated = lowered(jax.nn.silu(pre_ref[...]))
-    feed_total.begin(matmul(activated, w_ref[:, hidden : hidden + width]))
-    stream_ref[...] = stream_mid_ref[...] + feed_total.rest()
-    final, _ = norm_forward(stream_ref[...], *gain_of(norms_ref, 6))
-    places_down = lax.broadcasted_iota(jnp.int32, (own_ref.shape[0], stream_ref.shape[0]), 1)
+    pre_dec_ref[...] = matmul(lowered(normed), w_dec_ref[:, :hidden])
+    activated = lowered(jax.nn.silu(pre_dec_ref[...]))
+    feed_total.begin(matmul(activated, w_dec_ref[:, hidden:in_start]))
+    stream_out_ref[...] = stream_mid_ref[...] + feed_total.rest()
+    final, _ = norm_forward(stream_out_ref[...], *gain_of(norms_ref, 6))
+    places_down = lax.broadcasted_iota(jnp.int32, (own_ref.shape[0], dec_len), 1)
     chosen = lowered(jnp.where(places_down == positions_ref[...], 1.0, 0.0))
     own_ref[...] = lowered(matmul(chosen, lowered(final)))
     selected_ref[group] = own_ref[...]
     copies = [
         send(own_ref, selected_ref.at[group], select_sems.at[0, step], select_sems.at[1, step], peer)
-        for step, peer in enumerate(peers)
+        for step, peer in enumerate(far)
     ]
     exchange.finish()
     for copy in copies:
@@ -1042,9 +1069,9 @@
 
 def head_kernel(
     groups, shares, shard_rows,
-    selected_ref, zero_ref, one_ref, two_ref, three_ref, targets_ref, weights_ref, counted_ref,
-    loss_ref, grad_out_ref, head_ref,
-    logits_ref, dz_ref, stats_ref, turned_ref, share_stats_ref, group_stats_ref, stat_sems,
+    selected_ref, zero_ref, one_ref, two_ref, targets_ref, weights_ref, counted_ref,
+    loss_ref, grad_out_ref, head_ref, head_out_ref,
+    head_sems, logits_ref, dz_ref, stats_ref, turned_ref, share_stats_ref, group_stats_ref, stat_sems,
     part_ref, core_ref, side_ref, group_ref, sum_ref, sems,
 ):
     group, share, core, core_peer, side_peer = places()
@@ -1053,19 +1080,18 @@
     meet(near + far)
     rows, width = selected_ref.shape
     chunk = logits_ref.shape[1]
-    tables = (zero_ref, one_ref, two_ref, three_ref)
-    starts = np.cumsum([0] + [ref.shape[1] for ref in tables])
     vocab_total = shard_rows * shares
     first = group * chunk
     limit = jnp.minimum(shard_rows - first, vocab_total - 1 - share * shard_rows - first)
     block = 384
     step_rows = 32
 
+    tables = (zero_ref, one_ref, two_ref)
+    starts = np.cumsum([0] + [ref.shape[1] for ref in tables]).tolist()
     for ref, start in zip(tables, starts):
-        step = 512 if ref.shape[1] % 512 == 0 else 384
-        for low in range(0, ref.shape[1], step):
-            logits_ref[:, start + low : start + low + step] = matmul(
-                selected_ref[...], ref[:, low : low + step]
+        for low in range(0, ref.shape[1], block):
+            logits_ref[:, start + low : start + low + block] = matmul(
+                selected_ref[...], ref[:, low : low + block]
             )
     stats_ref[...] = jnp.zeros_like(stats_ref)
 
@@ -1123,6 +1149,23 @@
     lax.fori_loop(0, rows // step_rows, make_dz, 0)
     loss_rows = rows // groups
     half, quarter = loss_rows // 2, loss_rows // 4
+
+    def head_part(index):
+        at = slice(index * block, (index + 1) * block)
+        head_ref[:, at] = lowered(contract_rows(selected_ref[...], dz_ref[:, at]))
+
+    early = head_out_ref.shape[2] // block
+    for index in range(early):
+        head_part(index)
+    width_out = width // groups
+    exchange = Exchange(
+        lambda index: head_ref.at[
+            pl.ds(pl.multiple_of(index * width_out, 16), width_out), pl.ds(0, early * block)
+        ],
+        head_out_ref,
+        head_sems,
+        groups,
+    )
     grad_rows = 0.0
     for ref, start in zip(tables, starts):
         grad_rows = grad_rows + times_transposed(dz_ref[:, start : start + ref.shape[1]], ref[...])
@@ -1130,13 +1173,8 @@
     mine = pl.ds(pl.multiple_of(core * half, 16), half)
     other = pl.ds(pl.multiple_of((1 - core) * half, 16), half)
     copy = send(part_ref.at[:, other, :], core_ref, sems.at[0, 0], sems.at[1, 0], core_peer)
-
-    def head_part(index):
-        at = slice(index * block, (index + 1) * block)
-        head_ref[:, at] = lowered(contract_rows(selected_ref[...], dz_ref[:, at]))
-
     parts = chunk // block
-    head_part(0)
+    middle = (early + parts) // 2
     copy.wait()
     part_ref[:, mine, :] = lowered(
         part_ref[:, mine, :].astype(jnp.float32) + core_ref[...].astype(jnp.float32)
@@ -1145,7 +1183,7 @@
     my_quarter = pl.ds(pl.multiple_of(base + side * quarter, 16), quarter)
     other_quarter = pl.ds(pl.multiple_of(base + (1 - side) * quarter, 16), quarter)
     copy = send(part_ref.at[:, other_quarter, :], side_ref, sems.at[0, 1], sems.at[1, 1], side_peer)
-    for index in range(1, parts // 2):
+    for index in range(early, middle):
         head_part(index)
     copy.wait()
     side_ref[...] = lowered(
@@ -1156,7 +1194,7 @@
         send(side_ref.at[peer[0]], group_ref.at[group], sems.at[0, 2 + step], sems.at[1, 2 + step], peer)
         for step, peer in enumerate(far)
     ]
-    for index in range(parts // 2, parts):
+    for index in range(middle, parts):
         head_part(index)
     for copy in copies:
         copy.wait()
@@ -1172,6 +1210,7 @@
     ]
     for copy in copies:
         copy.wait()
+    exchange.finish()
 
 
 def put_grads(grads_ref, start, value):
@@ -1210,7 +1249,7 @@
 
 
 def back_kernel(
-    groups, shares, first_wide, norm_start, norm_count, refs_in, refs_out, *refs
+    groups, shares, first_wide, refs_in, refs_out, *refs
 ):
     inputs, outputs, scratch = refs[:refs_in], refs[refs_in : refs_in + refs_out], refs[refs_in + refs_out :]
     (
@@ -1228,10 +1267,10 @@
         grad_ref, grad_enc_ref,
         context_ref, gq_ref, gkv_ref, gqkv_ref, gqkv_enc_ref, context_enc_grad_ref,
         g_enc_ref, g_self_ref, g_cross_ref, rows_dec_ref, rows_mid_ref, rows_ref,
-        norm_rows_ref, turned_ref, blocks_ref, block_sems, cut_ref, token_sems, share_sems, dec_sems, dec_own_ref,
+        norm_rows_ref, blocks_ref, block_sems, cut_ref, token_sems, share_sems, dec_sems, dec_own_ref,
         local_sems,
-    ) = scratch[:38]
-    rest = scratch[38:]
+    ) = scratch[:37]
+    rest = scratch[37:]
     stream_ref = pre_enc_ref
     small_one, large_one = rest[:4], rest[4:8]
     small_two, large_two = small_one[:1] + rest[8:11], large_one[:1] + rest[11:14]
@@ -1253,7 +1292,10 @@
     load_looked = Late(looked_hbm, looked_ref, load_sems.at[8])
     meet(peers + group_peers(group, share, groups))
     exchange = Exchange(
-        head_blocks(head_in_ref, 0, head_out_ref.shape[2]), head_out_ref, head_sems, groups
+        head_blocks(head_in_ref, head_in_ref.shape[2] - head_out_ref.shape[2], head_out_ref.shape[2]),
+        head_out_ref,
+        head_sems,
+        groups,
     )
     width = stream_out_ref.shape[1]
     own = q_ref.shape[1]
@@ -1339,66 +1381,35 @@
         grad_enc_ref, stream_enc_ref, norms_ref, 1, feed_total.finish(), rows_mid_ref, 2
     )
     self_total.last()
-    tokens = cut_ref.shape[1]
-    part = cut_ref.shape[2]
+    tokens, part = looked_ref.shape[0], cut_ref.shape[2]
+    quarter = tokens // shares
+    block_rows = cut_ref.shape[1] // shares
+
+    def put_tokens(first, rows):
+        for index in range(groups):
+            for piece in range(shares):
+                low, high = max(first, piece * quarter), min(first + rows.shape[0], (piece + 1) * quarter)
+                if low < high:
+                    to = piece * block_rows - piece * quarter
+                    cut_ref[index, to + low : to + high] = rows[
+                        low - first : high - first, index * part : (index + 1) * part
+                    ]
+
     grad_dec = norm_step(
         grad_ref, stream_dec_ref, norms_ref, 3, self_total.finish(), rows_mid_ref, 4
     )
-    grad_low = lowered(grad_dec * math.sqrt(width))
-    for index in range(groups):
-        cut_ref[index, enc_len:tokens] = grad_low[:, index * part : (index + 1) * part]
+    put_tokens(enc_len, lowered(grad_dec * math.sqrt(width)))
 
     total = Total(large_one)
     grad_low = lowered(grad_enc_ref[...])
-    context_enc_grad_ref[...] = lowered(times_transposed(grad_low, out_rows_ref[0]))
-    heads_backward(
-        qkv_enc_ref, qkv_enc_ref, starts, logs_enc_ref, context_enc_grad_ref, gqkv_enc_ref, gqkv_enc_ref, starts,
-        False,
-    )
-    total.begin(times_transposed(gqkv_enc_ref[...], w_ref[:, : 3 * own]))
-    dec_line.beside()
     g_enc_ref[...] = lowered(contract_rows(context_enc_ref[...], grad_low))
-    total.middle()
-    load_place()
-    stream_ref[...] = stream_of(looked_ref, 0, stream_two_ref)
-    normed, _ = norm_forward(stream_ref[...], *gain_of(norms_ref, 0))
     wide = blocks_ref.shape[2]
     in_wide = last_grads_ref.shape[4] - wide
-    put_grads(last_grads_ref, 0, contract_rows(lowered(normed), gqkv_enc_ref[...]))
-    put_grads(last_grads_ref, 3 * own, jnp.zeros((width, in_wide - 3 * own), jnp.float32))
     blocks_ref[...] = jnp.zeros_like(blocks_ref)
     for piece in range(shares):
         at = slice(piece * own, (piece + 1) * own)
         for matrix, source in enumerate((g_enc_ref, g_self_ref, g_cross_ref)):
             blocks_ref[piece, :, matrix * own : (matrix + 1) * own] = source[:, at]
-    total.last()
-    grad_enc = norm_step(grad_enc_ref, stream_ref, norms_ref, 0, total.finish(), rows_ref, 0)
-    grad_low = lowered(grad_enc * math.sqrt(width))
-    for index in range(groups):
-        cut_ref[index, 0:enc_len] = grad_low[:, index * part : (index + 1) * part]
-    quarter = tokens // shares
-    own_rows = pl.ds(pl.multiple_of(share * quarter, 64), quarter)
-    to_groups = Exchange(
-        lambda index: cut_ref.at[index, own_rows, :], own_tokens_ref.at[share], token_sems, groups
-    )
-    norm_rows_ref[...] = jnp.zeros_like(norm_rows_ref)
-    order = (
-        (0, rows_ref, 0),
-        (1, rows_mid_ref, 2),
-        (2, rows_mid_ref, 0),
-        (3, rows_mid_ref, 4),
-        (4, rows_dec_ref, 4),
-        (5, rows_dec_ref, 2),
-        (6, rows_dec_ref, 0),
-    )
-    for row, source, slot in order:
-        norm_rows_ref[64 + row : 65 + row, :] = source[slot : slot + 1, :]
-        norm_rows_ref[71 + row : 72 + row, :] = source[slot + 1 : slot + 2, :]
-    turned_ref[...] = jnp.transpose(norm_rows_ref[...])
-    own_norms = turned_ref[pl.ds(pl.multiple_of(share * own, 64), own), :]
-    for piece in range(shares):
-        tail = blocks_ref[piece, :, wide - 128 :].astype(jnp.float32)
-        blocks_ref[piece, :, wide - 128 :] = lowered(tail + own_norms)
     copies = []
     for half in range(2):
         target = last_grads_ref.at[share // 2, lax.rem(share, 2), half, :, pl.ds(in_wide, wide)]
@@ -1418,9 +1429,48 @@
         )
         keep.start()
         copies.append(keep)
+    context_enc_grad_ref[...] = lowered(times_transposed(grad_low, out_rows_ref[0]))
+    heads_backward(
+        qkv_enc_ref, qkv_enc_ref, starts, logs_enc_ref, context_enc_grad_ref, gqkv_enc_ref, gqkv_enc_ref, starts,
+        False,
+    )
+    total.begin(times_transposed(gqkv_enc_ref[...], w_ref[:, : 3 * own]))
+    load_place()
+    stream_ref[...] = stream_of(looked_ref, 0, stream_two_ref)
+    normed, _ = norm_forward(stream_ref[...], *gain_of(norms_ref, 0))
+    total.middle()
+    put_grads(last_grads_ref, 0, contract_rows(lowered(normed), gqkv_enc_ref[...]))
+    put_grads(last_grads_ref, 3 * own, jnp.zeros((width, in_wide - 3 * own), jnp.float32))
     for copy in copies:
         copy.wait()
     last_line.begin()
+    dec_line.beside()
+    total.last()
+    grad_enc = norm_step(grad_enc_ref, stream_ref, norms_ref, 0, total.finish(), rows_ref, 0)
+    put_tokens(0, lowered(grad_enc * math.sqrt(width)))
+    norm_rows_ref[...] = jnp.zeros_like(norm_rows_ref)
+    order = (
+        (0, rows_ref, 0),
+        (1, rows_mid_ref, 2),
+        (2, rows_mid_ref, 0),
+        (3, rows_mid_ref, 4),
+        (4, rows_dec_ref, 4),
+        (5, rows_dec_ref, 2),
+        (6, rows_dec_ref, 0),
+    )
+    for row, source, slot in order:
+        norm_rows_ref[row : row + 1, :] = source[slot : slot + 1, :]
+        norm_rows_ref[7 + row : 8 + row, :] = source[slot + 1 : slot + 2, :]
+    norm_low = lowered(norm_rows_ref[...])
+    for index in range(groups):
+        for piece in range(shares):
+            cut_ref[index, piece * block_rows + quarter : (piece + 1) * block_rows] = norm_low[
+                :, index * part : (index + 1) * part
+            ]
+    own_rows = pl.ds(pl.multiple_of(share * block_rows, 16), block_rows)
+    to_groups = Exchange(
+        lambda index: cut_ref.at[index, own_rows, :], own_tokens_ref.at[share], token_sems, groups
+    )
     mid_line.beside()
     dec_line.beyond()
     to_groups.finish()
@@ -1443,10 +1493,6 @@
     for ref in (dec_own_ref, own_ref):
         value = ref[...].astype(jnp.float32)
         value = value * value
-        if ref is own_ref:
-            column = lax.broadcasted_iota(jnp.int32, value.shape, 1)
-            norm_part = (column >= norm_start) & (column < norm_start + norm_count)
-            value = jnp.where(norm_part, value / shares, value)
         squares = squares + jnp.sum(jnp.sum(value, axis=0, keepdims=True), axis=1, keepdims=True)
     lane = lax.broadcasted_iota(jnp.int32, squares_ref.shape, 1)
     squares_ref[...] = jnp.where(lane == 0, squares, 0.0)
@@ -1456,9 +1502,9 @@
 
 def look_kernel(
     groups,
-    picked_ref, across_ref,
-    looked_ref, table_ref,
-    send_ref, core_ref, side_ref, group_ref, sems, table_sems,
+    picked_ref,
+    looked_ref,
+    send_ref, core_ref, side_ref, group_ref, sems,
 ):
     group, share, core, core_peer, side_peer = places()
     side = share // 2
@@ -1481,10 +1527,6 @@
     ]
     for copy in copies:
         copy.wait()
-    chunk, columns = across_ref.shape[1] // groups, table_ref.shape[2]
-    exchange = Exchange(
-        table_blocks(across_ref, chunk, 0, columns), table_ref, table_sems, groups
-    )
     for index in range(groups):
         send_ref[:, index * width : (index + 1) * width] = group_ref[index]
     at = pl.ds(pl.multiple_of(core * half + side * quarter, 16), quarter)
@@ -1494,7 +1536,6 @@
     end = end + 1
     both = looked_ref.at[mine, :]
     send(both, both, sems.at[0, end], sems.at[1, end], core_peer).wait()
-    exchange.finish()
 
 
 def squares_kernel(
@@ -1547,13 +1588,16 @@
         out[0] = value
 
 
-def dense_update(name, rate, place_grads, factor, grads, w, first, second, parts):
+def dense_update(name, rate, place_grads, factor, grads, w, first, second, parts, cut=None):
     matrices, rows, columns = w.shape
     rows = rows // parts
     own = pl.BlockSpec((1, rows, columns), lambda matrix, part: (matrix, part, 0))
     shares, width = grads[0].shape[:2]
     grad_specs = [
-        pl.BlockSpec((shares, width, member.shape[2]), lambda matrix, part: (0, 0, 0))
+        pl.BlockSpec(
+            (shares, width, cut[0] if cut else member.shape[2]),
+            lambda matrix, part: (0, 0, cut[1] if cut else 0),
+        )
         for member in grads
     ]
     return pl.pallas_call(
@@ -1586,11 +1630,62 @@
     return place
 
 
-def prepare_kernel(
-    groups, shares, gap,
-    numbers_ref, hits_ref, in_ref, out_ref, up_ref, down_ref, norms_ref,
-    all_numbers_ref, all_hits_ref, early_ref, dec_ref,
-    square_ref, sems, local_sems,
+def cut_kernel(groups, shares, gap, in_ref, out_ref, up_ref, down_ref, norms_ref, early_ref, dec_ref, square_ref):
+    share = lax.axis_index("vocab")
+    width, model_width = in_ref.shape[1], out_ref.shape[2]
+    own = model_width // shares
+    piece = up_ref.shape[2] // groups // shares
+    hidden = groups * piece
+    in_wide = 3 * own + gap
+    early_ref[...] = jnp.zeros_like(early_ref)
+    dec_ref[...] = jnp.zeros_like(dec_ref)
+
+    def columns(target, start, source, groups_in, size, index):
+        step = shares * size
+        for number in range(groups_in):
+            low = number * step + index * size
+            target[:, start + number * size : start + (number + 1) * size] = lowered(
+                source[:, low : low + size]
+            )
+
+    def put(index):
+        columns(early_ref, 0, in_ref.at[0], 3, own, index)
+        columns(early_ref, in_wide, in_ref.at[1], 3, own, index)
+        for matrix in range(3):
+            columns(early_ref, 2 * in_wide + matrix * own, out_ref.at[matrix], 1, own, index)
+        rows = slice(index * (down_ref.shape[1] // shares), (index + 1) * (down_ref.shape[1] // shares))
+        for matrix, (target, start) in enumerate(((early_ref, 3 * in_wide), (dec_ref, 0))):
+            columns(target, start, up_ref.at[matrix], groups, piece, index)
+            start = start + hidden
+            target[:, start : start + model_width] = lowered(down_ref[matrix, rows, :])
+        columns(dec_ref, hidden + model_width, in_ref.at[2], 3, own, index)
+
+    for index in range(shares):
+        pl.when(share == index)(partial(put, index))
+    square_ref[...] = jnp.zeros_like(square_ref)
+    square_ref[0 : norms_ref.shape[0], 0:width] = norms_ref[...]
+    end = 3 * in_wide
+    early_ref[:, end - gap : end] = lowered(jnp.transpose(square_ref[...])[0:width, 0:gap])
+
+
+def cut_weights(groups, shares, gap, inputs, early_wide, dec_wide):
+    width = inputs[0].shape[1]
+    return pl.pallas_call(
+        partial(cut_kernel, groups, shares, gap),
+        out_shape=(
+            jax.ShapeDtypeStruct((width, early_wide), jnp.bfloat16),
+            jax.ShapeDtypeStruct((width, dec_wide), jnp.bfloat16),
+        ),
+        in_specs=[pl.BlockSpec(memory_space=pltpu.VMEM)] * len(inputs),
+        out_specs=(pl.BlockSpec(memory_space=pltpu.VMEM),) * 2,
+        scratch_shapes=[pltpu.VMEM((128, 128), jnp.float32)],
+        compiler_params=pltpu.CompilerParams(vmem_limit_bytes=VMEM_BYTES),
+        name="cut_weights",
+    )(*inputs)
+
+
+def numbers_kernel(
+    groups, numbers_ref, hits_ref, all_numbers_ref, all_hits_ref, sems, local_sems
 ):
     group, share, _, _, _ = places()
     peers = group_peers(group, share, groups)
@@ -1606,40 +1701,6 @@
         keep = pltpu.make_async_copy(source, target.at[group], local_sems.at[number])
         keep.start()
         copies.append(keep)
-    width, model_width = in_ref.shape[1], out_ref.shape[2]
-    own = model_width // shares
-    piece = up_ref.shape[2] // groups // shares
-    hidden = groups * piece
-    early_ref[...] = jnp.zeros_like(early_ref)
-    dec_ref[...] = jnp.zeros_like(dec_ref)
-
-    def put(index):
-        def columns(target, start, source, groups_in, size):
-            step = shares * size
-            for number in range(groups_in):
-                low = number * step + index * size
-                target[:, start + number * size : start + (number + 1) * size] = lowered(
-                    source[:, low : low + size]
-                )
-
-        in_wide = 3 * own + gap
-        columns(early_ref, 0, in_ref.at[0], 3, own)
-        columns(early_ref, in_wide, in_ref.at[1], 3, own)
-        for matrix in range(3):
-            columns(early_ref, 2 * in_wide + matrix * own, out_ref.at[matrix], 1, own)
-        rows = slice(index * (down_ref.shape[1] // shares), (index + 1) * (down_ref.shape[1] // shares))
-        for matrix, (target, start) in enumerate(((early_ref, 3 * in_wide), (dec_ref, 0))):
-            columns(target, start, up_ref.at[matrix], groups, piece)
-            start = start + hidden
-            target[:, start : start + model_width] = lowered(down_ref[matrix, rows, :])
-        columns(dec_ref, hidden + model_width, in_ref.at[2], 3, own)
-
-    for index in range(shares):
-        pl.when(share == index)(partial(put, index))
-    square_ref[...] = jnp.zeros_like(square_ref)
-    square_ref[0 : norms_ref.shape[0], 0:width] = norms_ref[...]
-    end = 3 * (3 * own + gap)
-    early_ref[:, end - gap : end] = lowered(jnp.transpose(square_ref[...])[0:width, 0:gap])
     for copy in copies:
         copy.wait()
 
@@ -1697,30 +1758,28 @@
     in_wide = own_in + gap
     dec_wide = own_up + model_width + in_wide
     first_wide = 3 * in_wide
-    early_wide = first_wide + own_up + model_width
+    enc_wide = own_up + model_width
     chunk = -(-shard_rows // (groups * 3072)) * 3072
-    table_cuts = (chunk // 8, chunk // 3, chunk // 6, 3 * chunk // 8)
-    table_starts = np.cumsum((0,) + table_cuts).tolist()
-    numbers, hits, mine_early, mine_dec = call(
-        partial(prepare_kernel, groups, shares, gap),
-        "prepare",
+    table_cuts = (chunk // 4, 5 * chunk // 24, chunk // 6, 3 * chunk // 8)
+    early_wide = first_wide + enc_wide
+    mine_early, mine_dec = cut_weights(
+        groups, shares, gap, (attn_in, attn_out, ffn_up, ffn_down, norms), early_wide, dec_wide
+    )
+    w_early = lax.all_gather(mine_early, "dp", axis=0, tiled=True)
+    w_dec = lax.all_gather(mine_dec, "dp", axis=0, tiled=True)
+    numbers, hits = call(
+        partial(numbers_kernel, groups),
+        "numbers",
         1,
-        [
-            numbers.reshape(8, number_lanes), hits.reshape(8, span // 8),
-            attn_in, attn_out, ffn_up, ffn_down, norms,
-        ],
+        [numbers.reshape(8, number_lanes), hits.reshape(8, span // 8)],
         [
             shape_of((groups, 8, number_lanes), jnp.int32),
             shape_of((groups, 8, span // 8), jnp.int32),
-            shape_of((part_width, early_wide), bf16),
-            shape_of((part_width, dec_wide), bf16),
         ],
-        [pltpu.VMEM((128, 128), f32), sems((2, 2, groups - 1)), sems((2,))],
+        [sems((2, 2, groups - 1)), sems((2,))],
         0,
     )
     hits = hits.reshape(groups, span)
-    w_early = lax.all_gather(mine_early, "dp", axis=0, tiled=True)
-    w_dec = lax.all_gather(mine_dec, "dp", axis=0, tiled=True)
     numbers = numbers.reshape(groups, 8 * number_lanes)
     all_labels = numbers[:, enc_len:tokens]
     all_positions = numbers[:, tokens : tokens + loss_count]
@@ -1731,92 +1790,89 @@
     token_count = jnp.sum(all_counted)
 
     picked, across = pick_rows(hits, groups * tokens, embedding.T, groups * chunk)
-    looked, table_zero = call(
+    place_enc = positions_numpy(enc_len, model_width)
+    place_dec = positions_numpy(dec_len, model_width)
+    enc_macs, dec_macs = enc_len * model_width, dec_len * model_width
+    total_enc, total_dec = total_scratch(enc_len, model_width), total_scratch(dec_len, model_width)
+    block_shape = (2, 2, 2, part_width)
+    (looked,) = call(
         partial(look_kernel, groups),
         "look",
         2,
-        [picked.reshape(groups, tokens, part_width), across],
-        [
-            shape_of((tokens, model_width), bf16),
-            shape_of((groups, part_width, table_cuts[0]), bf16),
-        ],
+        [picked.reshape(groups, tokens, part_width)],
+        [shape_of((tokens, model_width), bf16)],
         [
             pltpu.VMEM((tokens // 4, model_width), bf16),
             pltpu.VMEM((groups, tokens // 2, part_width), bf16),
             pltpu.VMEM((groups, tokens // 4, part_width), bf16),
             pltpu.VMEM((groups, tokens // 4, part_width), bf16),
             sems((2, groups + 3)),
-            sems((2, groups)),
         ],
         0,
-        (1,),
-        (1,),
-    )
-
-
-    place_enc = positions_numpy(enc_len, model_width)
-    place_dec = positions_numpy(dec_len, model_width)
-    enc_macs, dec_macs = enc_len * model_width, dec_len * model_width
-    total_enc, total_dec = total_scratch(enc_len, model_width), total_scratch(dec_len, model_width)
+    )
+    table_zero = across.reshape(part_width, groups, chunk)[:, :, : table_cuts[0]]
+    table_zero = lax.all_to_all(table_zero.transpose(1, 0, 2), "dp", 0, 0)
+    forward_inputs = [looked, place_enc, place_dec, w_early, across]
+    forward_outputs = [
+        shape_of((groups, part_width, sum(table_cuts[1:3])), bf16),
+        shape_of((3, own, model_width), bf16),
+        shape_of((16, model_width), f32),
+        shape_of((enc_len, 3 * own), bf16),
+        shape_of((enc_len, own), bf16),
+        shape_of((enc_len, 128), f32),
+        shape_of((enc_len, model_width), f32),
+        shape_of((enc_len, own_up), f32),
+        shape_of((enc_len, model_width), f32),
+        shape_of((enc_len, model_width), bf16),
+        shape_of((dec_len, 3 * own), bf16),
+        shape_of((dec_len, own), bf16),
+        shape_of((dec_len, 128), f32),
+        shape_of((dec_len, model_width), f32),
+    ]
     (
-        qkv_enc, context_enc, logs_enc, stream_enc,
+        table_one, out_rows, norm_values,
+        qkv_enc, context_enc, logs_enc, stream_enc, pre_enc, stream_two, memory,
         qkv_dec, context_dec, logs_dec, stream_dec,
-        out_rows, norm_values, table_one,
     ) = call(
-        partial(first_kernel, groups, shares, table_starts[1], first_wide),
-        "first",
+        partial(
+            forward_kernel, groups, shares, table_cuts[0], table_cuts[1:3], len(forward_inputs),
+            len(forward_outputs),
+        ),
+        "forward",
         3,
-        [looked, place_enc, place_dec, w_early, across],
+        forward_inputs,
+        forward_outputs,
         [
-            shape_of((enc_len, 3 * own), bf16),
-            shape_of((enc_len, own), bf16),
-            shape_of((enc_len, 128), f32),
-            shape_of((enc_len, model_width), f32),
-            shape_of((dec_len, 3 * own), bf16),
-            shape_of((dec_len, own), bf16),
-            shape_of((dec_len, 128), f32),
-            shape_of((dec_len, model_width), f32),
-            shape_of((3, own, model_width), bf16),
-            shape_of((16, model_width), f32),
-            shape_of((groups, part_width, table_cuts[1]), bf16),
-        ],
-        [
-            sems((2, groups)),
+            sems((2, 2, groups)),
+            sems((3,)),
+            sems((2,)),
+            pltpu.VMEM((model_width, first_wide), bf16),
+            pltpu.VMEM((model_width, enc_wide), bf16),
+            pltpu.VMEM((enc_len, model_width), f32),
+            pltpu.VMEM((enc_len, own_up), f32),
+            pltpu.VMEM((enc_len, model_width), f32),
             pltpu.VMEM((shares, own, in_wide), bf16),
             sems((2, shares - 1)),
             sems,
-        ]
-        + total_enc
-        + total_dec,
-        8 * (enc_macs + dec_macs) * own,
-        (4,),
-        (10,),
-    )
-    pre_enc, stream_two, memory, table_two = call(
-        partial(enc_feed_kernel, groups, table_starts[2], first_wide),
-        "enc_feed",
+            *total_dec,
+            *total_enc,
+            *total_enc[1:],
+        ],
+        8 * enc_macs * own_up,
+        (3, 4),
+        (0, 6, 7, 8),
+    )
+    (
+        table_two, q_cross, kv_cross, context_cross, logs_cross, stream_mid, pre_dec, stream_out, selected,
+    ) = call(
+        partial(dec_kernel, groups, sum(table_cuts[:3])),
+        "dec",
         4,
-        [stream_enc, norm_values, w_early, across],
         [
-            shape_of((enc_len, own_up), f32),
-            shape_of((enc_len, model_width), f32),
-            shape_of((enc_len, model_width), bf16),
-            shape_of((groups, part_width, table_cuts[2]), bf16),
+            stream_dec, memory, norm_values, out_rows, loss_positions.reshape(-1, 1), w_dec, across,
         ],
-        [sems((2, groups)), pltpu.VMEM((model_width, own_up + model_width), bf16), sems] + total_enc,
-        4 * enc_macs * own_up,
-        (2, 3),
-        (3,),
-    )
-    (
-        q_cross, kv_cross, context_cross, logs_cross, stream_mid, pre_dec, stream_out, selected,
-        table_three,
-    ) = call(
-        partial(dec_kernel, groups, table_starts[3]),
-        "dec",
-        5,
-        [stream_dec, memory, norm_values, w_dec, out_rows, loss_positions.reshape(-1, 1), across],
         [
+            shape_of((groups, part_width, table_cuts[3]), bf16),
             shape_of((dec_len, own), bf16),
             shape_of((enc_len, 2 * own), bf16),
             shape_of((dec_len, own), bf16),
@@ -1825,18 +1881,19 @@
             shape_of((dec_len, own_up), f32),
             shape_of((dec_len, model_width), f32),
             shape_of((groups, loss_count, model_width), bf16),
-            shape_of((groups, part_width, table_cuts[3]), bf16),
         ],
         [
+            pltpu.VMEM((model_width, dec_wide), bf16),
+            sems,
+            sems((2, groups)),
             pltpu.VMEM((loss_count, model_width), bf16),
             sems((2, groups - 1)),
-            sems((2, groups)),
-        ]
-        + total_dec
-        + total_dec,
-        4 * dec_macs * own_up + 8 * enc_macs * own,
-        (6,),
-        (8,),
+            *total_dec,
+            *total_dec[1:],
+        ],
+        8 * dec_macs * own_up,
+        (5, 6),
+        (0,),
     )
 
     rows_all = groups * loss_count
@@ -1844,7 +1901,8 @@
     targets = all_targets - first_row
     inside = (targets >= 0) & (targets < jnp.minimum(chunk, shard_rows - group * chunk))
     targets = jnp.where(inside, targets, -1)[:, None]
-    loss, grad_selected, head_grad = call(
+    head_cut = chunk // 8
+    loss, grad_selected, head_grad, head_zero = call(
         partial(head_kernel, groups, shares, shard_rows),
         "head",
         6,
@@ -1853,7 +1911,6 @@
             table_zero.reshape(model_width, -1),
             table_one.reshape(model_width, -1),
             table_two.reshape(model_width, -1),
-            table_three.reshape(model_width, -1),
             targets,
             (all_counted / token_count)[:, None],
             all_counted[None, :],
@@ -1862,8 +1919,10 @@
             shape_of((1, 128), f32),
             shape_of((loss_count, model_width), bf16),
             shape_of((model_width, chunk), bf16),
+            shape_of((groups, part_width, head_cut), bf16),
         ],
         [
+            sems((2, groups)),
             pltpu.VMEM((rows_all, chunk), f32),
             pltpu.VMEM((rows_all, chunk), bf16),
             pltpu.VMEM((rows_all, 128), f32),
@@ -1879,13 +1938,13 @@
             sems((2, groups + shares)),
         ],
         6 * rows_all * chunk * model_width,
+        (),
+        (3,),
     )
     loss_sum = loss[0, 0]
     head_grad = head_grad.reshape(groups, part_width, chunk)
     late_wide = dec_wide + 2 * in_wide
-    norm_start = dec_wide + in_wide + own_in
     quarter = tokens // shares
-    block_shape = (2, 2, 2, part_width)
     back_inputs = [
         grad_selected, loss_positions.reshape(1, -1), stream_out, stream_mid, pre_dec, norm_values, w_dec,
         out_rows, memory, stream_dec, q_cross, kv_cross, context_cross, logs_cross,
@@ -1894,16 +1953,16 @@
         head_grad,
     ]
 
-    head_grad, grad_tokens, dec_shares, late_own, dense_squares = call(
+    head_one, grad_tokens, dec_shares, late_own, dense_squares = call(
         partial(
-            back_kernel, groups, shares, first_wide, norm_start, norm_rows, len(back_inputs), 5
+            back_kernel, groups, shares, first_wide, len(back_inputs), 5
         ),
         "backward",
         7,
         back_inputs,
         [
-            shape_of((groups, part_width, chunk), bf16),
-            shape_of((shares, groups, quarter, part_width), bf16),
+            shape_of((groups, part_width, chunk - head_cut), bf16),
+            shape_of((shares, groups, quarter + 16, part_width), bf16),
             shape_of((shares, part_width, dec_wide), bf16),
             shape_of((part_width, late_wide), bf16),
             shape_of((1, 128), f32),
@@ -1937,11 +1996,10 @@
             pltpu.VMEM((8, model_width), f32),
             pltpu.VMEM((8, model_width), f32),
             pltpu.VMEM((8, model_width), f32),
-            pltpu.VMEM((128, model_width), f32),
-            pltpu.VMEM((model_width, 128), f32),
+            pltpu.VMEM((16, model_width), f32),
             pltpu.VMEM((shares, own, in_wide), bf16),
             sems((2, 2, shares - 1)),
-            pltpu.VMEM((groups, tokens, part_width), bf16),
+            pltpu.VMEM((groups, tokens + 16 * shares, part_width), bf16),
             sems((2, groups)),
             sems((2, 3)),
             sems((2, 3)),
@@ -1960,8 +2018,12 @@
         (0, 1, 2),
     )
     late_shares = lax.all_gather(late_own, "vocab", axis=0, tiled=False)
-    g_embedding, embedding_squares = spread_rows(hits, grad_tokens, head_grad)
-    g_embedding = g_embedding[:, :shard_rows].T
+    g_embedding, embedding_squares = spread_rows(
+        hits, groups * tokens, grad_tokens, (head_zero, head_one)
+    )
+    g_embedding = g_embedding[:, :shard_rows].astype(f32).T
+    g_norms = jnp.sum(grad_tokens[0, :, quarter : quarter + norm_rows].astype(f32), axis=0)
+    dense_squares = dense_squares + jnp.sum(g_norms * g_norms) / (shares * dense_squares.shape[1])
     (squares,) = call(
         partial(squares_kernel, groups, shares),
         "squares",
@@ -1998,7 +2060,7 @@
 
             @pl.when(pl.program_id(0) == matrix)
             def _(ref=ref):
-                wide_ref[...] = ref[pl.program_id(1), :, own_up : own_up + model_width]
+                wide_ref[...] = ref[pl.program_id(1)]
 
     scale = factor.reshape(1)
     new_in = dense_update(
@@ -2008,12 +2070,13 @@
         "adam_out", RATES[2], place_out, scale, grad_pair[:1], attn_out, attn_out_first, attn_out_second, 1
     )
     new_up = dense_update(
-        "adam_up", RATES[3], place_up, scale, grad_pair, ffn_up, ffn_up_first, ffn_up_second, 2
+        "adam_up", RATES[3], place_up, scale, grad_pair, ffn_up, ffn_up_first, ffn_up_second, 2,
+        (own_up, 0),
     )
     new_down = dense_update(
-        "adam_down", RATES[4], place_down, scale, grad_pair, ffn_down, ffn_down_first, ffn_down_second, shares
-    )
-    g_norms = late_own[:, norm_start : norm_start + norm_rows].astype(f32).T
+        "adam_down", RATES[4], place_down, scale, grad_pair, ffn_down, ffn_down_first, ffn_down_second, shares,
+        (model_width, 1),
+    )
     new_embedding = adam_update(
         embedding, embedding_first, embedding_second, g_embedding, factor, RATES[0]
     )

time: 666 us -> 645 us (0.968)
  Pallas kernels: 578 us -> 556 us
  waiting for transfers between devices: 25.1 us -> 17.3 us
    pallas_call x8 -> x7, Pallas kernels: 477 us -> 458 us  [call(): pl.pallas_call(kernel, out_shape=tuple(out_shape), in_specs=in_vmem(len(i...]
    all_gather x1, waiting for transfers between devices: 11.9 us -> 0.01 us  [local(): w_early = lax.all_gather(mine_early, 'dp', axis=0, tiled=True)]
  transfers between devices with their start and end apart: 3 -> 4, of which waited for: 2 -> 2; matrix products, arithmetic and copies ran while one was open for 5% -> 6% of each run, Pallas kernels for 27% -> 37%
where the time goes in v3:
time: 645 us; the launch traced here: 638 us
  Pallas kernels  556 us (86%)
  other arithmetic  27.5 us (4%)
  between operations  19.3 us (3%)
  waiting for transfers between devices  17.3 us (3%)
  local copies, waits for them, and re-layouts  12.3 us (2%)
    pallas_call x7, Pallas kernels, call(): pl.pallas_call(kernel, out_shape=tuple(out_shape), in_specs=in_vmem(len(i...  458 us
    pallas_call x4, Pallas kernels, dense_update(): pl.pallas_call(partial(dense_kernel, rate, place_grads), grid=(matrices,...  31.2 us
    pallas_call x1, Pallas kernels, spread_rows(): pl.pallas_call(spread_kernel, out_shape=(jax.ShapeDtypeStruct((width, chu...  29.9 us
    pallas_call x1, Pallas kernels, pick_rows(): pl.pallas_call(pick_kernel, out_shape=(jax.ShapeDtypeStruct((count, width...  28.7 us
    sub x2, other arithmetic, adam_update(): return (weight - rate * (corrected + DECAY * weight), new_first, new_second)  23.1 us
    all_gather x1, waiting for transfers between devices, local(): w_dec = lax.all_gather(mine_dec, 'dp', axis=0, tiled=True)  13.9 us
  transfers between devices with their start and end apart: 4, of which 2 were waited for; matrix products, arithmetic and copies ran while one was open for 6% of the time, Pallas kernels for 37%

profile of v3, /device:TPU:0, one launch (start us, length us, event | category | flops | bytes accessed | tf_op | source)
XLA Modules:
  0.0 638.2 jit_solution(5291754809987436504)
XLA Ops:
  7.2 0.0 copy-start.7
  7.2 0.0 copy-start.5
  7.2 0.0 copy-start.6
  7.2 0.0 all-gather.5.cloned.1.call-start
  7.3 4.8 cut_weights.1
  12.0 0.0 all-gather.5.cloned.1.call-update
  12.1 0.0 all-gather.7.cloned.1.call-start
  12.1 0.7 all-gather.7.cloned.1.call-update
  13.5 0.0 copy-done.7
  13.5 0.0 copy-done.5
  13.5 0.7 add_subtract_fusion.ids_ref
  14.2 3.9 list_hits.1
  18.1 0.0 copy-done.6
  18.1 0.1 pad_add_fusion
  18.2 0.6 pad.4
  18.8 11.5 %numbers.1 = (s32[8,8,128]{2,1,0:T(8,128)}, s32[8,8,128]{2,1,0:T(8,128)}) custom-call(s32[8,128]{1,0:T(8,128)} %bitcast.60, s32[8,128]{1,0:T(8,128)} %bitcast.59), custom_call_target="tpu_custom_call" | custom-call | bytes 73728 | tf_op jit(solution)/shard_map/numbers/pallas_call | solution.py:797
  30.3 1.4 copy.75
  31.7 28.7 %pick_rows.1 = (bf16[6144,96]{1,0:T(8,128)(2,1)}, bf16[96,24576]{1,0:T(8,128)(2,1)}) custom-call(s32[8,1024]{1,0:T(8,128)} %bitcast.51, f32[96,24026]{1,0:T(8,128)} %bitcast.46), custom_call_target="tpu_custom_call" | custom-call | tf_op jit(solution)/shard_map/pick_rows/pallas_call | solution.py:488
  60.4 5.3 copy.68
  65.7 0.0 copy-start.2
  65.7 0.1 slice.36
  65.8 1.2 copy.73
  67.0 5.3 all-to-all-start
  72.3 0.0 all-gather.9.cloned.1.call-start
  72.4 0.0 copy-done.2
  72.4 70.1 %look.1.refs_0_.refs_18_ = bf16[768,768]{1,0:T(8,128)(2,1)} custom-call(bf16[8,768,96]{2,1,0:T(8,128)(2,1)} %bitcast.49), custom_call_target="tpu_custom_call" | custom-call | bytes 2359296 | tf_op jit(solution)/shard_map/look/pallas_call | solution.py:797
  142.6 0.7 copy.60.positions_ref
  143.3 0.3 select_reduce_fusion
  143.6 0.2 sub.39
  143.8 0.2 slice_reduce_fusion
  144.0 0.1 fusion.6
  144.1 0.6 convert_reduce_fusion.1
  145.4 0.9 div.59.weights_ref
  146.3 0.7 reshape.149.counted_ref
  146.9 0.7 and_select_fusion.targets_ref
  147.7 60.5 %forward.1 = (bf16[8,96,1152]{2,1,0:T(8,128)(2,1)}, bf16[3,192,768]{2,1,0:T(8,128)(2,1)}, f32[16,768]{1,0:T(8,128)}, bf16[512,576]{1,0:T(8,128)(2,1)}, bf16[512,...) custom-call(bf16[768,768]{1,0:T(8,128)(2,1)} %look.1.refs_0_.refs_18, ...), custom_call_target="tpu_custom_call" | custom-call | flops 2415919104 | bytes 24133632 | tf_op jit(solution)/shard_map/forward/pallas_call | solution.py:797
  208.2 13.9 %all-gather.7.cloned.1.call-done.w_dec_hbm.refs_6_ = bf16[768,2176]{1,0:T(8,128)(2,1)} async-done(((bf16[96,2176]{1,0:T(8,128)(2,1)}), bf16[768,2176]{1,0:T(8,128)(2,1)}) %all-gather.7.cloned.1.call-update) | async-done | bytes 3342352 | tf_op jit(solution)/shard_map/all_gather | solution.py:1769
  222.1 58.6 %dec.1 = (bf16[8,96,1152]{2,1,0:T(8,128)(2,1)}, bf16[256,192]{1,0:T(8,128)(2,1)}, bf16[512,384]{1,0:T(8,128)(2,1)}, bf16[256,192]{1,0:T(8,128)(2,1)}, f32[256,12...) custom-call(f32[256,768]{1,0:T(8,128)} %get-tuple-element.77.stream_, ...), custom_call_target="tpu_custom_call" | custom-call | flops 1207959552 | bytes 16204032 | tf_op jit(solution)/shard_map/dec/pallas_call | solution.py:797
  280.6 0.0 all-to-all-done
  280.7 0.0 copy-start
  280.7 1.0 copy-done
  281.7 53.6 %head.1 = (f32[1,128]{1,0:T(1,128)}, bf16[64,768]{1,0:T(8,128)(2,1)}, bf16[768,3072]{1,0:T(8,128)(2,1)}, bf16[8,96,384]{2,1,0:T(8,128)(2,1)}) custom-call(bf16[512,768]{1,0:T(8,128)(2,1)} %bitcast.66, bf16[768,768]{1,0:T(8,128)(2,1)} %bitcast.50, bf16[768,1152]{1,0:T(8,128)(2,1)} %bitcast.64, bf16[768,1152]{1,0:T(8,128)(2,1)} %bitcast.65, ...), custom_call_target="tpu_custom_call" | custom-call | flops 7247757312 | bytes 10918400 | tf_op jit(solution)/shard_map/head/pallas_call | solution.py:797
  335.2 188.3 %backward.1 = (bf16[8,96,2688]{2,1,0:T(8,128)(2,1)}, bf16[4,8,208,96]{3,2,1,0:T(8,128)(2,1)}, bf16[4,96,2176]{2,1,0:T(8,128)(2,1)}, bf16[96,3456]{1,0:T(8,128)(2,1)}, f32[1,128]{1,0:T(1,128)}) custom-call(bf16[64,768]{1,0:T(8,128)(2,1)} %get-tuple-element.87.refs_0_, s32[1,64]{1,0:T(1,128)} %refs_1_.3, f32[256,768]{1,0:T(8,128)} %get-tuple-element.88.refs_2_, ...), custom_call_target="tpu_custom_call" | custom-call | flops 7247757312 | bytes 36627200 | tf_op jit(solution)/shard_map/backward/pallas_call | solution.py:797
  523.5 0.0 copy-start.8
  523.5 0.0 copy-start.1
  523.5 0.0 copy-start.3
  523.5 0.0 copy-start.4
  523.6 0.8 convert_reduce_fusion
  524.3 0.6 multiply_reduce_fusion
  524.9 29.9 %spread_rows.1 = (bf16[96,24576]{1,0:T(8,128)(2,1)}, f32[1,128]{1,0:T(1,128)}) custom-call(s32[8,1024]{1,0:T(8,128)} %bitcast.52, bf16[4,8,208,96]{3,2,1,0:T(8,128)(2,1)} %get-tuple-element.105.grads_ref, bf16[8,96,384]{2,1,0:T(8,128)(2,1)} %get-tuple-element.106.zero_ref, bf16[8,96,2688]{2,1,0:T(8,128)(2,1)} %get-tuple-element.107.one_ref), custom_call_target="tpu_custom_call" | custom-call | tf_op jit(solution)/shard_map/spread_rows/pallas_call | solution.py:547
  555.5 0.0 copy-done.8
  555.5 0.5 broadcast_add_fusion.dense_ref
  556.1 15.3 %squares.1 = f32[1,128]{1,0:T(1,128)} custom-call(f32[1,128]{1,0:T(1,128)} %get-tuple-element.108.embedding_ref, f32[1,128]{1,0:T(1,128)} %broadcast_add_fusion.dense_ref), custom_call_target="tpu_custom_call" | custom-call | bytes 1536 | tf_op jit(solution)/shard_map/squares/pallas_call | solution.py:797
  572.0 0.0 all-gather.9.cloned.1.call-update
  572.1 0.0 copy-done.1
  572.1 0.0 copy-done.3
  572.1 0.0 copy-done.4
  572.1 0.6 multiply_subtract_fusion.1
  572.7 22.5 %multiply_subtract_fusion = (f32[24026,96]{0,1:T(8,128)}, f32[24026,96]{0,1:T(8,128)}, f32[24026,96]{0,1:T(8,128)}) fusion(f32[24026,96]{0,1:T(8,128)} %param.28, f32[]{:T(128)} %min_shard_map.3, bf16[96,24576]{1,0:T(8,128)(2,1)} %get-tuple-element.110, f32[24026,96]{0,1:T(8,128)} %param.34, f32[24026,96]{0,1:T(8,128)} %param.40), kind=kLoop, calls=%fused_computation.4 | loop fusion | flops 39210432 | bytes 59968900 | tf_op jit(solution)/shard_map/sub | solution.py:214
  595.2 2.7 all-gather.9.cloned.1.call-done
  597.9 5.2 adam_out.1
  603.1 9.7 %adam_in.1 = (f32[3,96,2304]{2,1,0:T(8,128)}, f32[3,96,2304]{2,1,0:T(8,128)}, f32[3,96,2304]{2,1,0:T(8,128)}) custom-call(f32[1]{0:T(128)} %bitcast.17.factor_ref, bf16[4,96,3456]{2,1,0:T(8,128)(2,1)} %bitcast.43, bf16[4,96,2176]{2,1,0:T(8,128)(2,1)} %get-tuple-element.112.refs_1_, f32[3,96,2304]{2,1,0:T(8,128)} %refs_2_.5, f32[3,96,2304]{2,1,0:T(8,128)} %refs_3_.4, ...), custom_call_target="tpu_custom_call" | custom-call | tf_op jit(solution)/shard_map/adam_in/pallas_call | solution.py:1603
  612.9 7.6 %adam_up.1 = (f32[2,96,3072]{2,1,0:T(8,128)}, f32[2,96,3072]{2,1,0:T(8,128)}, f32[2,96,3072]{2,1,0:T(8,128)}) custom-call(f32[1]{0:T(128)} %bitcast.17.factor_ref, bf16[4,96,3456]{2,1,0:T(8,128)(2,1)} %bitcast.44, bf16[4,96,2176]{2,1,0:T(8,128)(2,1)} %get-tuple-element.112.refs_1_, f32[2,96,3072]{2,1,0:T(8,128)} %refs_2_.7, f32[2,96,3072]{2,1,0:T(8,128)} %refs_3_.6, ...), custom_call_target="tpu_custom_call" | custom-call | tf_op jit(solution)/shard_map/adam_up/pallas_call | solution.py:1603
  620.4 8.7 %adam_down.1 = (f32[2,384,768]{2,1,0:T(8,128)}, f32[2,384,768]{2,1,0:T(8,128)}, f32[2,384,768]{2,1,0:T(8,128)}) custom-call(f32[1]{0:T(128)} %bitcast.17.factor_ref, bf16[4,96,3456]{2,1,0:T(8,128)(2,1)} %bitcast.45, bf16[4,96,2176]{2,1,0:T(8,128)(2,1)} %get-tuple-element.112.refs_1_, f32[2,384,768]{2,1,0:T(8,128)} %refs_2_.8, f32[2,384,768]{2,1,0:T(8,128)} %refs_3_.7, ...), custom_call_target="tpu_custom_call" | custom-call | tf_op jit(solution)/shard_map/adam_down/pallas_call | solution.py:1603
  (8 shorter events, 0.0 us)
Async XLA Ops:
  7.2 6.3 copy-start.7
  7.2 6.3 copy-start.5
  7.2 10.9 %copy-start.6 = (s32[1,64]{1,0:T(1,128)S(1)}, s32[1,64]{1,0:T(1,128)}, u32[]{:S(2)}) copy-start(s32[1,64]{1,0:T(1,128)} %refs_1_.3) | copy-start | bytes 772
  7.2 140.5 %all-gather.5.cloned.1.call-start = ((), (), s32[]{:S(2)}) async-start(), calls=%async_computation.1 | async-start | bytes 5971968 | tf_op jit(solution)/shard_map/all_gather | solution.py:1768
  12.1 210.0 %all-gather.7.cloned.1.call-start = ((), (), s32[]{:S(2)}) async-start(), calls=%async_computation.2 | async-start | bytes 3760128 | tf_op jit(solution)/shard_map/all_gather | solution.py:1769
  65.7 6.7 %copy-start.2 = (s32[8,8,128]{2,1,0:T(8,128)S(1)}, s32[8,8,128]{2,1,0:T(8,128)}, u32[]{:S(2)}) copy-start(s32[8,8,128]{2,1,0:T(8,128)} %get-tuple-element.85) | copy-start | bytes 98308
  67.0 213.6 %all-to-all-start = ((bf16[8,96,768]{2,1,0:T(8,128)(2,1)}), bf16[8,96,768]{2,1,0:T(8,128)(2,1)S(1)}, u32[]{:S(2)}, u32[]{:S(2)}) async-start(bf16[8,96,768]{2,1,0:T(8,128)(2,1)} %bitcast.34), calls=%async_computation | async-start | bytes 2359296 | tf_op jit(solution)/shard_map/all_to_all | solution.py:1814
  72.3 525.6 %all-gather.9.cloned.1.call-start = ((), (), s32[]{:S(2)}) async-start(), calls=%async_computation.3 | async-start | bytes 3317760 | tf_op jit(solution)/shard_map/all_gather | solution.py:2020
  280.7 1.0 copy-start
  523.5 32.0 %copy-start.8 = (f32[1,128]{1,0:T(1,128)S(1)}, f32[1,128]{1,0:T(1,128)}, u32[]{:S(2)}) copy-start(f32[1,128]{1,0:T(1,128)} %get-tuple-element.109) | copy-start | bytes 1540
  523.5 48.5 %copy-start.1 = (f32[14,96]{1,0:T(8,128)S(1)}, f32[14,96]{1,0:T(8,128)}, u32[]{:S(2)}) copy-start(f32[14,96]{1,0:T(8,128)} %norms_ref.1) | copy-start | bytes 16132
  523.5 48.5 %copy-start.3 = (f32[14,96]{1,0:T(8,128)S(1)}, f32[14,96]{1,0:T(8,128)}, u32[]{:S(2)}) copy-start(f32[14,96]{1,0:T(8,128)} %param.39) | copy-start | bytes 16132
  523.5 48.5 %copy-start.4 = (f32[14,96]{1,0:T(8,128)S(1)}, f32[14,96]{1,0:T(8,128)}, u32[]{:S(2)}) copy-start(f32[14,96]{1,0:T(8,128)} %param.45) | copy-start | bytes 16132
  620.4 8.7 %copy-start.9 = (f32[1,128]{1,0:T(1,128)S(1)}, f32[1,128]{1,0:T(1,128)}, u32[]{:S(2)}) copy-start(f32[1,128]{1,0:T(1,128)} %get-tuple-element.86) | copy-start | bytes 1540
Sparse Core Ops, SparseCore 0:
  12.2 117.8 all-gather.4
  132.8 89.1 all-gather.6
  572.2 25.6 all-gather.8

commit v4 on v3

--- a/solution.py
+++ b/solution.py
@@ -454,7 +454,7 @@
         lax.fori_loop(0, lists_ref[group, span - 1], one, 0)
 
 
-def pick_kernel(lists_ref, table_ref, out_ref, across_ref, wide_ref, turned_ref):
+def pick_kernel(lists_ref, table_ref, out_ref, across_ref, piece_ref, wide_ref, turned_ref):
     tokens = wide_ref.shape[0] // lists_ref.shape[0]
     width, rows = table_ref.shape
     total = across_ref.shape[1]
@@ -467,6 +467,11 @@
         if high < low + step:
             across_ref[:, high : low + step] = jnp.zeros((width, low + step - high), jnp.bfloat16)
 
+    groups, _, columns = piece_ref.shape
+    for group in range(groups):
+        start = group * (total // groups)
+        piece_ref[group] = across_ref[:, start : start + columns]
+
     def turn(piece, carry):
         for part in range(8):
             start = pl.multiple_of(piece * step + part * 128, 128)
@@ -483,19 +488,21 @@
     out_ref[...] = wide_ref[...].astype(jnp.bfloat16)
 
 
-def pick_rows(lists, count, table, total):
+def pick_rows(lists, count, table, total, columns):
     width = table.shape[0]
     return pl.pallas_call(
         pick_kernel,
         out_shape=(
             jax.ShapeDtypeStruct((count, width), jnp.bfloat16),
             jax.ShapeDtypeStruct((width, total), jnp.bfloat16),
+            jax.ShapeDtypeStruct((lists.shape[0], width, columns), jnp.bfloat16),
         ),
         in_specs=[
             pl.BlockSpec(memory_space=pltpu.SMEM),
             pl.BlockSpec(memory_space=pltpu.VMEM),
         ],
         out_specs=(
+            pl.BlockSpec(memory_space=pltpu.VMEM),
             pl.BlockSpec(memory_space=pltpu.VMEM),
             pl.BlockSpec(memory_space=pltpu.VMEM),
         ),
@@ -751,6 +758,33 @@
             self.blocks[self.high, self.low, self.place].astype(jnp.float32)
             + self.far_in[...].astype(jnp.float32)
         )
+
+
+class Rows:
+    def __init__(self, value_ref, send_ref, recv_ref, sems):
+        group, share = lax.axis_index("dp"), lax.axis_index("vocab")
+        self.recv = recv_ref
+        shares, _, own = send_ref.shape
+        for piece in range(shares):
+            send_ref[piece] = value_ref[:, piece * own : (piece + 1) * own]
+        self.copies = [
+            send(send_ref.at[peer[1]], recv_ref.at[share], sems.at[0, step], sems.at[1, step], peer)
+            for step, peer in enumerate(share_peers(group, share, shares))
+        ]
+        keep = pltpu.make_async_copy(send_ref.at[share], recv_ref.at[share], sems.at[0, shares - 1])
+        keep.start()
+        self.copies.append(keep)
+
+    def put(self, grads_ref, start):
+        for copy in self.copies:
+            copy.wait()
+        shares, _, own = self.recv.shape
+        part = grads_ref.shape[3]
+        for piece in range(shares):
+            for half in range(2):
+                grads_ref[piece // 2, piece % 2, half, :, start : start + own] = self.recv[
+                    piece, half * part : (half + 1) * part
+                ]
 
 
 class Late:
@@ -1267,10 +1301,11 @@
         grad_ref, grad_enc_ref,
         context_ref, gq_ref, gkv_ref, gqkv_ref, gqkv_enc_ref, context_enc_grad_ref,
         g_enc_ref, g_self_ref, g_cross_ref, rows_dec_ref, rows_mid_ref, rows_ref,
-        norm_rows_ref, blocks_ref, block_sems, cut_ref, token_sems, share_sems, dec_sems, dec_own_ref,
+        norm_rows_ref, block_sems, cut_ref, token_sems, share_sems, dec_sems, dec_own_ref,
         local_sems,
-    ) = scratch[:37]
-    rest = scratch[37:]
+    ) = scratch[:36]
+    row_refs = scratch[36:42]
+    rest = scratch[42:]
     stream_ref = pre_enc_ref
     small_one, large_one = rest[:4], rest[4:8]
     small_two, large_two = small_one[:1] + rest[8:11], large_one[:1] + rest[11:14]
@@ -1332,15 +1367,15 @@
         w_early_hbm.at[:, pl.ds(0, first_wide)], w_ref.at[:, pl.ds(0, first_wide)], load_sems.at[9]
     )
     g_cross_ref[...] = lowered(contract_rows(context_cross_ref[...], grad_low))
+    cross_rows = Rows(g_cross_ref, row_refs[0], row_refs[1], block_sems.at[0])
     memory_total.middle()
     cross_total.middle()
     load_dec()
     load_memory()
     normed, _ = norm_forward(stream_dec_ref[...], *gain_of(norms_ref, 4))
-    gap = dec_grads_ref.shape[4] - in_start - 3 * own
     put_grads(dec_grads_ref, in_start, contract_rows(lowered(normed), gq_ref[...]))
     put_grads(dec_grads_ref, in_start + own, contract_rows(memory_ref[...], gkv_ref[...]))
-    put_grads(dec_grads_ref, in_start + 3 * own, jnp.zeros((width, gap), jnp.float32))
+    cross_rows.put(dec_grads_ref, in_start + 3 * own)
     dec_line.begin()
     memory_total.last()
     cross_total.last()
@@ -1369,13 +1404,14 @@
     w_start = first_wide // 3
     self_total.begin(times_transposed(gqkv_ref[...], w_ref[:, w_start : w_start + 3 * own]))
     g_self_ref[...] = lowered(contract_rows(context_dec_ref[...], grad_low))
+    self_rows = Rows(g_self_ref, row_refs[2], row_refs[3], block_sems.at[1])
     self_total.middle()
     load_looked()
     enc_len = stream_enc_ref.shape[0]
     stream_dec_ref[...] = stream_of(looked_ref, enc_len, place_dec_ref)
     normed, _ = norm_forward(stream_dec_ref[...], *gain_of(norms_ref, 3))
     put_grads(mid_grads_ref, in_start, contract_rows(lowered(normed), gqkv_ref[...]))
-    put_grads(mid_grads_ref, in_start + 3 * own, jnp.zeros((width, gap), jnp.float32))
+    self_rows.put(mid_grads_ref, in_start + 3 * own)
     mid_line.begin()
     grad_enc_ref[...] = norm_step(
         grad_enc_ref, stream_enc_ref, norms_ref, 1, feed_total.finish(), rows_mid_ref, 2
@@ -1403,32 +1439,7 @@
     total = Total(large_one)
     grad_low = lowered(grad_enc_ref[...])
     g_enc_ref[...] = lowered(contract_rows(context_enc_ref[...], grad_low))
-    wide = blocks_ref.shape[2]
-    in_wide = last_grads_ref.shape[4] - wide
-    blocks_ref[...] = jnp.zeros_like(blocks_ref)
-    for piece in range(shares):
-        at = slice(piece * own, (piece + 1) * own)
-        for matrix, source in enumerate((g_enc_ref, g_self_ref, g_cross_ref)):
-            blocks_ref[piece, :, matrix * own : (matrix + 1) * own] = source[:, at]
-    copies = []
-    for half in range(2):
-        target = last_grads_ref.at[share // 2, lax.rem(share, 2), half, :, pl.ds(in_wide, wide)]
-        source_rows = pl.ds(half * part, part)
-        for step, peer in enumerate(peers):
-            copies.append(
-                send(
-                    blocks_ref.at[peer[1], source_rows, :],
-                    target,
-                    block_sems.at[half, 0, step],
-                    block_sems.at[half, 1, step],
-                    peer,
-                )
-            )
-        keep = pltpu.make_async_copy(
-            blocks_ref.at[share, source_rows, :], target, local_sems.at[half]
-        )
-        keep.start()
-        copies.append(keep)
+    enc_rows = Rows(g_enc_ref, row_refs[4], row_refs[5], block_sems.at[2])
     context_enc_grad_ref[...] = lowered(times_transposed(grad_low, out_rows_ref[0]))
     heads_backward(
         qkv_enc_ref, qkv_enc_ref, starts, logs_enc_ref, context_enc_grad_ref, gqkv_enc_ref, gqkv_enc_ref, starts,
@@ -1440,9 +1451,7 @@
     normed, _ = norm_forward(stream_ref[...], *gain_of(norms_ref, 0))
     total.middle()
     put_grads(last_grads_ref, 0, contract_rows(lowered(normed), gqkv_enc_ref[...]))
-    put_grads(last_grads_ref, 3 * own, jnp.zeros((width, in_wide - 3 * own), jnp.float32))
-    for copy in copies:
-        copy.wait()
+    enc_rows.put(last_grads_ref, 3 * own)
     last_line.begin()
     dec_line.beside()
     total.last()
@@ -1789,7 +1798,9 @@
     all_counted = (all_positions < all_lengths).reshape(-1).astype(f32)
     token_count = jnp.sum(all_counted)
 
-    picked, across = pick_rows(hits, groups * tokens, embedding.T, groups * chunk)
+    picked, across, table_zero = pick_rows(
+        hits, groups * tokens, embedding.T, groups * chunk, table_cuts[0]
+    )
     place_enc = positions_numpy(enc_len, model_width)
     place_dec = positions_numpy(dec_len, model_width)
     enc_macs, dec_macs = enc_len * model_width, dec_len * model_width
@@ -1810,8 +1821,7 @@
         ],
         0,
     )
-    table_zero = across.reshape(part_width, groups, chunk)[:, :, : table_cuts[0]]
-    table_zero = lax.all_to_all(table_zero.transpose(1, 0, 2), "dp", 0, 0)
+    table_zero = lax.all_to_all(table_zero, "dp", 0, 0)
     forward_inputs = [looked, place_enc, place_dec, w_early, across]
     forward_outputs = [
         shape_of((groups, part_width, sum(table_cuts[1:3])), bf16),
@@ -1943,7 +1953,9 @@
     )
     loss_sum = loss[0, 0]
     head_grad = head_grad.reshape(groups, part_width, chunk)
-    late_wide = dec_wide + 2 * in_wide
+    last_wide = own_in + own
+    back_wide = own_up + model_width + last_wide
+    late_wide = back_wide + last_wide
     quarter = tokens // shares
     back_inputs = [
         grad_selected, loss_positions.reshape(1, -1), stream_out, stream_mid, pre_dec, norm_values, w_dec,
@@ -1963,7 +1975,7 @@
         [
             shape_of((groups, part_width, chunk - head_cut), bf16),
             shape_of((shares, groups, quarter + 16, part_width), bf16),
-            shape_of((shares, part_width, dec_wide), bf16),
+            shape_of((shares, part_width, back_wide), bf16),
             shape_of((part_width, late_wide), bf16),
             shape_of((1, 128), f32),
         ],
@@ -1979,9 +1991,9 @@
             pltpu.VMEM((enc_len, model_width), f32),
             pltpu.VMEM((enc_len, own_up), f32),
             pltpu.VMEM((tokens, model_width), bf16),
-            pltpu.VMEM(block_shape + (dec_wide,), bf16),
-            pltpu.VMEM(block_shape + (dec_wide,), bf16),
-            pltpu.VMEM(block_shape + (2 * in_wide,), bf16),
+            pltpu.VMEM(block_shape + (back_wide,), bf16),
+            pltpu.VMEM(block_shape + (back_wide,), bf16),
+            pltpu.VMEM(block_shape + (last_wide,), bf16),
             pltpu.VMEM((dec_len, model_width), f32),
             pltpu.VMEM((enc_len, model_width), f32),
             pltpu.VMEM((dec_len, own), bf16),
@@ -1997,21 +2009,21 @@
             pltpu.VMEM((8, model_width), f32),
             pltpu.VMEM((8, model_width), f32),
             pltpu.VMEM((16, model_width), f32),
-            pltpu.VMEM((shares, own, in_wide), bf16),
-            sems((2, 2, shares - 1)),
+            sems((3, 2, shares)),
             pltpu.VMEM((groups, tokens + 16 * shares, part_width), bf16),
             sems((2, groups)),
             sems((2, 3)),
             sems((2, 3)),
-            pltpu.VMEM((part_width, dec_wide), bf16),
+            pltpu.VMEM((part_width, back_wide), bf16),
             sems((3,)),
+            *[pltpu.VMEM((shares, own, own), bf16)] * 6,
             *total_dec,
             *total_enc,
             *total_dec[1:],
             *total_enc[1:],
-            *line_scratch(part_width, dec_wide),
-            *line_scratch(part_width, dec_wide),
-            *line_scratch(part_width, 2 * in_wide),
+            *line_scratch(part_width, back_wide),
+            *line_scratch(part_width, back_wide),
+            *line_scratch(part_width, last_wide),
         ],
         16 * (enc_macs + dec_macs) * own_up,
         (6, 7, 8, 9, 14, 15, 16, 17, 18, 19, 27),
@@ -2040,41 +2052,45 @@
     grad_norm = jnp.sqrt(squares[0, 0])
     factor = jnp.minimum(1.0, CLIP / (grad_norm + 1e-06))
     grad_pair = [late_shares, dec_shares]
-    in_start, late_in, late_out = own_up + model_width, dec_wide, dec_wide + in_wide
+    in_start, late_in = own_up + model_width, back_wide
 
     def place_in(wide_ref, late_ref, dec_ref):
         place_columns(3, 0, late_ref, late_in)(wide_ref)
         place_columns(3, 1, late_ref, in_start)(wide_ref)
         place_columns(3, 2, dec_ref, in_start)(wide_ref)
 
-    def place_out(wide_ref, late_ref):
-        for matrix in range(3):
-            place_columns(1, matrix, late_ref, late_out + matrix * own)(wide_ref)
+    def place_out(wide_ref, late_ref, dec_ref):
+        place_columns(1, 0, late_ref, late_in + own_in)(wide_ref)
+        place_columns(1, 1, late_ref, in_start + own_in)(wide_ref)
+        place_columns(1, 2, dec_ref, in_start + own_in)(wide_ref)
 
     def place_up(wide_ref, late_ref, dec_ref):
         place_columns(groups, 0, late_ref, 0)(wide_ref)
         place_columns(groups, 1, dec_ref, 0)(wide_ref)
 
+    down_rows = ffn_down.shape[1] // shares
+
     def place_down(wide_ref, late_ref, dec_ref):
         for matrix, ref in enumerate((late_ref, dec_ref)):
 
             @pl.when(pl.program_id(0) == matrix)
             def _(ref=ref):
-                wide_ref[...] = ref[pl.program_id(1)]
+                for piece in range(shares):
+                    wide_ref[piece * down_rows : (piece + 1) * down_rows] = ref[piece]
 
     scale = factor.reshape(1)
     new_in = dense_update(
         "adam_in", RATES[1], place_in, scale, grad_pair, attn_in, attn_in_first, attn_in_second, 2
     )
     new_out = dense_update(
-        "adam_out", RATES[2], place_out, scale, grad_pair[:1], attn_out, attn_out_first, attn_out_second, 1
+        "adam_out", RATES[2], place_out, scale, grad_pair, attn_out, attn_out_first, attn_out_second, 1
     )
     new_up = dense_update(
         "adam_up", RATES[3], place_up, scale, grad_pair, ffn_up, ffn_up_first, ffn_up_second, 2,
         (own_up, 0),
     )
     new_down = dense_update(
-        "adam_down", RATES[4], place_down, scale, grad_pair, ffn_down, ffn_down_first, ffn_down_second, shares,
+        "adam_down", RATES[4], place_down, scale, grad_pair, ffn_down, ffn_down_first, ffn_down_second, 1,
         (model_width, 1),
     )
     new_embedding = adam_update(

time: 645 us -> 646 us (level)
  Pallas kernels: 556 us -> 567 us
  local copies, waits for them, and re-layouts: 12.3 us -> 5.7 us
    pallas_call x7, Pallas kernels: 458 us -> 466 us  [call(): pl.pallas_call(kernel, out_shape=tuple(out_shape), in_specs=in_vmem(len(i...]
    unnamed x24 -> x22, local copies, waits for them, and re-layouts: 8.95 us -> 2.44 us
  transfers between devices with their start and end apart: 4 -> 4, of which waited for: 2 -> 2; matrix products, arithmetic and copies ran while one was open for 6% -> 5% of each run, Pallas kernels for 37% -> 38%
where the time goes in v4:
time: 646 us; the launch traced here: 640 us
  Pallas kernels  567 us (88%)
  other arithmetic  27.6 us (4%)
  between operations  19.3 us (3%)
  waiting for transfers between devices  15.4 us (2%)
    pallas_call x7, Pallas kernels, call(): pl.pallas_call(kernel, out_shape=tuple(out_shape), in_specs=in_vmem(len(i...  466 us
    pallas_call x1, Pallas kernels, spread_rows(): pl.pallas_call(spread_kernel, out_shape=(jax.ShapeDtypeStruct((width, chu...  31.9 us
    pallas_call x1, Pallas kernels, pick_rows(): pl.pallas_call(pick_kernel, out_shape=(jax.ShapeDtypeStruct((count, width...  30.9 us
    pallas_call x4, Pallas kernels, dense_update(): pl.pallas_call(partial(dense_kernel, rate, place_grads), grid=(matrices,...  29.1 us
    sub x2, other arithmetic, adam_update(): return (weight - rate * (corrected + DECAY * weight), new_first, new_second)  23.3 us
    all_gather x1, waiting for transfers between devices, local(): w_dec = lax.all_gather(mine_dec, 'dp', axis=0, tiled=True)  14.4 us
  transfers between devices with their start and end apart: 4, of which 2 were waited for; matrix products, arithmetic and copies ran while one was open for 5% of the time, Pallas kernels for 38%

profile of v4, /device:TPU:0, one launch (start us, length us, event | category | flops | bytes accessed | tf_op | source)
XLA Modules:
  0.0 640.3 jit_solution(9664238017154984740)
XLA Ops:
  7.2 0.0 copy-start.7
  7.2 0.0 copy-start.5
  7.2 0.0 copy-start.6
  7.2 0.0 all-gather.5.cloned.1.call-start
  7.3 4.8 cut_weights.1
  12.0 0.0 all-gather.5.cloned.1.call-update
  12.1 0.0 all-gather.7.cloned.1.call-start
  12.1 0.7 all-gather.7.cloned.1.call-update
  13.5 0.0 copy-done.7
  13.5 0.0 copy-done.5
  13.5 0.7 add_subtract_fusion.ids_ref
  14.2 3.9 list_hits.1
  18.1 0.0 copy-done.6
  18.1 0.1 pad_add_fusion
  18.2 0.6 pad.4
  18.8 11.5 %numbers.1 = (s32[8,8,128]{2,1,0:T(8,128)}, s32[8,8,128]{2,1,0:T(8,128)}) custom-call(s32[8,128]{1,0:T(8,128)} %bitcast.53, s32[8,128]{1,0:T(8,128)} %bitcast.52), custom_call_target="tpu_custom_call" | custom-call | bytes 73728 | tf_op jit(solution)/shard_map/numbers/pallas_call | solution.py:831
  30.3 1.4 copy.67
  31.7 0.0 copy-start.2
  31.7 30.9 %pick_rows.1 = (bf16[6144,96]{1,0:T(8,128)(2,1)}, bf16[96,24576]{1,0:T(8,128)(2,1)}, bf16[8,96,768]{2,1,0:T(8,128)(2,1)}) custom-call(s32[8,1024]{1,0:T(8,128)} %bitcast.44, f32[96,24026]{1,0:T(8,128)} %bitcast.40), custom_call_target="tpu_custom_call" | custom-call | tf_op jit(solution)/shard_map/pick_rows/pallas_call | solution.py:493
  62.6 5.3 all-to-all-start
  68.0 0.0 all-gather.9.cloned.1.call-start
  68.0 0.0 copy-done.2
  68.1 72.9 %look.1.refs_0_.refs_18_ = bf16[768,768]{1,0:T(8,128)(2,1)} custom-call(bf16[8,768,96]{2,1,0:T(8,128)(2,1)} %bitcast.42), custom_call_target="tpu_custom_call" | custom-call | bytes 2359296 | tf_op jit(solution)/shard_map/look/pallas_call | solution.py:831
  141.0 0.7 copy.57.positions_ref
  141.7 0.3 select_reduce_fusion
  142.0 0.2 sub.39
  142.2 0.2 slice_reduce_fusion
  142.4 0.1 fusion.6
  142.5 0.6 convert_reduce_fusion.1
  143.8 0.9 div.59.weights_ref
  144.7 0.7 reshape.145.counted_ref
  145.4 0.7 and_select_fusion.targets_ref
  146.1 0.0 all-gather.5.cloned.1.call-done.refs_3_.refs_17_
  146.1 65.0 %forward.1 = (bf16[8,96,1152]{2,1,0:T(8,128)(2,1)}, bf16[3,192,768]{2,1,0:T(8,128)(2,1)}, f32[16,768]{1,0:T(8,128)}, bf16[512,576]{1,0:T(8,128)(2,1)}, bf16[512,...) custom-call(bf16[768,768]{1,0:T(8,128)(2,1)} %look.1.refs_0_.refs_18, ...), custom_call_target="tpu_custom_call" | custom-call | flops 2415919104 | bytes 24133632 | tf_op jit(solution)/shard_map/forward/pallas_call | solution.py:831
  211.1 14.4 %all-gather.7.cloned.1.call-done.w_dec_hbm.refs_6_ = bf16[768,2176]{1,0:T(8,128)(2,1)} async-done(((bf16[96,2176]{1,0:T(8,128)(2,1)}), bf16[768,2176]{1,0:T(8,128)(2,1)}) %all-gather.7.cloned.1.call-update) | async-done | bytes 3342352 | tf_op jit(solution)/shard_map/all_gather | solution.py:1778
  225.4 58.7 %dec.1 = (bf16[8,96,1152]{2,1,0:T(8,128)(2,1)}, bf16[256,192]{1,0:T(8,128)(2,1)}, bf16[512,384]{1,0:T(8,128)(2,1)}, bf16[256,192]{1,0:T(8,128)(2,1)}, f32[256,12...) custom-call(f32[256,768]{1,0:T(8,128)} %get-tuple-element.78.stream_, ...), custom_call_target="tpu_custom_call" | custom-call | flops 1207959552 | bytes 16204032 | tf_op jit(solution)/shard_map/dec/pallas_call | solution.py:831
  284.1 0.0 all-to-all-done
  284.1 0.0 copy-start
  284.1 1.0 copy-done
  285.1 53.4 %head.1 = (f32[1,128]{1,0:T(1,128)}, bf16[64,768]{1,0:T(8,128)(2,1)}, bf16[768,3072]{1,0:T(8,128)(2,1)}, bf16[8,96,384]{2,1,0:T(8,128)(2,1)}) custom-call(bf16[512,768]{1,0:T(8,128)(2,1)} %bitcast.59, bf16[768,768]{1,0:T(8,128)(2,1)} %bitcast.43, bf16[768,1152]{1,0:T(8,128)(2,1)} %bitcast.57, bf16[768,1152]{1,0:T(8,128)(2,1)} %bitcast.58, ...), custom_call_target="tpu_custom_call" | custom-call | flops 7247757312 | bytes 10918400 | tf_op jit(solution)/shard_map/head/pallas_call | solution.py:831
  338.5 190.3 %backward.1 = (bf16[8,96,2688]{2,1,0:T(8,128)(2,1)}, bf16[4,8,208,96]{3,2,1,0:T(8,128)(2,1)}, bf16[4,96,2304]{2,1,0:T(8,128)(2,1)}, bf16[96,3072]{1,0:T(8,128)(2,1)}, f32[1,128]{1,0:T(1,128)}) custom-call(bf16[64,768]{1,0:T(8,128)(2,1)} %get-tuple-element.89.refs_0_, s32[1,64]{1,0:T(1,128)} %refs_1_.2, f32[256,768]{1,0:T(8,128)} %get-tuple-element.90.refs_2_, ...), custom_call_target="tpu_custom_call" | custom-call | flops 7247757312 | bytes 36651776 | tf_op jit(solution)/shard_map/backward/pallas_call | solution.py:831
  528.8 0.0 copy-start.8
  528.8 0.8 convert_reduce_fusion
  529.6 0.6 multiply_reduce_fusion
  530.2 31.9 %spread_rows.1 = (bf16[96,24576]{1,0:T(8,128)(2,1)}, f32[1,128]{1,0:T(1,128)}) custom-call(s32[8,1024]{1,0:T(8,128)} %bitcast.45, bf16[4,8,208,96]{3,2,1,0:T(8,128)(2,1)} %get-tuple-element.107.grads_ref, bf16[8,96,384]{2,1,0:T(8,128)(2,1)} %get-tuple-element.108.zero_ref, bf16[8,96,2688]{2,1,0:T(8,128)(2,1)} %get-tuple-element.109.one_ref), custom_call_target="tpu_custom_call" | custom-call | tf_op jit(solution)/shard_map/spread_rows/pallas_call | solution.py:554
  562.7 0.0 copy-done.8
  562.8 0.5 broadcast_add_fusion.dense_ref
  563.3 14.5 %squares.1 = f32[1,128]{1,0:T(1,128)} custom-call(f32[1,128]{1,0:T(1,128)} %get-tuple-element.110.embedding_ref, f32[1,128]{1,0:T(1,128)} %broadcast_add_fusion.dense_ref), custom_call_target="tpu_custom_call" | custom-call | bytes 1536 | tf_op jit(solution)/shard_map/squares/pallas_call | solution.py:831
  578.5 0.0 all-gather.9.cloned.1.call-update
  578.5 0.0 copy-start.1
  578.5 0.0 copy-start.3
  578.5 0.0 copy-start.4
  578.5 22.6 %multiply_subtract_fusion = (f32[24026,96]{0,1:T(8,128)}, f32[24026,96]{0,1:T(8,128)}, f32[24026,96]{0,1:T(8,128)}) fusion(f32[24026,96]{0,1:T(8,128)} %param.28, f32[]{:T(128)} %min_shard_map.3, bf16[96,24576]{1,0:T(8,128)(2,1)} %get-tuple-element.112, f32[24026,96]{0,1:T(8,128)} %param.34, f32[24026,96]{0,1:T(8,128)} %param.40), kind=kLoop, calls=%fused_computation.4 | loop fusion | flops 39210432 | bytes 59968900 | tf_op jit(solution)/shard_map/sub | solution.py:214
  601.1 0.0 copy-done.1
  601.1 0.0 copy-done.3
  601.2 0.0 copy-done.4
  601.2 0.6 multiply_subtract_fusion.1
  601.8 0.3 all-gather.9.cloned.1.call-done
  602.1 9.7 %adam_in.1 = (f32[3,96,2304]{2,1,0:T(8,128)}, f32[3,96,2304]{2,1,0:T(8,128)}, f32[3,96,2304]{2,1,0:T(8,128)}) custom-call(f32[1]{0:T(128)} %bitcast.16.factor_ref, bf16[4,96,3072]{2,1,0:T(8,128)(2,1)} %bitcast.36, bf16[4,96,2304]{2,1,0:T(8,128)(2,1)} %get-tuple-element.114.refs_1_, f32[3,96,2304]{2,1,0:T(8,128)} %refs_2_.5, f32[3,96,2304]{2,1,0:T(8,128)} %refs_3_.4, ...), custom_call_target="tpu_custom_call" | custom-call | tf_op jit(solution)/shard_map/adam_in/pallas_call | solution.py:1612
  611.8 5.7 adam_out.1
  617.4 7.6 %adam_up.1 = (f32[2,96,3072]{2,1,0:T(8,128)}, f32[2,96,3072]{2,1,0:T(8,128)}, f32[2,96,3072]{2,1,0:T(8,128)}) custom-call(f32[1]{0:T(128)} %bitcast.16.factor_ref, bf16[4,96,3072]{2,1,0:T(8,128)(2,1)} %bitcast.38, bf16[4,96,2304]{2,1,0:T(8,128)(2,1)} %get-tuple-element.114.refs_1_, f32[2,96,3072]{2,1,0:T(8,128)} %refs_2_.7, f32[2,96,3072]{2,1,0:T(8,128)} %refs_3_.6, ...), custom_call_target="tpu_custom_call" | custom-call | tf_op jit(solution)/shard_map/adam_up/pallas_call | solution.py:1612
  625.0 0.0 copy-start.9
  625.0 6.2 adam_down.1
  631.2 0.0 copy-done.9
  (5 shorter events, 0.0 us)
Async XLA Ops:
  7.2 6.3 copy-start.7
  7.2 6.3 copy-start.5
  7.2 10.9 %copy-start.6 = (s32[1,64]{1,0:T(1,128)S(1)}, s32[1,64]{1,0:T(1,128)}, u32[]{:S(2)}) copy-start(s32[1,64]{1,0:T(1,128)} %refs_1_.2) | copy-start | bytes 772
  7.2 138.9 %all-gather.5.cloned.1.call-start = ((), (), s32[]{:S(2)}) async-start(), calls=%async_computation.1 | async-start | bytes 5971968 | tf_op jit(solution)/shard_map/all_gather | solution.py:1777
  12.1 213.4 %all-gather.7.cloned.1.call-start = ((), (), s32[]{:S(2)}) async-start(), calls=%async_computation.2 | async-start | bytes 3760128 | tf_op jit(solution)/shard_map/all_gather | solution.py:1778
  31.7 36.3 %copy-start.2 = (s32[8,8,128]{2,1,0:T(8,128)S(1)}, s32[8,8,128]{2,1,0:T(8,128)}, u32[]{:S(2)}) copy-start(s32[8,8,128]{2,1,0:T(8,128)} %get-tuple-element.87) | copy-start | bytes 98308
  62.6 221.5 %all-to-all-start = ((bf16[8,96,768]{2,1,0:T(8,128)(2,1)}), bf16[8,96,768]{2,1,0:T(8,128)(2,1)S(1)}, u32[]{:S(2)}, u32[]{:S(2)}) async-start(bf16[8,96,768]{2,1,0:T(8,128)(2,1)} %get-tuple-element.84), calls=%async_computation | async-start | bytes 2359296 | tf_op jit(solution)/shard_map/all_to_all | solution.py:1824
  68.0 534.1 %all-gather.9.cloned.1.call-start = ((), (), s32[]{:S(2)}) async-start(), calls=%async_computation.3 | async-start | bytes 2949120 | tf_op jit(solution)/shard_map/all_gather | solution.py:2032
  284.1 1.0 copy-start
  528.8 34.0 %copy-start.8 = (f32[1,128]{1,0:T(1,128)S(1)}, f32[1,128]{1,0:T(1,128)}, u32[]{:S(2)}) copy-start(f32[1,128]{1,0:T(1,128)} %get-tuple-element.111) | copy-start | bytes 1540
  578.5 22.7 %copy-start.1 = (f32[14,96]{1,0:T(8,128)S(1)}, f32[14,96]{1,0:T(8,128)}, u32[]{:S(2)}) copy-start(f32[14,96]{1,0:T(8,128)} %norms_ref.1) | copy-start | bytes 16132
  578.5 22.7 %copy-start.3 = (f32[14,96]{1,0:T(8,128)S(1)}, f32[14,96]{1,0:T(8,128)}, u32[]{:S(2)}) copy-start(f32[14,96]{1,0:T(8,128)} %param.39) | copy-start | bytes 16132
  578.5 22.6 %copy-start.4 = (f32[14,96]{1,0:T(8,128)S(1)}, f32[14,96]{1,0:T(8,128)}, u32[]{:S(2)}) copy-start(f32[14,96]{1,0:T(8,128)} %param.45) | copy-start | bytes 16132
  625.0 6.2 copy-start.9
Sparse Core Ops, SparseCore 0:
  12.2 120.1 all-gather.4
  135.1 90.2 all-gather.6
  578.6 23.4 all-gather.8

commit v5 on v4

--- a/solution.py
+++ b/solution.py
@@ -1326,12 +1326,20 @@
     )
     load_looked = Late(looked_hbm, looked_ref, load_sems.at[8])
     meet(peers + group_peers(group, share, groups))
-    exchange = Exchange(
-        head_blocks(head_in_ref, head_in_ref.shape[2] - head_out_ref.shape[2], head_out_ref.shape[2]),
-        head_out_ref,
-        head_sems,
-        groups,
-    )
+    columns = head_out_ref.shape[2]
+    skipped = head_in_ref.shape[2] - columns
+    cuts = (0, 3 * columns // 7, 5 * columns // 7, columns)
+
+    def head_piece(index):
+        low, wide = cuts[index], cuts[index + 1] - cuts[index]
+        return Exchange(
+            head_blocks(head_in_ref, skipped + low, wide),
+            head_out_ref.at[:, :, pl.ds(low, wide)],
+            head_sems.at[index],
+            groups,
+        )
+
+    pieces = [head_piece(0)]
     width = stream_out_ref.shape[1]
     own = q_ref.shape[1]
     hidden = pre_dec_ref.shape[1]
@@ -1377,6 +1385,7 @@
     put_grads(dec_grads_ref, in_start + own, contract_rows(memory_ref[...], gkv_ref[...]))
     cross_rows.put(dec_grads_ref, in_start + 3 * own)
     dec_line.begin()
+    pieces.append(head_piece(1))
     memory_total.last()
     cross_total.last()
     summed = memory_total.finish()
@@ -1413,6 +1422,7 @@
     put_grads(mid_grads_ref, in_start, contract_rows(lowered(normed), gqkv_ref[...]))
     self_rows.put(mid_grads_ref, in_start + 3 * own)
     mid_line.begin()
+    pieces.append(head_piece(2))
     grad_enc_ref[...] = norm_step(
         grad_enc_ref, stream_enc_ref, norms_ref, 1, feed_total.finish(), rows_mid_ref, 2
     )
@@ -1506,14 +1516,15 @@
     lane = lax.broadcasted_iota(jnp.int32, squares_ref.shape, 1)
     squares_ref[...] = jnp.where(lane == 0, squares, 0.0)
     dec_gather.finish()
-    exchange.finish()
+    for piece in pieces:
+        piece.finish()
 
 
 def look_kernel(
     groups,
-    picked_ref,
-    looked_ref,
-    send_ref, core_ref, side_ref, group_ref, sems,
+    picked_ref, piece_ref,
+    looked_ref, table_ref,
+    send_ref, core_ref, side_ref, group_ref, sems, table_sems,
 ):
     group, share, core, core_peer, side_peer = places()
     side = share // 2
@@ -1534,6 +1545,7 @@
         send(side_ref.at[peer[0]], group_ref.at[group], sems.at[0, 2 + step], sems.at[1, 2 + step], peer)
         for step, peer in enumerate(far)
     ]
+    exchange = Exchange(lambda index: piece_ref.at[index], table_ref, table_sems, groups)
     for copy in copies:
         copy.wait()
     for index in range(groups):
@@ -1545,6 +1557,7 @@
     end = end + 1
     both = looked_ref.at[mine, :]
     send(both, both, sems.at[0, end], sems.at[1, end], core_peer).wait()
+    exchange.finish()
 
 
 def squares_kernel(
@@ -1769,7 +1782,7 @@
     first_wide = 3 * in_wide
     enc_wide = own_up + model_width
     chunk = -(-shard_rows // (groups * 3072)) * 3072
-    table_cuts = (chunk // 4, 5 * chunk // 24, chunk // 6, 3 * chunk // 8)
+    table_cuts = (chunk // 8, chunk // 4, chunk // 4, 3 * chunk // 8)
     early_wide = first_wide + enc_wide
     mine_early, mine_dec = cut_weights(
         groups, shares, gap, (attn_in, attn_out, ffn_up, ffn_down, norms), early_wide, dec_wide
@@ -1806,22 +1819,27 @@
     enc_macs, dec_macs = enc_len * model_width, dec_len * model_width
     total_enc, total_dec = total_scratch(enc_len, model_width), total_scratch(dec_len, model_width)
     block_shape = (2, 2, 2, part_width)
-    (looked,) = call(
+    looked, table_zero = call(
         partial(look_kernel, groups),
         "look",
         2,
-        [picked.reshape(groups, tokens, part_width)],
-        [shape_of((tokens, model_width), bf16)],
+        [picked.reshape(groups, tokens, part_width), table_zero],
+        [
+            shape_of((tokens, model_width), bf16),
+            shape_of((groups, part_width, table_cuts[0]), bf16),
+        ],
         [
             pltpu.VMEM((tokens // 4, model_width), bf16),
             pltpu.VMEM((groups, tokens // 2, part_width), bf16),
             pltpu.VMEM((groups, tokens // 4, part_width), bf16),
             pltpu.VMEM((groups, tokens // 4, part_width), bf16),
             sems((2, groups + 3)),
+            sems((2, groups)),
         ],
         0,
-    )
-    table_zero = lax.all_to_all(table_zero, "dp", 0, 0)
+        (1,),
+        (1,),
+    )
     forward_inputs = [looked, place_enc, place_dec, w_early, across]
     forward_outputs = [
         shape_of((groups, part_width, sum(table_cuts[1:3])), bf16),
@@ -1980,7 +1998,7 @@
             shape_of((1, 128), f32),
         ],
         [
-            sems((2, groups)),
+            sems((3, 2, groups)),
             sems((11,)),
             pltpu.VMEM((model_width, dec_wide), bf16),
             pltpu.VMEM((model_width, own_up + model_width), bf16),

time: 646 us -> 644 us (level)
  waiting for transfers between devices: 15.4 us -> 27.6 us
  Pallas kernels: 567 us -> 558 us
    all_gather x1, waiting for transfers between devices: 14.4 us -> 26 us  [local(): w_dec = lax.all_gather(mine_dec, 'dp', axis=0, tiled=True)]
  transfers between devices with their start and end apart: 4 -> 3, of which waited for: 2 -> 2; matrix products, arithmetic and copies ran while one was open for 5% -> 5% of each run, Pallas kernels for 38% -> 27%
where the time goes in v5:
time: 644 us; the launch traced here: 637 us
  Pallas kernels  558 us (87%)
  waiting for transfers between devices  27.6 us (4%)
  other arithmetic  27.1 us (4%)
  between operations  19.3 us (3%)
    pallas_call x7, Pallas kernels, call(): pl.pallas_call(kernel, out_shape=tuple(out_shape), in_specs=in_vmem(len(i...  460 us
    pallas_call x1, Pallas kernels, spread_rows(): pl.pallas_call(spread_kernel, out_shape=(jax.ShapeDtypeStruct((width, chu...  30.5 us
    pallas_call x1, Pallas kernels, pick_rows(): pl.pallas_call(pick_kernel, out_shape=(jax.ShapeDtypeStruct((count, width...  29.4 us
    pallas_call x4, Pallas kernels, dense_update(): pl.pallas_call(partial(dense_kernel, rate, place_grads), grid=(matrices,...  29.1 us
    all_gather x1, waiting for transfers between devices, local(): w_dec = lax.all_gather(mine_dec, 'dp', axis=0, tiled=True)  26 us
    sub x2, other arithmetic, adam_update(): return (weight - rate * (corrected + DECAY * weight), new_first, new_second)  22.7 us
  transfers between devices with their start and end apart: 3, of which 2 were waited for; matrix products, arithmetic and copies ran while one was open for 5% of the time, Pallas kernels for 27%

profile of v5, /device:TPU:0, one launch (start us, length us, event | category | flops | bytes accessed | tf_op | source)
XLA Modules:
  0.0 637.3 jit_solution(10538006284314564695)
XLA Ops:
  7.2 0.0 copy-start.5
  7.2 0.0 copy-start.3
  7.2 0.0 copy-start.4
  7.2 0.0 all-gather.5.cloned.1.call-start
  7.3 4.8 cut_weights.1
  12.0 0.0 all-gather.5.cloned.1.call-update
  12.1 0.0 all-gather.7.cloned.1.call-start
  12.1 0.7 all-gather.7.cloned.1.call-update
  12.8 0.0 all-gather.9.cloned.1.call-start
  13.5 0.0 copy-done.5
  13.5 0.0 copy-done.3
  13.5 0.7 add_subtract_fusion.ids_ref
  14.2 3.9 list_hits.1
  18.2 0.0 copy-done.4
  18.2 0.1 pad_add_fusion
  18.2 0.6 pad.4
  18.8 11.5 %numbers.1 = (s32[8,8,128]{2,1,0:T(8,128)}, s32[8,8,128]{2,1,0:T(8,128)}) custom-call(s32[8,128]{1,0:T(8,128)} %bitcast.52, s32[8,128]{1,0:T(8,128)} %bitcast.51), custom_call_target="tpu_custom_call" | custom-call | bytes 73728 | tf_op jit(solution)/shard_map/numbers/pallas_call | solution.py:831
  30.4 0.8 copy.66
  31.2 1.4 copy.67
  32.6 0.7 copy.57.positions_ref
  33.3 0.3 select_reduce_fusion
  33.6 0.2 sub.39
  33.8 0.2 slice_reduce_fusion
  34.0 0.1 fusion.6
  34.1 0.6 convert_reduce_fusion.1
  35.4 0.9 div.59.weights_ref
  36.3 0.7 reshape.145.counted_ref
  36.9 29.4 %pick_rows.1 = (bf16[6144,96]{1,0:T(8,128)(2,1)}, bf16[96,24576]{1,0:T(8,128)(2,1)}, bf16[8,96,384]{2,1,0:T(8,128)(2,1)}) custom-call(s32[8,1024]{1,0:T(8,128)} %bitcast.43, f32[96,24026]{1,0:T(8,128)} %bitcast.40), custom_call_target="tpu_custom_call" | custom-call | tf_op jit(solution)/shard_map/pick_rows/pallas_call | solution.py:493
  66.3 51.3 %look.1 = (bf16[768,768]{1,0:T(8,128)(2,1)}, bf16[8,96,384]{2,1,0:T(8,128)(2,1)}) custom-call(bf16[8,768,96]{2,1,0:T(8,128)(2,1)} %bitcast.42, bf16[8,96,384]{2,1,0:T(8,128)(2,1)} %get-tuple-element.78.piece_ref), custom_call_target="tpu_custom_call" | custom-call | bytes 3538944 | tf_op jit(solution)/shard_map/look/pallas_call | solution.py:831
  117.7 0.7 and_select_fusion.targets_ref
  118.4 0.9 all-gather.5.cloned.1.call-done.refs_3_.refs_17_
  119.3 76.2 %forward.1 = (bf16[8,96,1536]{2,1,0:T(8,128)(2,1)}, bf16[3,192,768]{2,1,0:T(8,128)(2,1)}, f32[16,768]{1,0:T(8,128)}, bf16[512,576]{1,0:T(8,128)(2,1)}, bf16[512,...) custom-call(bf16[768,768]{1,0:T(8,128)(2,1)} %get-tuple-element.79.r, ...), custom_call_target="tpu_custom_call" | custom-call | flops 2415919104 | bytes 24723456 | tf_op jit(solution)/shard_map/forward/pallas_call | solution.py:831
  195.5 26.0 %all-gather.7.cloned.1.call-done.w_dec_hbm.refs_6_ = bf16[768,2176]{1,0:T(8,128)(2,1)} async-done(((bf16[96,2176]{1,0:T(8,128)(2,1)}), bf16[768,2176]{1,0:T(8,128)(2,1)}) %all-gather.7.cloned.1.call-update) | async-done | bytes 3342352 | tf_op jit(solution)/shard_map/all_gather | solution.py:1791
  221.5 59.4 %dec.1 = (bf16[8,96,1152]{2,1,0:T(8,128)(2,1)}, bf16[256,192]{1,0:T(8,128)(2,1)}, bf16[512,384]{1,0:T(8,128)(2,1)}, bf16[256,192]{1,0:T(8,128)(2,1)}, f32[256,12...) custom-call(f32[256,768]{1,0:T(8,128)} %get-tuple-element.82.stream_, ...), custom_call_target="tpu_custom_call" | custom-call | flops 1207959552 | bytes 16204032 | tf_op jit(solution)/shard_map/dec/pallas_call | solution.py:831
  280.9 51.6 %head.1 = (f32[1,128]{1,0:T(1,128)}, bf16[64,768]{1,0:T(8,128)(2,1)}, bf16[768,3072]{1,0:T(8,128)(2,1)}, bf16[8,96,384]{2,1,0:T(8,128)(2,1)}) custom-call(bf16[512,768]{1,0:T(8,128)(2,1)} %bitcast.58, bf16[768,384]{1,0:T(8,128)(2,1)} %bitcast.59, bf16[768,1536]{1,0:T(8,128)(2,1)} %bitcast.56, bf16[768,1152]{1,0:T(8,128)(2,1)} %bitcast.57, ...), custom_call_target="tpu_custom_call" | custom-call | flops 7247757312 | bytes 10918400 | tf_op jit(solution)/shard_map/head/pallas_call | solution.py:831
  332.5 198.3 %backward.1 = (bf16[8,96,2688]{2,1,0:T(8,128)(2,1)}, bf16[4,8,208,96]{3,2,1,0:T(8,128)(2,1)}, bf16[4,96,2304]{2,1,0:T(8,128)(2,1)}, bf16[96,3072]{1,0:T(8,128)(2,1)}, f32[1,128]{1,0:T(1,128)}) custom-call(bf16[64,768]{1,0:T(8,128)(2,1)} %get-tuple-element.93.refs_0_, s32[1,64]{1,0:T(1,128)} %refs_1_.2, f32[256,768]{1,0:T(8,128)} %get-tuple-element.94.refs_2_, ...), custom_call_target="tpu_custom_call" | custom-call | flops 7247757312 | bytes 36651776 | tf_op jit(solution)/shard_map/backward/pallas_call | solution.py:831
  530.9 0.0 copy-start.6
  530.9 0.8 convert_reduce_fusion
  531.6 0.6 multiply_reduce_fusion
  532.2 30.5 %spread_rows.1 = (bf16[96,24576]{1,0:T(8,128)(2,1)}, f32[1,128]{1,0:T(1,128)}) custom-call(s32[8,1024]{1,0:T(8,128)} %bitcast.44, bf16[4,8,208,96]{3,2,1,0:T(8,128)(2,1)} %get-tuple-element.111.grads_ref, bf16[8,96,384]{2,1,0:T(8,128)(2,1)} %get-tuple-element.112.zero_ref, bf16[8,96,2688]{2,1,0:T(8,128)(2,1)} %get-tuple-element.113.one_ref), custom_call_target="tpu_custom_call" | custom-call | tf_op jit(solution)/shard_map/spread_rows/pallas_call | solution.py:554
  563.4 0.0 copy-done.6
  563.4 0.5 broadcast_add_fusion.dense_ref
  563.9 11.6 %squares.1 = f32[1,128]{1,0:T(1,128)} custom-call(f32[1,128]{1,0:T(1,128)} %get-tuple-element.114.embedding_ref, f32[1,128]{1,0:T(1,128)} %broadcast_add_fusion.dense_ref), custom_call_target="tpu_custom_call" | custom-call | bytes 1536 | tf_op jit(solution)/shard_map/squares/pallas_call | solution.py:831
  576.3 0.0 all-gather.9.cloned.1.call-update
  576.3 0.0 copy-start
  576.3 0.0 copy-start.1
  576.3 0.0 copy-start.2
  576.3 22.0 %multiply_subtract_fusion = (f32[24026,96]{0,1:T(8,128)}, f32[24026,96]{0,1:T(8,128)}, f32[24026,96]{0,1:T(8,128)}) fusion(f32[24026,96]{0,1:T(8,128)} %param.28, f32[]{:T(128)} %min_shard_map.3, bf16[96,24576]{1,0:T(8,128)(2,1)} %get-tuple-element.116, f32[24026,96]{0,1:T(8,128)} %param.34, f32[24026,96]{0,1:T(8,128)} %param.40), kind=kLoop, calls=%fused_computation.4 | loop fusion | flops 39210432 | bytes 59968900 | tf_op jit(solution)/shard_map/sub | solution.py:214
  598.4 0.0 copy-done
  598.4 0.0 copy-done.1
  598.4 0.0 copy-done.2
  598.4 0.6 multiply_subtract_fusion.1
  599.0 0.0 all-gather.9.cloned.1.call-done
  599.0 9.7 %adam_in.1 = (f32[3,96,2304]{2,1,0:T(8,128)}, f32[3,96,2304]{2,1,0:T(8,128)}, f32[3,96,2304]{2,1,0:T(8,128)}) custom-call(f32[1]{0:T(128)} %bitcast.16.factor_ref, bf16[4,96,3072]{2,1,0:T(8,128)(2,1)} %bitcast.36, bf16[4,96,2304]{2,1,0:T(8,128)(2,1)} %get-tuple-element.118.refs_1_, f32[3,96,2304]{2,1,0:T(8,128)} %refs_2_.5, f32[3,96,2304]{2,1,0:T(8,128)} %refs_3_.4, ...), custom_call_target="tpu_custom_call" | custom-call | tf_op jit(solution)/shard_map/adam_in/pallas_call | solution.py:1625
  608.7 5.7 adam_out.1
  614.4 7.6 %adam_up.1 = (f32[2,96,3072]{2,1,0:T(8,128)}, f32[2,96,3072]{2,1,0:T(8,128)}, f32[2,96,3072]{2,1,0:T(8,128)}) custom-call(f32[1]{0:T(128)} %bitcast.16.factor_ref, bf16[4,96,3072]{2,1,0:T(8,128)(2,1)} %bitcast.38, bf16[4,96,2304]{2,1,0:T(8,128)(2,1)} %get-tuple-element.118.refs_1_, f32[2,96,3072]{2,1,0:T(8,128)} %refs_2_.7, f32[2,96,3072]{2,1,0:T(8,128)} %refs_3_.6, ...), custom_call_target="tpu_custom_call" | custom-call | tf_op jit(solution)/shard_map/adam_up/pallas_call | solution.py:1625
  622.0 0.0 copy-start.7
  622.0 6.2 adam_down.1
  628.2 0.0 copy-done.7
  (4 shorter events, 0.0 us)
Async XLA Ops:
  7.2 6.3 copy-start.5
  7.2 6.3 copy-start.3
  7.2 10.9 %copy-start.4 = (s32[1,64]{1,0:T(1,128)S(1)}, s32[1,64]{1,0:T(1,128)}, u32[]{:S(2)}) copy-start(s32[1,64]{1,0:T(1,128)} %refs_1_.2) | copy-start | bytes 772
  7.2 112.1 %all-gather.5.cloned.1.call-start = ((), (), s32[]{:S(2)}) async-start(), calls=%async_computation | async-start | bytes 5971968 | tf_op jit(solution)/shard_map/all_gather | solution.py:1790
  12.1 209.4 %all-gather.7.cloned.1.call-start = ((), (), s32[]{:S(2)}) async-start(), calls=%async_computation.1 | async-start | bytes 3760128 | tf_op jit(solution)/shard_map/all_gather | solution.py:1791
  12.8 586.2 %all-gather.9.cloned.1.call-start = ((), (), s32[]{:S(2)}) async-start(), calls=%async_computation.2 | async-start | bytes 2949120 | tf_op jit(solution)/shard_map/all_gather | solution.py:2050
  530.9 32.5 %copy-start.6 = (f32[1,128]{1,0:T(1,128)S(1)}, f32[1,128]{1,0:T(1,128)}, u32[]{:S(2)}) copy-start(f32[1,128]{1,0:T(1,128)} %get-tuple-element.115) | copy-start | bytes 1540
  576.3 22.1 %copy-start = (f32[14,96]{1,0:T(8,128)S(1)}, f32[14,96]{1,0:T(8,128)}, u32[]{:S(2)}) copy-start(f32[14,96]{1,0:T(8,128)} %norms_ref.1) | copy-start | bytes 16132
  576.3 22.1 %copy-start.1 = (f32[14,96]{1,0:T(8,128)S(1)}, f32[14,96]{1,0:T(8,128)}, u32[]{:S(2)}) copy-start(f32[14,96]{1,0:T(8,128)} %param.39) | copy-start | bytes 16132
  576.3 22.1 %copy-start.2 = (f32[14,96]{1,0:T(8,128)S(1)}, f32[14,96]{1,0:T(8,128)}, u32[]{:S(2)}) copy-start(f32[14,96]{1,0:T(8,128)} %param.45) | copy-start | bytes 16132
  622.0 6.2 copy-start.7
Sparse Core Ops, SparseCore 0:
  12.2 107.0 all-gather.4
  122.1 99.3 all-gather.6
  576.4 22.3 all-gather.8

commit v6 on v5

--- a/solution.py
+++ b/solution.py
@@ -1339,7 +1339,7 @@
             groups,
         )
 
-    pieces = [head_piece(0)]
+    pieces = [head_piece(index) for index in range(3)]
     width = stream_out_ref.shape[1]
     own = q_ref.shape[1]
     hidden = pre_dec_ref.shape[1]
@@ -1385,7 +1385,6 @@
     put_grads(dec_grads_ref, in_start + own, contract_rows(memory_ref[...], gkv_ref[...]))
     cross_rows.put(dec_grads_ref, in_start + 3 * own)
     dec_line.begin()
-    pieces.append(head_piece(1))
     memory_total.last()
     cross_total.last()
     summed = memory_total.finish()
@@ -1422,7 +1421,6 @@
     put_grads(mid_grads_ref, in_start, contract_rows(lowered(normed), gqkv_ref[...]))
     self_rows.put(mid_grads_ref, in_start + 3 * own)
     mid_line.begin()
-    pieces.append(head_piece(2))
     grad_enc_ref[...] = norm_step(
         grad_enc_ref, stream_enc_ref, norms_ref, 1, feed_total.finish(), rows_mid_ref, 2
     )

time: 644 us -> 641 us (level)
  transfers between devices with their start and end apart: 3 -> 3, of which waited for: 2 -> 2; matrix products, arithmetic and copies ran while one was open for 5% -> 5% of each run, Pallas kernels for 27% -> 28%
where the time goes in v6:
time: 641 us; the launch traced here: 639 us
  Pallas kernels  561 us (88%)
  other arithmetic  27.1 us (4%)
  waiting for transfers between devices  25.8 us (4%)
  between operations  19.3 us (3%)
    pallas_call x7, Pallas kernels, call(): pl.pallas_call(kernel, out_shape=tuple(out_shape), in_specs=in_vmem(len(i...  466 us
    pallas_call x1, Pallas kernels, spread_rows(): pl.pallas_call(spread_kernel, out_shape=(jax.ShapeDtypeStruct((width, chu...  29.5 us
    pallas_call x4, Pallas kernels, dense_update(): pl.pallas_call(partial(dense_kernel, rate, place_grads), grid=(matrices,...  29.1 us
    pallas_call x1, Pallas kernels, pick_rows(): pl.pallas_call(pick_kernel, out_shape=(jax.ShapeDtypeStruct((count, width...  28.5 us
    all_gather x1, waiting for transfers between devices, local(): w_dec = lax.all_gather(mine_dec, 'dp', axis=0, tiled=True)  24.8 us
    sub x2, other arithmetic, adam_update(): return (weight - rate * (corrected + DECAY * weight), new_first, new_second)  22.7 us
  transfers between devices with their start and end apart: 3, of which 2 were waited for; matrix products, arithmetic and copies ran while one was open for 5% of the time, Pallas kernels for 28%

profile of v6, /device:TPU:0, one launch (start us, length us, event | category | flops | bytes accessed | tf_op | source)
XLA Modules:
  0.0 639.2 jit_solution(14111637042500720939)
XLA Ops:
  7.2 0.0 copy-start.5
  7.2 0.0 copy-start.3
  7.2 0.0 copy-start.4
  7.2 0.0 all-gather.5.cloned.1.call-start
  7.3 4.8 cut_weights.1
  12.0 0.0 all-gather.5.cloned.1.call-update
  12.1 0.0 all-gather.7.cloned.1.call-start
  12.1 0.7 all-gather.7.cloned.1.call-update
  12.8 0.0 all-gather.9.cloned.1.call-start
  13.5 0.0 copy-done.5
  13.5 0.0 copy-done.3
  13.5 0.7 add_subtract_fusion.ids_ref
  14.2 3.9 list_hits.1
  18.2 0.0 copy-done.4
  18.2 0.1 pad_add_fusion
  18.2 0.6 pad.4
  18.8 11.5 %numbers.1 = (s32[8,8,128]{2,1,0:T(8,128)}, s32[8,8,128]{2,1,0:T(8,128)}) custom-call(s32[8,128]{1,0:T(8,128)} %bitcast.52, s32[8,128]{1,0:T(8,128)} %bitcast.51), custom_call_target="tpu_custom_call" | custom-call | bytes 73728 | tf_op jit(solution)/shard_map/numbers/pallas_call | solution.py:831
  30.4 0.8 copy.66
  31.2 1.4 copy.67
  32.6 0.7 copy.57.positions_ref
  33.3 0.3 select_reduce_fusion
  33.6 0.2 sub.39
  33.8 0.2 slice_reduce_fusion
  34.0 0.1 fusion.6
  34.1 0.6 convert_reduce_fusion.1
  35.4 0.9 div.59.weights_ref
  36.3 0.7 reshape.145.counted_ref
  36.9 28.5 %pick_rows.1 = (bf16[6144,96]{1,0:T(8,128)(2,1)}, bf16[96,24576]{1,0:T(8,128)(2,1)}, bf16[8,96,384]{2,1,0:T(8,128)(2,1)}) custom-call(s32[8,1024]{1,0:T(8,128)} %bitcast.43, f32[96,24026]{1,0:T(8,128)} %bitcast.40), custom_call_target="tpu_custom_call" | custom-call | tf_op jit(solution)/shard_map/pick_rows/pallas_call | solution.py:493
  65.5 54.7 %look.1 = (bf16[768,768]{1,0:T(8,128)(2,1)}, bf16[8,96,384]{2,1,0:T(8,128)(2,1)}) custom-call(bf16[8,768,96]{2,1,0:T(8,128)(2,1)} %bitcast.42, bf16[8,96,384]{2,1,0:T(8,128)(2,1)} %get-tuple-element.78.piece_ref), custom_call_target="tpu_custom_call" | custom-call | bytes 3538944 | tf_op jit(solution)/shard_map/look/pallas_call | solution.py:831
  120.1 0.7 and_select_fusion.targets_ref
  120.9 0.0 all-gather.5.cloned.1.call-done.refs_3_.refs_17_
  120.9 79.0 %forward.1 = (bf16[8,96,1536]{2,1,0:T(8,128)(2,1)}, bf16[3,192,768]{2,1,0:T(8,128)(2,1)}, f32[16,768]{1,0:T(8,128)}, bf16[512,576]{1,0:T(8,128)(2,1)}, bf16[512,...) custom-call(bf16[768,768]{1,0:T(8,128)(2,1)} %get-tuple-element.79.r, ...), custom_call_target="tpu_custom_call" | custom-call | flops 2415919104 | bytes 24723456 | tf_op jit(solution)/shard_map/forward/pallas_call | solution.py:831
  199.8 24.8 %all-gather.7.cloned.1.call-done.w_dec_hbm.refs_6_ = bf16[768,2176]{1,0:T(8,128)(2,1)} async-done(((bf16[96,2176]{1,0:T(8,128)(2,1)}), bf16[768,2176]{1,0:T(8,128)(2,1)}) %all-gather.7.cloned.1.call-update) | async-done | bytes 3342352 | tf_op jit(solution)/shard_map/all_gather | solution.py:1789
  224.7 58.4 %dec.1 = (bf16[8,96,1152]{2,1,0:T(8,128)(2,1)}, bf16[256,192]{1,0:T(8,128)(2,1)}, bf16[512,384]{1,0:T(8,128)(2,1)}, bf16[256,192]{1,0:T(8,128)(2,1)}, f32[256,12...) custom-call(f32[256,768]{1,0:T(8,128)} %get-tuple-element.82.stream_, ...), custom_call_target="tpu_custom_call" | custom-call | flops 1207959552 | bytes 16204032 | tf_op jit(solution)/shard_map/dec/pallas_call | solution.py:831
  283.1 53.8 %head.1 = (f32[1,128]{1,0:T(1,128)}, bf16[64,768]{1,0:T(8,128)(2,1)}, bf16[768,3072]{1,0:T(8,128)(2,1)}, bf16[8,96,384]{2,1,0:T(8,128)(2,1)}) custom-call(bf16[512,768]{1,0:T(8,128)(2,1)} %bitcast.58, bf16[768,384]{1,0:T(8,128)(2,1)} %bitcast.59, bf16[768,1536]{1,0:T(8,128)(2,1)} %bitcast.56, bf16[768,1152]{1,0:T(8,128)(2,1)} %bitcast.57, ...), custom_call_target="tpu_custom_call" | custom-call | flops 7247757312 | bytes 10918400 | tf_op jit(solution)/shard_map/head/pallas_call | solution.py:831
  336.8 191.4 %backward.1 = (bf16[8,96,2688]{2,1,0:T(8,128)(2,1)}, bf16[4,8,208,96]{3,2,1,0:T(8,128)(2,1)}, bf16[4,96,2304]{2,1,0:T(8,128)(2,1)}, bf16[96,3072]{1,0:T(8,128)(2,1)}, f32[1,128]{1,0:T(1,128)}) custom-call(bf16[64,768]{1,0:T(8,128)(2,1)} %get-tuple-element.93.refs_0_, s32[1,64]{1,0:T(1,128)} %refs_1_.2, f32[256,768]{1,0:T(8,128)} %get-tuple-element.94.refs_2_, ...), custom_call_target="tpu_custom_call" | custom-call | flops 7247757312 | bytes 36651776 | tf_op jit(solution)/shard_map/backward/pallas_call | solution.py:831
  528.3 0.0 copy-start.6
  528.3 0.8 convert_reduce_fusion
  529.0 0.6 multiply_reduce_fusion
  529.7 29.5 %spread_rows.1 = (bf16[96,24576]{1,0:T(8,128)(2,1)}, f32[1,128]{1,0:T(1,128)}) custom-call(s32[8,1024]{1,0:T(8,128)} %bitcast.44, bf16[4,8,208,96]{3,2,1,0:T(8,128)(2,1)} %get-tuple-element.111.grads_ref, bf16[8,96,384]{2,1,0:T(8,128)(2,1)} %get-tuple-element.112.zero_ref, bf16[8,96,2688]{2,1,0:T(8,128)(2,1)} %get-tuple-element.113.one_ref), custom_call_target="tpu_custom_call" | custom-call | tf_op jit(solution)/shard_map/spread_rows/pallas_call | solution.py:554
  559.8 0.0 copy-done.6
  559.9 0.5 broadcast_add_fusion.dense_ref
  560.4 16.9 %squares.1 = f32[1,128]{1,0:T(1,128)} custom-call(f32[1,128]{1,0:T(1,128)} %get-tuple-element.114.embedding_ref, f32[1,128]{1,0:T(1,128)} %broadcast_add_fusion.dense_ref), custom_call_target="tpu_custom_call" | custom-call | bytes 1536 | tf_op jit(solution)/shard_map/squares/pallas_call | solution.py:831
  578.0 0.0 all-gather.9.cloned.1.call-update
  578.0 0.0 copy-start
  578.0 0.0 copy-start.1
  578.1 0.0 copy-start.2
  578.1 22.0 %multiply_subtract_fusion = (f32[24026,96]{0,1:T(8,128)}, f32[24026,96]{0,1:T(8,128)}, f32[24026,96]{0,1:T(8,128)}) fusion(f32[24026,96]{0,1:T(8,128)} %param.28, f32[]{:T(128)} %min_shard_map.3, bf16[96,24576]{1,0:T(8,128)(2,1)} %get-tuple-element.116, f32[24026,96]{0,1:T(8,128)} %param.34, f32[24026,96]{0,1:T(8,128)} %param.40), kind=kLoop, calls=%fused_computation.4 | loop fusion | flops 39210432 | bytes 59968900 | tf_op jit(solution)/shard_map/sub | solution.py:214
  600.1 0.0 copy-done
  600.1 0.0 copy-done.1
  600.1 0.0 copy-done.2
  600.1 0.6 multiply_subtract_fusion.1
  600.8 0.2 all-gather.9.cloned.1.call-done
  601.0 9.7 %adam_in.1 = (f32[3,96,2304]{2,1,0:T(8,128)}, f32[3,96,2304]{2,1,0:T(8,128)}, f32[3,96,2304]{2,1,0:T(8,128)}) custom-call(f32[1]{0:T(128)} %bitcast.16.factor_ref, bf16[4,96,3072]{2,1,0:T(8,128)(2,1)} %bitcast.36, bf16[4,96,2304]{2,1,0:T(8,128)(2,1)} %get-tuple-element.118.refs_1_, f32[3,96,2304]{2,1,0:T(8,128)} %refs_2_.5, f32[3,96,2304]{2,1,0:T(8,128)} %refs_3_.4, ...), custom_call_target="tpu_custom_call" | custom-call | tf_op jit(solution)/shard_map/adam_in/pallas_call | solution.py:1623
  610.7 5.7 adam_out.1
  616.3 7.6 %adam_up.1 = (f32[2,96,3072]{2,1,0:T(8,128)}, f32[2,96,3072]{2,1,0:T(8,128)}, f32[2,96,3072]{2,1,0:T(8,128)}) custom-call(f32[1]{0:T(128)} %bitcast.16.factor_ref, bf16[4,96,3072]{2,1,0:T(8,128)(2,1)} %bitcast.38, bf16[4,96,2304]{2,1,0:T(8,128)(2,1)} %get-tuple-element.118.refs_1_, f32[2,96,3072]{2,1,0:T(8,128)} %refs_2_.7, f32[2,96,3072]{2,1,0:T(8,128)} %refs_3_.6, ...), custom_call_target="tpu_custom_call" | custom-call | tf_op jit(solution)/shard_map/adam_up/pallas_call | solution.py:1623
  623.9 0.0 copy-start.7
  623.9 6.2 adam_down.1
  630.1 0.0 copy-done.7
  (4 shorter events, 0.0 us)
Async XLA Ops:
  7.2 6.3 copy-start.5
  7.2 6.3 copy-start.3
  7.2 10.9 %copy-start.4 = (s32[1,64]{1,0:T(1,128)S(1)}, s32[1,64]{1,0:T(1,128)}, u32[]{:S(2)}) copy-start(s32[1,64]{1,0:T(1,128)} %refs_1_.2) | copy-start | bytes 772
  7.2 113.6 %all-gather.5.cloned.1.call-start = ((), (), s32[]{:S(2)}) async-start(), calls=%async_computation | async-start | bytes 5971968 | tf_op jit(solution)/shard_map/all_gather | solution.py:1788
  12.1 212.6 %all-gather.7.cloned.1.call-start = ((), (), s32[]{:S(2)}) async-start(), calls=%async_computation.1 | async-start | bytes 3760128 | tf_op jit(solution)/shard_map/all_gather | solution.py:1789
  12.8 588.2 %all-gather.9.cloned.1.call-start = ((), (), s32[]{:S(2)}) async-start(), calls=%async_computation.2 | async-start | bytes 2949120 | tf_op jit(solution)/shard_map/all_gather | solution.py:2048
  528.3 31.6 %copy-start.6 = (f32[1,128]{1,0:T(1,128)S(1)}, f32[1,128]{1,0:T(1,128)}, u32[]{:S(2)}) copy-start(f32[1,128]{1,0:T(1,128)} %get-tuple-element.115) | copy-start | bytes 1540
  578.0 22.1 %copy-start = (f32[14,96]{1,0:T(8,128)S(1)}, f32[14,96]{1,0:T(8,128)}, u32[]{:S(2)}) copy-start(f32[14,96]{1,0:T(8,128)} %norms_ref.1) | copy-start | bytes 16132
  578.0 22.1 %copy-start.1 = (f32[14,96]{1,0:T(8,128)S(1)}, f32[14,96]{1,0:T(8,128)}, u32[]{:S(2)}) copy-start(f32[14,96]{1,0:T(8,128)} %param.39) | copy-start | bytes 16132
  578.1 22.1 %copy-start.2 = (f32[14,96]{1,0:T(8,128)S(1)}, f32[14,96]{1,0:T(8,128)}, u32[]{:S(2)}) copy-start(f32[14,96]{1,0:T(8,128)} %param.45) | copy-start | bytes 16132
  623.9 6.2 copy-start.7
Sparse Core Ops, SparseCore 0:
  12.2 107.7 all-gather.4
  122.7 101.9 all-gather.6
  578.2 22.7 all-gather.8
